TPU v7x, 512 devices: a whole 4x8x8 slice. The times are simulated.
512 devices in a mesh: seq: 8 (over x, core), chan: 64 (over z, y).
Axes of the slice: x: 4, y: 8, z: 8, core: 2. Of those that a mesh axis runs over, the one named last changes fastest.
Arguments:
- activations: bfloat16 [4096, 4096], P('seq', 'chan'), may hold values from -6 to 6
- in_weight: bfloat16 [3, 4096, 4096], P(None, 'chan'), may hold values from -0.09375 to 0.09375
- short_taps: float32 [3, 3, 4096], P(None, None, 'chan'), may hold values from -3.5 to 3.5
- long_filter: bfloat16 [4096, 4096], P('chan', 'seq'), may hold values from -0.09375 to 0.09375
- skip_gain: float32 [4096], P('chan'), may hold values from -4 to 4
Outputs:
- mixed: bfloat16 [4096, 4096], P('seq', 'chan')
All inputs are finite; a program needn't handle non-finite values.
Results may differ from a plain program's by a relative error of at most 0.0076.
Values may be sent and summed in bfloat16 or wider, within the bound.
No kernel may reach another device: no remote copies, remote signals or barrier semaphores. Data moves between devices by JAX's collectives and lax.ppermute only.
A program may use at most 64 MiB of HBM per device.

v0:
```python
import math

import jax
import jax.numpy as jnp
from jax import lax
from jax.sharding import PartitionSpec as P


def from_behind(block, axis, distance):
    devices = range(lax.axis_size(axis))
    route = [(i - distance, i) for i in devices if i - distance in devices]
    return lax.ppermute(block, axis, route)


def tables(length):
    double = 2 * length
    freq_index = jnp.arange(double, dtype=jnp.int32)
    phase = (freq_index[:, None] * freq_index[None, :] % double).astype(jnp.float32) * (
        2.0 * math.pi / double
    )
    return (jnp.cos(phase).astype(jnp.bfloat16), jnp.sin(phase).astype(jnp.bfloat16))


def spectrum(signal, cosine, sine):
    real_part = jnp.einsum("ft,...tc->...fc", cosine, signal, preferred_element_type=jnp.float32)
    imag_part = -jnp.einsum("ft,...tc->...fc", sine, signal, preferred_element_type=jnp.float32)
    return (real_part, imag_part)


def lag_spectrum(lags, cosine, sine):
    real_part = jnp.einsum("ft,...ct->...fc", cosine, lags, preferred_element_type=jnp.float32)
    imag_part = -jnp.einsum("ft,...ct->...fc", sine, lags, preferred_element_type=jnp.float32)
    return (real_part, imag_part)


def multiply_add(totals, filter_real, filter_imag, signal_real, signal_imag):
    return (
        totals[0] + filter_real * signal_real - filter_imag * signal_imag,
        totals[1] + filter_real * signal_imag + filter_imag * signal_real,
    )


def on_device(activations, in_weight, short_taps, long_filter, skip_gain):
    rows = activations.shape[0]
    channels = in_weight.shape[1]
    proj = jnp.einsum(
        "tk,sck->tsc",
        lax.all_gather(activations, "chan", axis=1, tiled=True),
        in_weight,
        preferred_element_type=jnp.float32,
    ).astype(jnp.bfloat16)
    earlier = from_behind(proj[rows - 2 :], "seq", 1)
    padded = jnp.concatenate([earlier, proj], axis=0).astype(jnp.float32)
    feat = (
        short_taps[:, 0, :] * padded[2:]
        + short_taps[:, 1, :] * padded[1:-1]
        + short_taps[:, 2, :] * padded[:-2]
    )
    gated = (feat[:, 1, :] * feat[:, 2, :]).astype(jnp.bfloat16)
    table_cos, table_sin = tables(rows)
    cosine = table_cos[:, :rows]
    sine = table_sin[:, :rows]
    double = 2 * rows
    seq_count = lax.axis_size("seq")
    all_lags = lax.all_gather(long_filter, "seq", axis=1, tiled=True)
    lag_blocks = jnp.transpose(all_lags.reshape(channels, seq_count, rows), (1, 0, 2))
    lag_real, lag_imag = lag_spectrum(lag_blocks, cosine, sine)
    spectra = jnp.stack([lag_real, lag_imag], axis=1)
    zero_spec = jnp.zeros((double, channels), jnp.float32)
    current = (zero_spec, zero_spec)
    previous = (zero_spec, zero_spec)
    moving = gated
    for section in range(seq_count):
        if section > 0:
            moving = from_behind(moving, "seq", 1)
        signal_real, signal_imag = spectrum(moving, cosine, sine)
        current = multiply_add(
            current, spectra[section, 0], spectra[section, 1], signal_real, signal_imag
        )
        if section > 0:
            previous = multiply_add(
                previous, spectra[section - 1, 0], spectra[section - 1, 1], signal_real, signal_imag
            )
    cur_real = current[0].astype(jnp.bfloat16)
    cur_imag = current[1].astype(jnp.bfloat16)
    prev_real = previous[0].astype(jnp.bfloat16)
    prev_imag = previous[1].astype(jnp.bfloat16)
    conv = (
        jnp.dot(table_cos[:rows], cur_real, preferred_element_type=jnp.float32)
        - jnp.dot(table_sin[:rows], cur_imag, preferred_element_type=jnp.float32)
        + jnp.dot(table_cos[rows:], prev_real, preferred_element_type=jnp.float32)
        - jnp.dot(table_sin[rows:], prev_imag, preferred_element_type=jnp.float32)
    ) / double
    return (feat[:, 0, :] * (conv + skip_gain * gated.astype(jnp.float32))).astype(jnp.bfloat16)


def solution(mesh):
    in_specs = (
        P("seq", "chan"),
        P(None, "chan", None),
        P(None, None, "chan"),
        P("chan", "seq"),
        P("chan"),
    )
    out_specs = P("seq", "chan")
    return jax.shard_map(
        on_device, mesh=mesh, in_specs=in_specs, out_specs=out_specs, check_vma=False
    )
```

profile of v0, /device:TPU:1, one launch (start us, length us, event | category | flops | bytes accessed | tf_op | source)
XLA Modules:
  0.0 166.3 jit_solution(14995701161820373262)
XLA Ops:
  6.5 0.0 copy-start
  6.5 0.0 all-gather.2.cloned.1.call-start
  6.5 0.7 all-gather.2.cloned.1.call-update
  7.3 0.8 fusion.54
  8.1 20.0 %all_gather.7 = bf16[64,4096]{1,0:T(8,128)(2,1)S(1)} all-gather(bf16[64,512]{1,0:T(8,128)(2,1)} %param.8), channel_id=1, replica_groups=mesh['seq'=8,'chan'=64] {'seq'}, dimensions={1}, use_global_device_ids=true | all-gather | bytes 589824 | tf_op jit(solution)/shard_map/all_gather | solution.py:65
  28.1 15.7 %sine_convert_fusion = bf16[1024,1024]{1,0:T(8,128)(2,1)S(1)} fusion(), kind=kLoop, calls=%fused_computation.8 | loop fusion | flops 15728640 | bytes 2097152 | tf_op jit(solution)/shard_map/convert_element_type | solution.py:21
  43.8 0.0 copy-start.3
  43.8 1.3 copy-done.3
  45.1 2.1 %negate_bitcast_fusion = f32[8,1024,64]{1,2,0:T(8,128)} fusion(bf16[8,8,8,512]{3,2,1,0:T(8,128)(2,1)S(1)} %bitcast.266, bf16[1024,1024]{1,0:T(8,128)(2,1)S(1)} %sine_convert_fusion), kind=kOutput, calls=%fused_computation.13 | convolution fusion | flops 537395200 | bytes 3670016 | tf_op jit(solution)/shard_map/ft,...ct->...fc/dot_general | solution.py:32
  47.2 15.5 %cosine_convert_fusion = bf16[1024,1024]{1,0:T(8,128)(2,1)S(1)} fusion(), kind=kLoop, calls=%fused_computation.9 | loop fusion | flops 15728640 | bytes 2097152 | tf_op jit(solution)/shard_map/convert_element_type | solution.py:21
  62.8 0.0 copy-start.1
  62.8 1.3 copy-done.1
  64.1 2.1 %convolution_bitcast_fusion = f32[8,1024,64]{1,2,0:T(8,128)} fusion(bf16[8,8,8,512]{3,2,1,0:T(8,128)(2,1)S(1)} %bitcast.267, bf16[1024,1024]{1,0:T(8,128)(2,1)S(1)} %cosine_convert_fusion), kind=kOutput, calls=%fused_computation.14 | convolution fusion | flops 536870912 | bytes 3670016 | tf_op jit(solution)/shard_map/ft,...ct->...fc/dot_general | solution.py:31
  66.3 33.1 %all-gather.2.cloned.1.call-done = bf16[512,4096]{0,1:T(8,128)(2,1)} async-done(((bf16[512,64]{0,1:T(8,128)(2,1)}), bf16[512,4096]{0,1:T(8,128)(2,1)}) %all-gather.2.cloned.1.call-update) | async-done | bytes 4194320 | tf_op jit(solution)/shard_map/all_gather | solution.py:48
  99.3 0.0 copy-done
  99.3 3.2 %fusion.8 = bf16[512,3,64]{0,2,1:T(8,128)(2,1)S(1)} fusion(bf16[3,64,4096]{2,1,0:T(8,128)(2,1)S(1)} %copy-done, bf16[512,4096]{0,1:T(8,128)(2,1)} %all-gather.2.cloned.1.call-done), kind=kOutput, calls=%fused_computation.15 | convolution fusion | flops 805404672 | bytes 5963776 | tf_op jit(solution)/shard_map/tk,sck->tsc/dot_general | solution.py:46
  102.5 0.1 slice.190
  102.6 7.5 %collective-permute-start = (bf16[2,3,64]{0,2,1:T(8,128)(2,1)S(1)}, bf16[2,3,64]{0,2,1:T(8,128)(2,1)S(1)}, u32[]{:S(2)}, u32[]{:S(2)}) collective-permute-start(bf16[2,3,64]{0,2,1:T(8,128)(2,1)S(1)} %slice.190), channel_id=1, source_target_pairs={{0,64},{64,128},{128,192},{192,256},{256,320},{320,384},{384,448},... | collective-permute-start | bytes 2312 | tf_op jit(solution)/shard_map/ppermute | solution.py:12
  110.2 1.1 collective-permute-done
  111.3 0.1 maximum_convert_fusion
  111.4 0.4 fusion.24
  111.8 4.2 %collective-permute-start.1 = (bf16[512,64]{0,1:T(8,128)(2,1)S(1)}, bf16[512,64]{0,1:T(8,128)(2,1)S(1)}, u32[]{:S(2)}, u32[]{:S(2)}) collective-permute-start(bf16[512,64]{0,1:T(8,128)(2,1)S(1)} %fusion.27), channel_id=1, source_target_pairs={{0,64},{64,128},{128,192},{192,256},{256,320},{320,384},{384,448},... | collective-permute-start | bytes 196616 | tf_op jit(solution)/shard_map/ppermute | solution.py:12
  116.1 1.7 fusion.51
  117.7 1.7 %convolution_negate_fusion.7 = f32[1024,64]{0,1:T(8,128)S(1)} fusion(bf16[512,64]{0,1:T(8,128)(2,1)S(1)} %fusion.27, bf16[1024,1024]{1,0:T(8,128)(2,1)} %copy-done.3), kind=kOutput, calls=%fused_computation.23 | convolution fusion | flops 67174400 | bytes 1376256 | tf_op jit(solution)/shard_map/ft,...tc->...fc/dot_general | solution.py:26
  119.4 0.0 collective-permute-done.1
  119.4 2.2 %collective-permute-start.2 = (bf16[512,64]{0,1:T(8,128)(2,1)S(1)}, bf16[512,64]{0,1:T(8,128)(2,1)S(1)}, u32[]{:S(2)}, u32[]{:S(2)}) collective-permute-start(bf16[512,64]{0,1:T(8,128)(2,1)S(1)} %collective-permute-done.1), channel_id=1, source_target_pairs={{0,64},{64,128},{128,192},{192,256},{256,320},{320,384},{384,448},... | collective-permute-start | bytes 196616 | tf_op jit(solution)/shard_map/ppermute | solution.py:12
  121.6 1.7 fusion.49
  123.3 1.7 %convolution_negate_fusion.6 = f32[1024,64]{0,1:T(8,128)S(1)} fusion(bf16[512,64]{0,1:T(8,128)(2,1)S(1)} %collective-permute-done.1, bf16[1024,1024]{1,0:T(8,128)(2,1)} %copy-done.3), kind=kOutput, calls=%fused_computation.22 | convolution fusion | flops 67174400 | bytes 1376256 | tf_op jit(solution)/shard_map/ft,...tc->...fc/dot_general | solution.py:26
  125.0 0.0 collective-permute-done.2
  125.0 3.2 %collective-permute-start.3 = (bf16[512,64]{0,1:T(8,128)(2,1)S(1)}, bf16[512,64]{0,1:T(8,128)(2,1)S(1)}, u32[]{:S(2)}, u32[]{:S(2)}) collective-permute-start(bf16[512,64]{0,1:T(8,128)(2,1)S(1)} %collective-permute-done.2), channel_id=1, source_target_pairs={{0,64},{64,128},{128,192},{192,256},{256,320},{320,384},{384,448},... | collective-permute-start | bytes 196616 | tf_op jit(solution)/shard_map/ppermute | solution.py:12
  128.2 1.7 fusion.47
  129.8 1.7 %convolution_negate_fusion.5 = f32[1024,64]{0,1:T(8,128)S(1)} fusion(bf16[512,64]{0,1:T(8,128)(2,1)S(1)} %collective-permute-done.2, bf16[1024,1024]{1,0:T(8,128)(2,1)} %copy-done.3), kind=kOutput, calls=%fused_computation.21 | convolution fusion | flops 67174400 | bytes 1376256 | tf_op jit(solution)/shard_map/ft,...tc->...fc/dot_general | solution.py:26
  131.5 0.0 collective-permute-done.3
  131.5 2.2 %collective-permute-start.4 = (bf16[512,64]{0,1:T(8,128)(2,1)S(1)}, bf16[512,64]{0,1:T(8,128)(2,1)S(1)}, u32[]{:S(2)}, u32[]{:S(2)}) collective-permute-start(bf16[512,64]{0,1:T(8,128)(2,1)S(1)} %collective-permute-done.3), channel_id=1, source_target_pairs={{0,64},{64,128},{128,192},{192,256},{256,320},{320,384},{384,448},... | collective-permute-start | bytes 196616 | tf_op jit(solution)/shard_map/ppermute | solution.py:12
  133.7 1.7 fusion.45
  135.4 1.7 %convolution_negate_fusion.4 = f32[1024,64]{0,1:T(8,128)S(1)} fusion(bf16[512,64]{0,1:T(8,128)(2,1)S(1)} %collective-permute-done.3, bf16[1024,1024]{1,0:T(8,128)(2,1)} %copy-done.3), kind=kOutput, calls=%fused_computation.20 | convolution fusion | flops 67174400 | bytes 1376256 | tf_op jit(solution)/shard_map/ft,...tc->...fc/dot_general | solution.py:26
  137.1 0.0 collective-permute-done.4
  137.1 2.9 %collective-permute-start.5 = (bf16[512,64]{0,1:T(8,128)(2,1)S(1)}, bf16[512,64]{0,1:T(8,128)(2,1)S(1)}, u32[]{:S(2)}, u32[]{:S(2)}) collective-permute-start(bf16[512,64]{0,1:T(8,128)(2,1)S(1)} %collective-permute-done.4), channel_id=1, source_target_pairs={{0,64},{64,128},{128,192},{192,256},{256,320},{320,384},{384,448},... | collective-permute-start | bytes 196616 | tf_op jit(solution)/shard_map/ppermute | solution.py:12
  140.0 1.7 fusion.43
  141.6 1.7 %convolution_negate_fusion.3 = f32[1024,64]{0,1:T(8,128)S(1)} fusion(bf16[512,64]{0,1:T(8,128)(2,1)S(1)} %collective-permute-done.4, bf16[1024,1024]{1,0:T(8,128)(2,1)} %copy-done.3), kind=kOutput, calls=%fused_computation.19 | convolution fusion | flops 67174400 | bytes 1376256 | tf_op jit(solution)/shard_map/ft,...tc->...fc/dot_general | solution.py:26
  143.3 0.0 collective-permute-done.5
  143.3 2.2 %collective-permute-start.6 = (bf16[512,64]{0,1:T(8,128)(2,1)S(1)}, bf16[512,64]{0,1:T(8,128)(2,1)S(1)}, u32[]{:S(2)}, u32[]{:S(2)}) collective-permute-start(bf16[512,64]{0,1:T(8,128)(2,1)S(1)} %collective-permute-done.5), channel_id=1, source_target_pairs={{0,64},{64,128},{128,192},{192,256},{256,320},{320,384},{384,448},... | collective-permute-start | bytes 196616 | tf_op jit(solution)/shard_map/ppermute | solution.py:12
  145.5 0.0 copy-start.6
  145.6 1.8 %fusion.41 = f32[1024,64]{0,1:T(8,128)S(1)} fusion(bf16[512,64]{0,1:T(8,128)(2,1)S(1)} %collective-permute-done.5, bf16[1024,1024]{1,0:T(8,128)(2,1)} %copy-done.1), kind=kOutput, calls=%fused_computation.84 | convolution fusion | flops 67108864 | bytes 1376256 | tf_op jit(solution)/shard_map/ft,...tc->...fc/dot_general | solution.py:25
  147.4 0.0 copy-start.2
  147.4 1.8 %convolution_negate_fusion.2 = f32[1024,64]{0,1:T(8,128)S(1)} fusion(bf16[512,64]{0,1:T(8,128)(2,1)S(1)} %collective-permute-done.5, bf16[1024,1024]{1,0:T(8,128)(2,1)} %copy-done.3), kind=kOutput, calls=%fused_computation.18 | convolution fusion | flops 67174400 | bytes 1376256 | tf_op jit(solution)/shard_map/ft,...tc->...fc/dot_general | solution.py:26
  149.2 0.0 copy-start.4
  149.2 0.0 collective-permute-done.6
  149.2 2.4 %collective-permute-start.7 = (bf16[512,64]{0,1:T(8,128)(2,1)S(1)}, bf16[512,64]{0,1:T(8,128)(2,1)S(1)}, u32[]{:S(2)}, u32[]{:S(2)}) collective-permute-start(bf16[512,64]{0,1:T(8,128)(2,1)S(1)} %collective-permute-done.6), channel_id=1, source_target_pairs={{0,64},{64,128},{128,192},{192,256},{256,320},{320,384},{384,448},... | collective-permute-start | bytes 196616 | tf_op jit(solution)/shard_map/ppermute | solution.py:12
  151.6 1.7 fusion.39
  153.2 0.0 copy-start.5
  153.2 1.8 %convolution_negate_fusion.1 = f32[1024,64]{0,1:T(8,128)S(1)} fusion(bf16[512,64]{0,1:T(8,128)(2,1)S(1)} %collective-permute-done.6, bf16[1024,1024]{1,0:T(8,128)(2,1)} %copy-done.3), kind=kOutput, calls=%fused_computation.17 | convolution fusion | flops 67174400 | bytes 1376256 | tf_op jit(solution)/shard_map/ft,...tc->...fc/dot_general | solution.py:26
  155.0 0.0 collective-permute-done.7
  155.1 0.0 copy-done.2
  155.1 0.4 fusion.37
  155.5 0.0 copy-done.4
  155.5 0.4 convolution_negate_fusion
  156.0 0.0 copy-done.6
  156.0 0.0 copy-done.5
  156.0 0.8 fusion.18
  156.7 0.8 convolution_subtract_fusion.1
  157.5 0.7 convolution_add_fusion
  158.2 0.0 copy-done.7
  158.2 1.3 fusion.14
  (4 shorter events, 0.0 us)
Async XLA Ops:
  6.5 92.8 %copy-start = (bf16[3,64,4096]{2,1,0:T(8,128)(2,1)S(1)}, bf16[3,64,4096]{2,1,0:T(8,128)(2,1)}, u32[]{:S(2)}) copy-start(bf16[3,64,4096]{2,1,0:T(8,128)(2,1)} %param.6) | copy-start | bytes 4718596
  6.5 92.8 %all-gather.2.cloned.1.call-start = ((), (), s32[]{:S(2)}) async-start(), calls=%async_computation | async-start | bytes 4259840 | tf_op jit(solution)/shard_map/all_gather | solution.py:48
  43.8 1.4 copy-start.3
  62.8 1.3 copy-start.1
  102.6 8.7 %collective-permute-start = (bf16[2,3,64]{0,2,1:T(8,128)(2,1)S(1)}, bf16[2,3,64]{0,2,1:T(8,128)(2,1)S(1)}, u32[]{:S(2)}, u32[]{:S(2)}) collective-permute-start(bf16[2,3,64]{0,2,1:T(8,128)(2,1)S(1)} %slice.190), channel_id=1, source_target_pairs={{0,64},{64,128},{128,192},{192,256},{256,320},{320,384},{384,448},... | collective-permute-start | bytes 2312 | tf_op jit(solution)/shard_map/ppermute | solution.py:12
  111.8 7.6 %collective-permute-start.1 = (bf16[512,64]{0,1:T(8,128)(2,1)S(1)}, bf16[512,64]{0,1:T(8,128)(2,1)S(1)}, u32[]{:S(2)}, u32[]{:S(2)}) collective-permute-start(bf16[512,64]{0,1:T(8,128)(2,1)S(1)} %fusion.27), channel_id=1, source_target_pairs={{0,64},{64,128},{128,192},{192,256},{256,320},{320,384},{384,448},... | collective-permute-start | bytes 196616 | tf_op jit(solution)/shard_map/ppermute | solution.py:12
  119.4 5.6 %collective-permute-start.2 = (bf16[512,64]{0,1:T(8,128)(2,1)S(1)}, bf16[512,64]{0,1:T(8,128)(2,1)S(1)}, u32[]{:S(2)}, u32[]{:S(2)}) collective-permute-start(bf16[512,64]{0,1:T(8,128)(2,1)S(1)} %collective-permute-done.1), channel_id=1, source_target_pairs={{0,64},{64,128},{128,192},{192,256},{256,320},{320,384},{384,448},... | collective-permute-start | bytes 196616 | tf_op jit(solution)/shard_map/ppermute | solution.py:12
  125.0 6.5 %collective-permute-start.3 = (bf16[512,64]{0,1:T(8,128)(2,1)S(1)}, bf16[512,64]{0,1:T(8,128)(2,1)S(1)}, u32[]{:S(2)}, u32[]{:S(2)}) collective-permute-start(bf16[512,64]{0,1:T(8,128)(2,1)S(1)} %collective-permute-done.2), channel_id=1, source_target_pairs={{0,64},{64,128},{128,192},{192,256},{256,320},{320,384},{384,448},... | collective-permute-start | bytes 196616 | tf_op jit(solution)/shard_map/ppermute | solution.py:12
  131.5 5.6 %collective-permute-start.4 = (bf16[512,64]{0,1:T(8,128)(2,1)S(1)}, bf16[512,64]{0,1:T(8,128)(2,1)S(1)}, u32[]{:S(2)}, u32[]{:S(2)}) collective-permute-start(bf16[512,64]{0,1:T(8,128)(2,1)S(1)} %collective-permute-done.3), channel_id=1, source_target_pairs={{0,64},{64,128},{128,192},{192,256},{256,320},{320,384},{384,448},... | collective-permute-start | bytes 196616 | tf_op jit(solution)/shard_map/ppermute | solution.py:12
  137.1 6.2 %collective-permute-start.5 = (bf16[512,64]{0,1:T(8,128)(2,1)S(1)}, bf16[512,64]{0,1:T(8,128)(2,1)S(1)}, u32[]{:S(2)}, u32[]{:S(2)}) collective-permute-start(bf16[512,64]{0,1:T(8,128)(2,1)S(1)} %collective-permute-done.4), channel_id=1, source_target_pairs={{0,64},{64,128},{128,192},{192,256},{256,320},{320,384},{384,448},... | collective-permute-start | bytes 196616 | tf_op jit(solution)/shard_map/ppermute | solution.py:12
  143.3 5.9 %collective-permute-start.6 = (bf16[512,64]{0,1:T(8,128)(2,1)S(1)}, bf16[512,64]{0,1:T(8,128)(2,1)S(1)}, u32[]{:S(2)}, u32[]{:S(2)}) collective-permute-start(bf16[512,64]{0,1:T(8,128)(2,1)S(1)} %collective-permute-done.5), channel_id=1, source_target_pairs={{0,64},{64,128},{128,192},{192,256},{256,320},{320,384},{384,448},... | collective-permute-start | bytes 196616 | tf_op jit(solution)/shard_map/ppermute | solution.py:12
  145.5 10.4 %copy-start.6 = (f32[8,1024,64]{1,2,0:T(8,128)S(1)}, f32[8,1024,64]{1,2,0:T(8,128)}, u32[]{:S(2)}) copy-start(f32[8,1024,64]{1,2,0:T(8,128)} %negate_bitcast_fusion) | copy-start | bytes 6291460
  147.4 7.7 %copy-start.2 = (bf16[1024,1024]{1,0:T(8,128)(2,1)S(1)}, bf16[1024,1024]{1,0:T(8,128)(2,1)}, u32[]{:S(2)}) copy-start(bf16[1024,1024]{1,0:T(8,128)(2,1)} %copy-done.1) | copy-start | bytes 6291460
  149.2 6.3 %copy-start.4 = (bf16[1024,1024]{1,0:T(8,128)(2,1)S(1)}, bf16[1024,1024]{1,0:T(8,128)(2,1)}, u32[]{:S(2)}) copy-start(bf16[1024,1024]{1,0:T(8,128)(2,1)} %copy-done.3) | copy-start | bytes 6291460
  149.2 5.9 %collective-permute-start.7 = (bf16[512,64]{0,1:T(8,128)(2,1)S(1)}, bf16[512,64]{0,1:T(8,128)(2,1)S(1)}, u32[]{:S(2)}, u32[]{:S(2)}) collective-permute-start(bf16[512,64]{0,1:T(8,128)(2,1)S(1)} %collective-permute-done.6), channel_id=1, source_target_pairs={{0,64},{64,128},{128,192},{192,256},{256,320},{320,384},{384,448},... | collective-permute-start | bytes 196616 | tf_op jit(solution)/shard_map/ppermute | solution.py:12
  153.2 2.8 %copy-start.5 = (f32[8,1024,64]{1,2,0:T(8,128)S(1)}, f32[8,1024,64]{1,2,0:T(8,128)}, u32[]{:S(2)}) copy-start(f32[8,1024,64]{1,2,0:T(8,128)} %convolution_bitcast_fusion) | copy-start | bytes 6291460
  157.5 0.7 copy-start.7
Sparse Core Ops, SparseCore 0:
  10.4 88.8 all-gather.1
where the time goes:
time: 167 us; the launch traced here: 166 us
  matrix products  35.5 us (21%)
  waiting for transfers between devices  34.9 us (21%)
  other arithmetic  31.7 us (19%)
  starting transfers between devices  26.9 us (16%)
  blocking collectives  20 us (12%)
  between operations  13.6 us (8%)
  local copies, waits for them, and re-layouts  3.6 us (2%)
    all_gather x1, waiting for transfers between devices, on_device(): lax.all_gather(activations, 'chan', axis=1, tiled=True)  33.1 us
    ppermute x8, starting transfers between devices, from_behind(): return lax.ppermute(block, axis, route)  26.9 us
    all_gather x1, blocking collectives, on_device(): all_lags = lax.all_gather(long_filter, 'seq', axis=1, tiled=True)  20 us
    convert_element_type x1, other arithmetic, tables(): jnp.sin(phase).astype(jnp.bfloat16)  15.7 us
    convert_element_type x1, other arithmetic, tables(): jnp.cos(phase).astype(jnp.bfloat16)  15.5 us
    dot_general x8, matrix products, spectrum(): jnp.einsum('ft,...tc->...fc', sine, signal, preferred_element_type=jnp.fl...  12.4 us
    dot_general x8, matrix products, spectrum(): jnp.einsum('ft,...tc->...fc', cosine, signal, preferred_element_type=jnp....  12.2 us
  transfers between devices with their start and end apart: 9, of which 2 were waited for; matrix products, arithmetic and copies ran while one was open for 36% of the time, Pallas kernels for 0%

commit v1 on v0

v1 whole, which is shorter than its diff:
```python
import math

import jax
import jax.numpy as jnp
import numpy as np
from jax import lax
from jax.experimental import pallas as pl
from jax.experimental.pallas import tpu as pltpu
from jax.sharding import PartitionSpec as P

BOTH = ("seq", "chan")
RING = 8
BLOCK = 512
F32 = jnp.float32
BF16 = jnp.bfloat16


def device_number(x, core, z, y):
    return ((x * 2 + core) * RING + z % RING) * RING + y % RING


def devices():
    return [
        (x, core, z, y)
        for x in range(4)
        for core in range(2)
        for z in range(RING)
        for y in range(RING)
    ]


def rings():
    return [
        [
            device_number(x, core, line, i) if core == 0 else device_number(x, core, i, line)
            for i in range(RING)
        ]
        for x in range(4)
        for core in range(2)
        for line in range(RING)
    ]


def shift(block, step):
    route = [
        (
            device_number(x, core, z, y),
            device_number(x, core, z + step, y)
            if core == 0
            else device_number(x, core, z, y + step),
        )
        for x, core, z, y in devices()
    ]
    return lax.ppermute(block, BOTH, route)


def tables():
    double = 2 * BLOCK
    freq = np.arange(BLOCK, dtype=np.int64)
    index = (freq[:, None] * freq[None, :]) % double
    phase = index.astype(np.float32) * np.float32(2.0 * math.pi / double)
    cosine = np.cos(phase).astype(jnp.bfloat16).astype(np.float32)
    sine = np.sin(phase).astype(jnp.bfloat16).astype(np.float32)
    nyquist = (1 - 2 * (freq % 2)).astype(np.float32)
    real, imag = cosine, -sine
    imag = imag.copy()
    imag[0] = nyquist
    forward = np.concatenate([real.T, imag.T], axis=1)
    weight = np.full((BLOCK, 1), 2.0 / double, np.float32)
    weight[0] = 1.0 / double
    inverse = np.concatenate([real * weight, imag * weight], axis=0)
    return forward.astype(jnp.bfloat16), inverse.astype(jnp.bfloat16)


def vmem():
    return pl.BlockSpec(memory_space=pltpu.VMEM)


def smem():
    return pl.BlockSpec(memory_space=pltpu.SMEM)


def params(mib):
    return pltpu.CompilerParams(vmem_limit_bytes=mib * 1024 * 1024)


def weight_kernel(place, weight, out):
    @pl.when(place[0] == 0)
    def _():
        for b in range(RING):
            out[b] = weight[:, b * BLOCK : (b + 1) * BLOCK]

    @pl.when(place[0] != 0)
    def _():
        for b in range(RING):
            out[b] = jnp.concatenate(
                [weight[:, (i * RING + b) * 64 : (i * RING + b) * 64 + 64] for i in range(RING)],
                axis=1,
            )


def first_kernel(place, weight, own, m1, p1, m2, p2, out):
    r = place[1]
    total = None
    for offset, block in ((0, own), (-1, m1), (1, p1), (-2, m2), (2, p2)):
        part = jnp.dot(
            weight[lax.rem(r + offset + RING, RING)], block[...], preferred_element_type=F32
        )
        total = part if total is None else total + part
    out[...] = total


def second_kernel(place, weight, before, m3, p3, low, high, lags, out):
    r = place[1]
    half = BLOCK // 2
    total = before[...]
    for offset, block in ((-3, m3), (3, p3)):
        total = total + jnp.dot(
            weight[lax.rem(r + offset + RING, RING)], block[...], preferred_element_type=F32
        )
    far = lax.rem(r + 4, RING)
    total = total + jnp.dot(weight[far, :, :half], low[...], preferred_element_type=F32)
    total = total + jnp.dot(weight[far, :, half:], high[...], preferred_element_type=F32)
    lag_rows = lags[...].astype(F32)
    pieces = []
    for d in range(RING):
        for s in range(3):
            pieces.append(total[s * 64 + d * 8 : s * 64 + d * 8 + 8])
        pieces.append(lag_rows[d * 8 : d * 8 + 8])
    out[...] = jnp.concatenate(pieces, axis=0).astype(BF16)


def conv_kernel(rows, taps, forward, inverse, out):
    data = rows[...].astype(F32)
    lane = lax.broadcasted_iota(jnp.int32, (8, RING * BLOCK), 1)

    def stream(s):
        return jnp.concatenate(
            [data[b * 32 + s * 8 : b * 32 + s * 8 + 8] for b in range(RING)], axis=1
        )

    def feature(s):
        now = stream(s)
        one = jnp.where(lane < 1, 0.0, pltpu.roll(now, 1, 1))
        two = jnp.where(lane < 2, 0.0, pltpu.roll(now, 2, 1))
        t = [taps[:, s * 3 + j : s * 3 + j + 1] for j in range(3)]
        return t[0] * now + t[1] * one + t[2] * two

    def by_block(value):
        return jnp.concatenate(
            [value[:, b * BLOCK : (b + 1) * BLOCK] for b in range(RING)], axis=0
        )

    gated = by_block(feature(1) * feature(2)).astype(BF16)
    lags = jnp.concatenate([data[b * 32 + 24 : b * 32 + 32] for b in range(RING)], axis=0)
    spec = jnp.dot(
        jnp.concatenate([gated, lags.astype(BF16)], axis=0),
        forward[...],
        preferred_element_type=F32,
    )
    reals, imags = [[] for _ in range(RING)], [[] for _ in range(RING)]
    wide = 128
    for piece in range(BLOCK // wide):
        here = slice(piece * wide, (piece + 1) * wide)
        there = slice(BLOCK + piece * wide, BLOCK + (piece + 1) * wide)
        freq = lax.broadcasted_iota(jnp.int32, (8, wide), 1) + piece * wide
        sign = (1 - 2 * lax.rem(freq, 2)).astype(F32)
        sig_re = [spec[b * 8 : b * 8 + 8, here] for b in range(RING)]
        sig_im = [spec[b * 8 : b * 8 + 8, there] for b in range(RING)]
        fil_re, fil_im, fil_last = [], [], []
        for m in range(RING):
            row = 64 + m * 8
            re, im = spec[row : row + 8, here], spec[row : row + 8, there]
            if m:
                re = re + sign * spec[row - 8 : row, here]
                im = im + sign * spec[row - 8 : row, there]
            fil_re.append(re)
            if piece == 0:
                fil_im.append(jnp.where(freq == 0, 0.0, im))
                fil_last.append(jnp.where(freq == 0, im, re))
            else:
                fil_im.append(im)
                fil_last.append(re)
        for b in range(RING):
            re = im = None
            for j in range(b + 1):
                m = b - j
                one = fil_re[m] * sig_re[j] - fil_im[m] * sig_im[j]
                two = fil_last[m] * sig_im[j] + fil_im[m] * sig_re[j]
                re = one if re is None else re + one
                im = two if im is None else im + two
            reals[b].append(re)
            imags[b].append(im)
    product = jnp.concatenate(
        [jnp.concatenate(reals[b] + imags[b], axis=1) for b in range(RING)], axis=0
    ).astype(BF16)
    conv = jnp.dot(product, inverse[...], preferred_element_type=F32)
    query = by_block(feature(0))
    skip = jnp.concatenate([taps[:, 9:10]] * RING, axis=0)
    out[...] = (query * (conv + skip * gated.astype(F32))).astype(BF16)


def on_device(activations, in_weight, short_taps, long_filter, skip_gain):
    position = lax.axis_index("seq")
    core = position % 2
    chan = lax.axis_index("chan")
    ring_place = jnp.where(core == 0, chan // RING, chan % RING)
    place = jnp.stack([core, ring_place]).astype(jnp.int32)

    shard = activations.T
    own = lax.all_to_all(
        jnp.broadcast_to(shard[None], (RING,) + shard.shape),
        BOTH,
        0,
        0,
        tiled=True,
        axis_index_groups=rings(),
    ).reshape(BLOCK, BLOCK)
    m2, p2 = shift(own, 2), shift(own, -2)
    m1, p1 = shift(own, 1), shift(own, -1)
    half = BLOCK // 2
    m3, p3 = shift(m2, 1), shift(p2, -1)
    low, high = shift(m2[:half], 2), shift(p2[half:], -2)

    weight = pl.pallas_call(
        weight_kernel,
        out_shape=jax.ShapeDtypeStruct((RING, 192, BLOCK), BF16),
        in_specs=[smem(), vmem()],
        out_specs=vmem(),
        compiler_params=params(24),
        cost_estimate=pl.CostEstimate(flops=0, bytes_accessed=3 << 20, transcendentals=0),
    )(place, in_weight.reshape(192, RING * BLOCK))
    before = pl.pallas_call(
        first_kernel,
        out_shape=jax.ShapeDtypeStruct((192, BLOCK), F32),
        in_specs=[smem()] + [vmem()] * 6,
        out_specs=vmem(),
        compiler_params=params(24),
        cost_estimate=pl.CostEstimate(
            flops=2 * 5 * 192 * BLOCK * BLOCK, bytes_accessed=4 << 20, transcendentals=0
        ),
    )(place, weight, own, m1, p1, m2, p2)
    messages = pl.pallas_call(
        second_kernel,
        out_shape=jax.ShapeDtypeStruct((RING * 32, BLOCK), BF16),
        in_specs=[smem()] + [vmem()] * 7,
        out_specs=vmem(),
        compiler_params=params(24),
        cost_estimate=pl.CostEstimate(
            flops=2 * 3 * 192 * BLOCK * BLOCK, bytes_accessed=4 << 20, transcendentals=0
        ),
    )(place, weight, before, m3, p3, low, high, long_filter)

    rows = lax.all_to_all(messages.reshape(RING, 32, BLOCK), "seq", 0, 0, tiled=True)
    taps = jnp.concatenate([short_taps.reshape(9, 64), skip_gain[None]], axis=0)
    taps = lax.dynamic_slice_in_dim(taps, position * 8, 8, axis=1).T
    forward, inverse = tables()
    mixed = pl.pallas_call(
        conv_kernel,
        out_shape=jax.ShapeDtypeStruct((RING * 8, BLOCK), BF16),
        in_specs=[vmem()] * 4,
        out_specs=vmem(),
        compiler_params=params(32),
        cost_estimate=pl.CostEstimate(
            flops=2 * (128 * 512 * 1024 + 64 * 1024 * 512), bytes_accessed=3 << 20, transcendentals=0
        ),
    )(rows.reshape(RING * 32, BLOCK), taps, forward, inverse)
    back = lax.all_to_all(mixed.reshape(RING, 8, BLOCK), "seq", 0, 0, tiled=True)
    return back.reshape(64, BLOCK).T


def solution(mesh):
    in_specs = (
        P("seq", "chan"),
        P(None, "chan", None),
        P(None, None, "chan"),
        P("chan", "seq"),
        P("chan"),
    )
    return jax.shard_map(
        on_device, mesh=mesh, in_specs=in_specs, out_specs=P("seq", "chan"), check_vma=False
    )
```

time: 167 us -> 96.1 us (0.58)
  matrix products: 35.5 us -> 0 us
  other arithmetic: 31.7 us -> 0.16 us
  waiting for transfers between devices: 34.9 us -> 15.4 us
  between operations: 13.6 us -> 0.2 us
  starting transfers between devices: 26.9 us -> 38.6 us
  blocking collectives: 20 us -> 31.1 us
  Pallas kernels: 0 us -> 5.96 us
    dot_general x23 -> x0, matrix products: 35.5 us -> none  [the longest x8 12.4 us: spectrum(): jnp.einsum('ft,...tc->...fc', sine, signal, preferred_element_type=jnp.fl...]
    all_gather x1 -> x0, waiting for transfers between devices: 33.1 us -> none  [on_device(): lax.all_gather(activations, 'chan', axis=1, tiled=True)]
    convert_element_type x4 -> x0, other arithmetic: 31.4 us -> none  [the longest x1 15.7 us: tables(): jnp.sin(phase).astype(jnp.bfloat16)]
    all_to_all x0 -> x2, blocking collectives: none -> 31.1 us  [the longest x1 22.8 us: on_device(): lax.all_to_all(jnp.broadcast_to(shard[None], (RING,) + shard.shape), BOTH...]
    all_gather x1 -> x0, blocking collectives: 20 us -> none  [on_device(): all_lags = lax.all_gather(long_filter, 'seq', axis=1, tiled=True)]
    all_to_all x0 -> x1, starting transfers between devices: none -> 9.83 us  [on_device(): lax.all_to_all(messages.reshape(RING, 32, BLOCK), 'seq', 0, 0, tiled=True)]
    ppermute x8, waiting for transfers between devices: 1.15 us -> 9.12 us  [shift(): return lax.ppermute(block, BOTH, route)]
    all_to_all x0 -> x1, waiting for transfers between devices: none -> 6.32 us  [on_device(): lax.all_to_all(messages.reshape(RING, 32, BLOCK), 'seq', 0, 0, tiled=True)]
  transfers between devices with their start and end apart: 9 -> 9, of which waited for: 2 -> 5; matrix products, arithmetic and copies ran while one was open for 36% -> 2% of each run, Pallas kernels for 0% -> 3%
where the time goes in v1:
time: 96.1 us; the launch traced here: 95.5 us
  starting transfers between devices  38.6 us (40%)
  blocking collectives  31.1 us (32%)
  waiting for transfers between devices  15.4 us (16%)
  Pallas kernels  5.96 us (6%)
  local copies, waits for them, and re-layouts  4.04 us (4%)
    ppermute x8, starting transfers between devices, shift(): return lax.ppermute(block, BOTH, route)  28.8 us
    all_to_all x1, blocking collectives, on_device(): lax.all_to_all(jnp.broadcast_to(shard[None], (RING,) + shard.shape), BOTH...  22.8 us
    all_to_all x1, starting transfers between devices, on_device(): lax.all_to_all(messages.reshape(RING, 32, BLOCK), 'seq', 0, 0, tiled=True)  9.83 us
    ppermute x8, waiting for transfers between devices, shift(): return lax.ppermute(block, BOTH, route)  9.12 us
    all_to_all x1, blocking collectives, on_device(): lax.all_to_all(mixed.reshape(RING, 8, BLOCK), 'seq', 0, 0, tiled=True)  8.26 us
    all_to_all x1, waiting for transfers between devices, on_device(): lax.all_to_all(messages.reshape(RING, 32, BLOCK), 'seq', 0, 0, tiled=True)  6.32 us
    pallas_call x1, Pallas kernels, on_device(): pl.pallas_call(second_kernel, out_shape=jax.ShapeDtypeStruct((RING * 32,...  2.47 us
  transfers between devices with their start and end apart: 9, of which 5 were waited for; matrix products, arithmetic and copies ran while one was open for 2% of the time, Pallas kernels for 3%

profile of v1, /device:TPU:1, one launch (start us, length us, event | category | flops | bytes accessed | tf_op | source)
XLA Modules:
  0.0 95.5 jit_solution(4753902713354631530)
XLA Ops:
  0.0 0.0 copy-start
  0.0 1.0 %broadcast_in_dim.4 = bf16[8,64,512]{2,1,0:T(8,128)(2,1)S(1)} broadcast(bf16[64,512]{1,0:T(8,128)(2,1)} %bitcast.23), dimensions={1,2} | broadcast | bytes 589824 | tf_op jit(solution)/shard_map/broadcast_in_dim | solution.py:212
  1.0 22.8 %all_to_all.15 = bf16[8,64,512]{2,1,0:T(8,128)(2,1)S(1)} all-to-all(bf16[8,64,512]{2,1,0:T(8,128)(2,1)S(1)} %broadcast_in_dim.4), channel_id=1, replica_groups={{0,1,2,3,4,5,6,7},{8,9,10,11,12,13,14,15},{16,17,18,19,20,21,22,23},{24..., dimensions={0} | all-to-all | bytes 1048576 | tf_op jit(solution)/shard_map/all_to_all | solution.py:211
  23.8 4.2 %collective-permute-start.2 = (bf16[512,512]{1,0:T(8,128)(2,1)S(1)}, bf16[512,512]{1,0:T(8,128)(2,1)S(1)}, u32[]{:S(2)}, u32[]{:S(2)}) collective-permute-start(bf16[512,512]{1,0:T(8,128)(2,1)S(1)} %bitcast.13), channel_id=1, source_target_pairs={{0,16},{1,17},{2,18},{3,19},{4,20},{5,21},{6,22},{7,23},{8,24},{9,... | collective-permute-start | bytes 1572872 | tf_op jit(solution)/shard_map/ppermute | solution.py:54
  28.0 3.6 %collective-permute-start.3 = (bf16[512,512]{1,0:T(8,128)(2,1)S(1)}, bf16[512,512]{1,0:T(8,128)(2,1)S(1)}, u32[]{:S(2)}, u32[]{:S(2)}) collective-permute-start(bf16[512,512]{1,0:T(8,128)(2,1)S(1)} %bitcast.14), channel_id=1, source_target_pairs={{0,48},{1,49},{2,50},{3,51},{4,52},{5,53},{6,54},{7,55},{8,56},{9,... | collective-permute-start | bytes 1572872 | tf_op jit(solution)/shard_map/ppermute | solution.py:54
  31.6 2.8 %collective-permute-start = (bf16[512,512]{1,0:T(8,128)(2,1)S(1)}, bf16[512,512]{1,0:T(8,128)(2,1)S(1)}, u32[]{:S(2)}, u32[]{:S(2)}) collective-permute-start(bf16[512,512]{1,0:T(8,128)(2,1)S(1)} %bitcast.15), channel_id=1, source_target_pairs={{0,8},{1,9},{2,10},{3,11},{4,12},{5,13},{6,14},{7,15},{8,16},{9,17... | collective-permute-start | bytes 1572872 | tf_op jit(solution)/shard_map/ppermute | solution.py:54
  34.4 3.7 %collective-permute-start.1 = (bf16[512,512]{1,0:T(8,128)(2,1)S(1)}, bf16[512,512]{1,0:T(8,128)(2,1)}, u32[]{:S(2)}, u32[]{:S(2)}) collective-permute-start(bf16[512,512]{1,0:T(8,128)(2,1)S(1)} %bitcast.16), channel_id=1, source_target_pairs={{0,56},{1,57},{2,58},{3,59},{4,60},{5,61},{6,62},{7,63},{8,0},{9,1... | collective-permute-start | bytes 1572872 | tf_op jit(solution)/shard_map/ppermute | solution.py:54
  38.1 1.4 %collective-permute-done.2.m2 = bf16[512,512]{1,0:T(8,128)(2,1)S(1)} collective-permute-done((bf16[512,512]{1,0:T(8,128)(2,1)S(1)}, bf16[512,512]{1,0:T(8,128)(2,1)S(1)}, u32[]{:S(2)}, u32[]{:S(2)}) %collective-permute-start.2) | collective-permute-done | bytes 524320 | tf_op jit(solution)/shard_map/ppermute | solution.py:54
  39.5 5.2 %collective-permute-start.4 = (bf16[512,512]{1,0:T(8,128)(2,1)S(1)}, bf16[512,512]{1,0:T(8,128)(2,1)}, u32[]{:S(2)}, u32[]{:S(2)}) collective-permute-start(bf16[512,512]{1,0:T(8,128)(2,1)S(1)} %collective-permute-done.2.m2), channel_id=1, source_target_pairs={{0,8},{1,9},{2,10},{3,11},{4,12},{5,13},{6,14},{7,15},{8,16},{9,17... | collective-permute-start | bytes 1572872 | tf_op jit(solution)/shard_map/ppermute | solution.py:54
  44.8 1.2 %collective-permute-done.3.p2 = bf16[512,512]{1,0:T(8,128)(2,1)S(1)} collective-permute-done((bf16[512,512]{1,0:T(8,128)(2,1)S(1)}, bf16[512,512]{1,0:T(8,128)(2,1)S(1)}, u32[]{:S(2)}, u32[]{:S(2)}) %collective-permute-start.3) | collective-permute-done | bytes 524320 | tf_op jit(solution)/shard_map/ppermute | solution.py:54
  46.0 1.9 %collective-permute-start.5 = (bf16[512,512]{1,0:T(8,128)(2,1)S(1)}, bf16[512,512]{1,0:T(8,128)(2,1)}, u32[]{:S(2)}, u32[]{:S(2)}) collective-permute-start(bf16[512,512]{1,0:T(8,128)(2,1)S(1)} %collective-permute-done.3.p2), channel_id=1, source_target_pairs={{0,56},{1,57},{2,58},{3,59},{4,60},{5,61},{6,62},{7,63},{8,0},{9,1... | collective-permute-start | bytes 1572872 | tf_op jit(solution)/shard_map/ppermute | solution.py:54
  47.9 0.7 slice.8
  48.6 4.4 %collective-permute-start.6 = (bf16[256,512]{1,0:T(8,128)(2,1)}, bf16[256,512]{1,0:T(8,128)(2,1)S(1)}, u32[]{:S(2)}, u32[]{:S(2)}) collective-permute-start(bf16[256,512]{1,0:T(8,128)(2,1)} %slice.8), channel_id=1, source_target_pairs={{0,16},{1,17},{2,18},{3,19},{4,20},{5,21},{6,22},{7,23},{8,24},{9,... | collective-permute-start | bytes 786440 | tf_op jit(solution)/shard_map/ppermute | solution.py:54
  53.0 0.7 slice.9
  53.8 0.0 collective-permute-done.m1
  53.8 0.0 copy-start.3
  53.8 0.8 copy-done.3
  54.6 3.0 %collective-permute-start.7 = (bf16[256,512]{1,0:T(8,128)(2,1)}, bf16[256,512]{1,0:T(8,128)(2,1)}, u32[]{:S(2)}, u32[]{:S(2)}) collective-permute-start(bf16[256,512]{1,0:T(8,128)(2,1)} %slice.9), channel_id=1, source_target_pairs={{0,48},{1,49},{2,50},{3,51},{4,52},{5,53},{6,54},{7,55},{8,56},{9,... | collective-permute-start | bytes 786440 | tf_op jit(solution)/shard_map/ppermute | solution.py:54
  57.6 0.1 pad_add_fusion.place
  57.7 0.0 copy-done
  57.7 0.0 copy-start.4
  57.7 1.0 %shard_map.73.weight = bf16[8,192,512]{2,1,0:T(8,128)(2,1)S(1)} custom-call(s32[2]{0:T(128)S(1)} %pad_add_fusion.place, bf16[192,4096]{1,0:T(8,128)(2,1)S(1)} %bitcast.18), custom_call_target="tpu_custom_call" | custom-call | bytes 3145728 | tf_op jit(solution)/shard_map/pallas_call | solution.py:225
  58.7 0.0 copy-start.5
  58.7 0.0 collective-permute-done.1.p1
  58.7 0.0 copy-done.4
  58.7 1.7 %shard_map.74.before = f32[192,512]{1,0:T(8,128)S(1)} custom-call(s32[2]{0:T(128)S(1)} %pad_add_fusion.place, bf16[8,192,512]{2,1,0:T(8,128)(2,1)S(1)} %shard_map.73.weight, bf16[512,512]{1,0:T(8,128)(2,1)S(1)} %bitcast.17, bf16[512,512]{1,0:T(8,128)(2,1)S(1)} %copy-done.4, bf16[512,512]{1,0:T(8,128)(2,1)} %collective-permute-done.1.p1, ...), custom_call_target="tpu_custom_call" | custom-call | flops 503316480 | bytes 4194304 | tf_op jit(solution)/shard_map/pallas_call | solution.py:233
  60.5 0.0 copy-start.6
  60.5 0.0 copy-start.7
  60.5 0.0 copy-start.1
  60.5 0.0 copy-start.2
  60.5 0.3 collective-permute-done.6.low
  60.9 6.2 %collective-permute-done.7.high = bf16[256,512]{1,0:T(8,128)(2,1)} collective-permute-done((bf16[256,512]{1,0:T(8,128)(2,1)}, bf16[256,512]{1,0:T(8,128)(2,1)}, u32[]{:S(2)}, u32[]{:S(2)}) %collective-permute-start.7) | collective-permute-done | bytes 262176 | tf_op jit(solution)/shard_map/ppermute | solution.py:54
  67.1 0.0 collective-permute-done.4.m3
  67.1 0.0 collective-permute-done.5.p3
  67.1 0.0 copy-done.5
  67.1 2.5 %shard_map.75 = bf16[256,512]{1,0:T(8,128)(2,1)} custom-call(s32[2]{0:T(128)S(1)} %pad_add_fusion.place, bf16[8,192,512]{2,1,0:T(8,128)(2,1)S(1)} %shard_map.73.weight, f32[192,512]{1,0:T(8,128)S(1)} %shard_map.74.before, bf16[512,512]{1,0:T(8,128)(2,1)} %collective-permute-done.4.m3, bf16[512,512]{1,0:T(8,128)(2,1)} %collective-permute-done.5.p3, ...), custom_call_target="tpu_custom_call" | custom-call | flops 301989888 | bytes 4194304 | tf_op jit(solution)/shard_map/pallas_call | solution.py:243
  69.5 9.8 %all-to-all-start.1 = ((bf16[8,32,512]{2,1,0:T(8,128)(2,1)}), bf16[8,32,512]{2,1,0:T(8,128)(2,1)S(1)}, u32[]{:S(2)}, u32[]{:S(2)}) async-start(bf16[8,32,512]{2,1,0:T(8,128)(2,1)} %bitcast.5), calls=%async_computation.1 | async-start | bytes 524288 | tf_op jit(solution)/shard_map/all_to_all | solution.py:254
  79.4 0.0 copy-done.6
  79.4 0.0 copy-done.7
  79.4 0.1 dynamic-slice_maximum_fusion
  79.5 0.1 copy.13
  79.6 6.3 %all-to-all-done.1 = bf16[8,32,512]{2,1,0:T(8,128)(2,1)S(1)} async-done(((bf16[8,32,512]{2,1,0:T(8,128)(2,1)}), bf16[8,32,512]{2,1,0:T(8,128)(2,1)S(1)}, u32[]{:S(2)}, u32[]{:S(2)}) %all-to-all-start.1) | async-done | bytes 262176 | tf_op jit(solution)/shard_map/all_to_all | solution.py:254
  85.9 0.0 copy-done.1
  85.9 0.0 copy-done.2
  85.9 0.7 shard_map.76
  86.6 8.3 %all_to_all.16 = bf16[8,8,512]{2,1,0:T(8,128)(2,1)S(1)} all-to-all(bf16[8,8,512]{2,1,0:T(8,128)(2,1)S(1)} %bitcast.20), channel_id=1, replica_groups=mesh['seq'=8,'chan'=64] {'seq'}, dimensions={0} | all-to-all | bytes 131072 | tf_op jit(solution)/shard_map/all_to_all | solution.py:268
  94.9 0.6 copy.15
  (1 shorter events, 0.0 us)
Async XLA Ops:
  0.0 57.7 %copy-start = (bf16[3,64,4096]{2,1,0:T(8,128)(2,1)S(1)}, bf16[3,64,4096]{2,1,0:T(8,128)(2,1)}, u32[]{:S(2)}) copy-start(bf16[3,64,4096]{2,1,0:T(8,128)(2,1)} %param.8) | copy-start | bytes 4718596
  23.8 15.7 %collective-permute-start.2 = (bf16[512,512]{1,0:T(8,128)(2,1)S(1)}, bf16[512,512]{1,0:T(8,128)(2,1)S(1)}, u32[]{:S(2)}, u32[]{:S(2)}) collective-permute-start(bf16[512,512]{1,0:T(8,128)(2,1)S(1)} %bitcast.13), channel_id=1, source_target_pairs={{0,16},{1,17},{2,18},{3,19},{4,20},{5,21},{6,22},{7,23},{8,24},{9,... | collective-permute-start | bytes 1572872 | tf_op jit(solution)/shard_map/ppermute | solution.py:54
  28.0 17.9 %collective-permute-start.3 = (bf16[512,512]{1,0:T(8,128)(2,1)S(1)}, bf16[512,512]{1,0:T(8,128)(2,1)S(1)}, u32[]{:S(2)}, u32[]{:S(2)}) collective-permute-start(bf16[512,512]{1,0:T(8,128)(2,1)S(1)} %bitcast.14), channel_id=1, source_target_pairs={{0,48},{1,49},{2,50},{3,51},{4,52},{5,53},{6,54},{7,55},{8,56},{9,... | collective-permute-start | bytes 1572872 | tf_op jit(solution)/shard_map/ppermute | solution.py:54
  31.6 22.2 %collective-permute-start = (bf16[512,512]{1,0:T(8,128)(2,1)S(1)}, bf16[512,512]{1,0:T(8,128)(2,1)S(1)}, u32[]{:S(2)}, u32[]{:S(2)}) collective-permute-start(bf16[512,512]{1,0:T(8,128)(2,1)S(1)} %bitcast.15), channel_id=1, source_target_pairs={{0,8},{1,9},{2,10},{3,11},{4,12},{5,13},{6,14},{7,15},{8,16},{9,17... | collective-permute-start | bytes 1572872 | tf_op jit(solution)/shard_map/ppermute | solution.py:54
  34.4 24.3 %collective-permute-start.1 = (bf16[512,512]{1,0:T(8,128)(2,1)S(1)}, bf16[512,512]{1,0:T(8,128)(2,1)}, u32[]{:S(2)}, u32[]{:S(2)}) collective-permute-start(bf16[512,512]{1,0:T(8,128)(2,1)S(1)} %bitcast.16), channel_id=1, source_target_pairs={{0,56},{1,57},{2,58},{3,59},{4,60},{5,61},{6,62},{7,63},{8,0},{9,1... | collective-permute-start | bytes 1572872 | tf_op jit(solution)/shard_map/ppermute | solution.py:54
  39.5 27.6 %collective-permute-start.4 = (bf16[512,512]{1,0:T(8,128)(2,1)S(1)}, bf16[512,512]{1,0:T(8,128)(2,1)}, u32[]{:S(2)}, u32[]{:S(2)}) collective-permute-start(bf16[512,512]{1,0:T(8,128)(2,1)S(1)} %collective-permute-done.2.m2), channel_id=1, source_target_pairs={{0,8},{1,9},{2,10},{3,11},{4,12},{5,13},{6,14},{7,15},{8,16},{9,17... | collective-permute-start | bytes 1572872 | tf_op jit(solution)/shard_map/ppermute | solution.py:54
  46.0 21.1 %collective-permute-start.5 = (bf16[512,512]{1,0:T(8,128)(2,1)S(1)}, bf16[512,512]{1,0:T(8,128)(2,1)}, u32[]{:S(2)}, u32[]{:S(2)}) collective-permute-start(bf16[512,512]{1,0:T(8,128)(2,1)S(1)} %collective-permute-done.3.p2), channel_id=1, source_target_pairs={{0,56},{1,57},{2,58},{3,59},{4,60},{5,61},{6,62},{7,63},{8,0},{9,1... | collective-permute-start | bytes 1572872 | tf_op jit(solution)/shard_map/ppermute | solution.py:54
  48.6 12.2 %collective-permute-start.6 = (bf16[256,512]{1,0:T(8,128)(2,1)}, bf16[256,512]{1,0:T(8,128)(2,1)S(1)}, u32[]{:S(2)}, u32[]{:S(2)}) collective-permute-start(bf16[256,512]{1,0:T(8,128)(2,1)} %slice.8), channel_id=1, source_target_pairs={{0,16},{1,17},{2,18},{3,19},{4,20},{5,21},{6,22},{7,23},{8,24},{9,... | collective-permute-start | bytes 786440 | tf_op jit(solution)/shard_map/ppermute | solution.py:54
  53.8 0.8 copy-start.3
  54.6 12.4 %collective-permute-start.7 = (bf16[256,512]{1,0:T(8,128)(2,1)}, bf16[256,512]{1,0:T(8,128)(2,1)}, u32[]{:S(2)}, u32[]{:S(2)}) collective-permute-start(bf16[256,512]{1,0:T(8,128)(2,1)} %slice.9), channel_id=1, source_target_pairs={{0,48},{1,49},{2,50},{3,51},{4,52},{5,53},{6,54},{7,55},{8,56},{9,... | collective-permute-start | bytes 786440 | tf_op jit(solution)/shard_map/ppermute | solution.py:54
  57.7 1.1 %copy-start.4 = (bf16[512,512]{1,0:T(8,128)(2,1)S(1)}, bf16[512,512]{1,0:T(8,128)(2,1)}, u32[]{:S(2)}) copy-start(bf16[512,512]{1,0:T(8,128)(2,1)} %copy-done.3) | copy-start | bytes 1572868
  58.7 8.3 %copy-start.5 = (bf16[64,512]{1,0:T(8,128)(2,1)S(1)}, bf16[64,512]{1,0:T(8,128)(2,1)}, u32[]{:S(2)}) copy-start(bf16[64,512]{1,0:T(8,128)(2,1)} %lags.1) | copy-start | bytes 196612
  60.5 18.9 %copy-start.6 = (f32[3,3,64]{2,1,0:T(4,128)S(1)}, f32[3,3,64]{2,1,0:T(4,128)}, u32[]{:S(2)}) copy-start(f32[3,3,64]{2,1,0:T(4,128)} %param.9) | copy-start | bytes 6916
  60.5 18.9 %copy-start.7 = (f32[64]{0:T(128)S(1)}, f32[64]{0:T(128)}, u32[]{:S(2)}) copy-start(f32[64]{0:T(128)} %param.11) | copy-start | bytes 772
  60.5 25.4 %copy-start.1 = (bf16[512,1024]{1,0:T(8,128)(2,1)S(1)}, bf16[512,1024]{1,0:T(8,128)(2,1)}, u32[]{:S(2)}) copy-start(bf16[512,1024]{1,0:T(8,128)(2,1)} %constant.51.clone.forward) | copy-start | bytes 3145732
  60.5 25.4 %copy-start.2 = (bf16[1024,512]{1,0:T(8,128)(2,1)S(1)}, bf16[1024,512]{1,0:T(8,128)(2,1)}, u32[]{:S(2)}) copy-start(bf16[1024,512]{1,0:T(8,128)(2,1)} %constant.52.clone.inverse) | copy-start | bytes 3145732
  69.5 16.3 %all-to-all-start.1 = ((bf16[8,32,512]{2,1,0:T(8,128)(2,1)}), bf16[8,32,512]{2,1,0:T(8,128)(2,1)S(1)}, u32[]{:S(2)}, u32[]{:S(2)}) async-start(bf16[8,32,512]{2,1,0:T(8,128)(2,1)} %bitcast.5), calls=%async_computation.1 | async-start | bytes 524288 | tf_op jit(solution)/shard_map/all_to_all | solution.py:254

commit v2 on v1

--- a/solution.py
+++ b/solution.py
@@ -41,16 +41,17 @@
     ]
 
 
-def shift(block, step):
-    route = [
-        (
-            device_number(x, core, z, y),
-            device_number(x, core, z + step, y)
-            if core == 0
-            else device_number(x, core, z, y + step),
-        )
-        for x, core, z, y in devices()
-    ]
+def shift(block, even, odd):
+    route = []
+    for x, core, z, y in devices():
+        here = y if core else z
+        there = here + (odd if here % 2 else even)
+        route.append(
+            (
+                device_number(x, core, z, y),
+                device_number(x, core, z, there) if core else device_number(x, core, there, y),
+            )
+        )
     return lax.ppermute(block, BOTH, route)
 
 
@@ -99,28 +100,26 @@
             )
 
 
-def first_kernel(place, weight, own, m1, p1, m2, p2, out):
+def project(place, weight, blocks, total):
     r = place[1]
-    total = None
-    for offset, block in ((0, own), (-1, m1), (1, p1), (-2, m2), (2, p2)):
+    sign = 1 - 2 * lax.rem(r, 2)
+    for offset, block in blocks:
         part = jnp.dot(
-            weight[lax.rem(r + offset + RING, RING)], block[...], preferred_element_type=F32
+            weight[lax.rem(r + sign * offset + RING, RING)],
+            block[...],
+            preferred_element_type=F32,
         )
         total = part if total is None else total + part
-    out[...] = total
-
-
-def second_kernel(place, weight, before, m3, p3, low, high, lags, out):
-    r = place[1]
-    half = BLOCK // 2
-    total = before[...]
-    for offset, block in ((-3, m3), (3, p3)):
-        total = total + jnp.dot(
-            weight[lax.rem(r + offset + RING, RING)], block[...], preferred_element_type=F32
-        )
-    far = lax.rem(r + 4, RING)
-    total = total + jnp.dot(weight[far, :, :half], low[...], preferred_element_type=F32)
-    total = total + jnp.dot(weight[far, :, half:], high[...], preferred_element_type=F32)
+    return total
+
+
+def first_kernel(place, weight, own, one_a, one_b, two_a, two_b, out):
+    blocks = ((0, own), (1, one_a), (-1, one_b), (-2, two_a), (2, two_b))
+    out[...] = project(place, weight, blocks, None)
+
+
+def second_kernel(place, weight, before, four, three_a, three_b, lags, out):
+    total = project(place, weight, ((4, four), (3, three_a), (-3, three_b)), before[...])
     lag_rows = lags[...].astype(F32)
     pieces = []
     for d in range(RING):
@@ -216,18 +215,17 @@
         tiled=True,
         axis_index_groups=rings(),
     ).reshape(BLOCK, BLOCK)
-    m2, p2 = shift(own, 2), shift(own, -2)
-    m1, p1 = shift(own, 1), shift(own, -1)
-    half = BLOCK // 2
-    m3, p3 = shift(m2, 1), shift(p2, -1)
-    low, high = shift(m2[:half], 2), shift(p2[half:], -2)
+    two_a, two_b = shift(own, 2, -2), shift(own, -2, 2)
+    one_a, one_b = shift(own, 1, -1), shift(own, -1, 1)
+    four = shift(two_a, 2, -2)
+    three_a, three_b = shift(two_a, 1, -1), shift(two_b, -1, 1)
 
     weight = pl.pallas_call(
         weight_kernel,
         out_shape=jax.ShapeDtypeStruct((RING, 192, BLOCK), BF16),
         in_specs=[smem(), vmem()],
         out_specs=vmem(),
-        compiler_params=params(24),
+        compiler_params=params(12),
         cost_estimate=pl.CostEstimate(flops=0, bytes_accessed=3 << 20, transcendentals=0),
     )(place, in_weight.reshape(192, RING * BLOCK))
     before = pl.pallas_call(
@@ -235,21 +233,21 @@
         out_shape=jax.ShapeDtypeStruct((192, BLOCK), F32),
         in_specs=[smem()] + [vmem()] * 6,
         out_specs=vmem(),
-        compiler_params=params(24),
+        compiler_params=params(12),
         cost_estimate=pl.CostEstimate(
             flops=2 * 5 * 192 * BLOCK * BLOCK, bytes_accessed=4 << 20, transcendentals=0
         ),
-    )(place, weight, own, m1, p1, m2, p2)
+    )(place, weight, own, one_a, one_b, two_a, two_b)
     messages = pl.pallas_call(
         second_kernel,
         out_shape=jax.ShapeDtypeStruct((RING * 32, BLOCK), BF16),
-        in_specs=[smem()] + [vmem()] * 7,
-        out_specs=vmem(),
-        compiler_params=params(24),
+        in_specs=[smem()] + [vmem()] * 6,
+        out_specs=vmem(),
+        compiler_params=params(12),
         cost_estimate=pl.CostEstimate(
             flops=2 * 3 * 192 * BLOCK * BLOCK, bytes_accessed=4 << 20, transcendentals=0
         ),
-    )(place, weight, before, m3, p3, low, high, long_filter)
+    )(place, weight, before, four, three_a, three_b, long_filter)
 
     rows = lax.all_to_all(messages.reshape(RING, 32, BLOCK), "seq", 0, 0, tiled=True)
     taps = jnp.concatenate([short_taps.reshape(9, 64), skip_gain[None]], axis=0)
@@ -260,7 +258,7 @@
         out_shape=jax.ShapeDtypeStruct((RING * 8, BLOCK), BF16),
         in_specs=[vmem()] * 4,
         out_specs=vmem(),
-        compiler_params=params(32),
+        compiler_params=params(12),
         cost_estimate=pl.CostEstimate(
             flops=2 * (128 * 512 * 1024 + 64 * 1024 * 512), bytes_accessed=3 << 20, transcendentals=0
         ),

time: 96.1 us -> 91.9 us (0.956)
  waiting for transfers between devices: 15.4 us -> 12.5 us
  local copies, waits for them, and re-layouts: 4.04 us -> 1.75 us
    ppermute x8 -> x7, waiting for transfers between devices: 9.12 us -> 6.2 us  [shift(): return lax.ppermute(block, BOTH, route)]
    all_to_all x1, starting transfers between devices: 9.83 us -> 11.7 us  [on_device(): lax.all_to_all(messages.reshape(RING, 32, BLOCK), 'seq', 0, 0, tiled=True)]
    slice x2 -> x0, local copies, waits for them, and re-layouts: 1.47 us -> none  [on_device(): low, high = (shift(m2[:half], 2), shift(p2[half:], -2))]
    ppermute x8 -> x7, starting transfers between devices: 28.8 us -> 27.8 us  [shift(): return lax.ppermute(block, BOTH, route)]
  transfers between devices with their start and end apart: 9 -> 8, of which waited for: 5 -> 4; matrix products, arithmetic and copies ran while one was open for 2% -> 0% of each run, Pallas kernels for 3% -> 3%
where the time goes in v2:
time: 91.9 us; the launch traced here: 91.4 us
  starting transfers between devices  39.5 us (43%)
  blocking collectives  31.1 us (34%)
  waiting for transfers between devices  12.5 us (14%)
  Pallas kernels  6.21 us (7%)
  local copies, waits for them, and re-layouts  1.75 us (2%)
    ppermute x7, starting transfers between devices, shift(): return lax.ppermute(block, BOTH, route)  27.8 us
    all_to_all x1, blocking collectives, on_device(): lax.all_to_all(jnp.broadcast_to(shard[None], (RING,) + shard.shape), BOTH...  22.8 us
    all_to_all x1, starting transfers between devices, on_device(): lax.all_to_all(messages.reshape(RING, 32, BLOCK), 'seq', 0, 0, tiled=True)  11.7 us
    all_to_all x1, blocking collectives, on_device(): lax.all_to_all(mixed.reshape(RING, 8, BLOCK), 'seq', 0, 0, tiled=True)  8.26 us
    all_to_all x1, waiting for transfers between devices, on_device(): lax.all_to_all(messages.reshape(RING, 32, BLOCK), 'seq', 0, 0, tiled=True)  6.32 us
    ppermute x7, waiting for transfers between devices, shift(): return lax.ppermute(block, BOTH, route)  6.2 us
    pallas_call x1, Pallas kernels, on_device(): pl.pallas_call(second_kernel, out_shape=jax.ShapeDtypeStruct((RING * 32,...  2.56 us
    pallas_call x1, Pallas kernels, on_device(): pl.pallas_call(first_kernel, out_shape=jax.ShapeDtypeStruct((192, BLOCK),...  1.88 us
  transfers between devices with their start and end apart: 8, of which 4 were waited for; matrix products, arithmetic and copies ran while one was open for 0% of the time, Pallas kernels for 3%

profile of v2, /device:TPU:1, one launch (start us, length us, event | category | flops | bytes accessed | tf_op | source)
XLA Modules:
  0.0 91.4 jit_solution(203736685102728632)
XLA Ops:
  0.0 0.0 copy-start
  0.0 1.0 %broadcast_in_dim.4 = bf16[8,64,512]{2,1,0:T(8,128)(2,1)S(1)} broadcast(bf16[64,512]{1,0:T(8,128)(2,1)} %bitcast.23), dimensions={1,2} | broadcast | bytes 589824 | tf_op jit(solution)/shard_map/broadcast_in_dim | solution.py:211
  1.0 22.8 %all_to_all.15 = bf16[8,64,512]{2,1,0:T(8,128)(2,1)S(1)} all-to-all(bf16[8,64,512]{2,1,0:T(8,128)(2,1)S(1)} %broadcast_in_dim.4), channel_id=1, replica_groups={{0,1,2,3,4,5,6,7},{8,9,10,11,12,13,14,15},{16,17,18,19,20,21,22,23},{24..., dimensions={0} | all-to-all | bytes 1048576 | tf_op jit(solution)/shard_map/all_to_all | solution.py:210
  23.8 4.2 %collective-permute-start.2 = (bf16[512,512]{1,0:T(8,128)(2,1)S(1)}, bf16[512,512]{1,0:T(8,128)(2,1)S(1)}, u32[]{:S(2)}, u32[]{:S(2)}) collective-permute-start(bf16[512,512]{1,0:T(8,128)(2,1)S(1)} %bitcast.13), channel_id=1, source_target_pairs={{0,16},{1,17},{2,18},{3,19},{4,20},{5,21},{6,22},{7,23},{8,56},{9,... | collective-permute-start | bytes 1572872 | tf_op jit(solution)/shard_map/ppermute | solution.py:55
  28.0 3.6 %collective-permute-start.3 = (bf16[512,512]{1,0:T(8,128)(2,1)S(1)}, bf16[512,512]{1,0:T(8,128)(2,1)S(1)}, u32[]{:S(2)}, u32[]{:S(2)}) collective-permute-start(bf16[512,512]{1,0:T(8,128)(2,1)S(1)} %bitcast.14), channel_id=1, source_target_pairs={{0,48},{1,49},{2,50},{3,51},{4,52},{5,53},{6,54},{7,55},{8,24},{9,... | collective-permute-start | bytes 1572872 | tf_op jit(solution)/shard_map/ppermute | solution.py:55
  31.6 2.3 %collective-permute-start = (bf16[512,512]{1,0:T(8,128)(2,1)S(1)}, bf16[512,512]{1,0:T(8,128)(2,1)}, u32[]{:S(2)}, u32[]{:S(2)}) collective-permute-start(bf16[512,512]{1,0:T(8,128)(2,1)S(1)} %bitcast.15), channel_id=1, source_target_pairs={{0,8},{1,9},{2,10},{3,11},{4,12},{5,13},{6,14},{7,15},{8,0},{9,1},... | collective-permute-start | bytes 1572872 | tf_op jit(solution)/shard_map/ppermute | solution.py:55
  33.9 4.3 %collective-permute-start.1 = (bf16[512,512]{1,0:T(8,128)(2,1)S(1)}, bf16[512,512]{1,0:T(8,128)(2,1)}, u32[]{:S(2)}, u32[]{:S(2)}) collective-permute-start(bf16[512,512]{1,0:T(8,128)(2,1)S(1)} %bitcast.16), channel_id=1, source_target_pairs={{0,56},{1,57},{2,58},{3,59},{4,60},{5,61},{6,62},{7,63},{8,16},{9,... | collective-permute-start | bytes 1572872 | tf_op jit(solution)/shard_map/ppermute | solution.py:55
  38.2 0.0 collective-permute-done.2.two_a
  38.3 7.0 %collective-permute-start.4 = (bf16[512,512]{1,0:T(8,128)(2,1)S(1)}, bf16[512,512]{1,0:T(8,128)(2,1)}, u32[]{:S(2)}, u32[]{:S(2)}) collective-permute-start(bf16[512,512]{1,0:T(8,128)(2,1)S(1)} %collective-permute-done.2.two_a), channel_id=1, source_target_pairs={{0,16},{1,17},{2,18},{3,19},{4,20},{5,21},{6,22},{7,23},{8,56},{9,... | collective-permute-start | bytes 1572872 | tf_op jit(solution)/shard_map/ppermute | solution.py:55
  45.2 4.5 %collective-permute-start.5 = (bf16[512,512]{1,0:T(8,128)(2,1)S(1)}, bf16[512,512]{1,0:T(8,128)(2,1)}, u32[]{:S(2)}, u32[]{:S(2)}) collective-permute-start(bf16[512,512]{1,0:T(8,128)(2,1)S(1)} %collective-permute-done.2.two_a), channel_id=1, source_target_pairs={{0,8},{1,9},{2,10},{3,11},{4,12},{5,13},{6,14},{7,15},{8,0},{9,1},... | collective-permute-start | bytes 1572872 | tf_op jit(solution)/shard_map/ppermute | solution.py:55
  49.8 0.0 collective-permute-done.3.two_b
  49.8 1.9 %collective-permute-start.6 = (bf16[512,512]{1,0:T(8,128)(2,1)S(1)}, bf16[512,512]{1,0:T(8,128)(2,1)}, u32[]{:S(2)}, u32[]{:S(2)}) collective-permute-start(bf16[512,512]{1,0:T(8,128)(2,1)S(1)} %collective-permute-done.3.two_b), channel_id=1, source_target_pairs={{0,56},{1,57},{2,58},{3,59},{4,60},{5,61},{6,62},{7,63},{8,16},{9,... | collective-permute-start | bytes 1572872 | tf_op jit(solution)/shard_map/ppermute | solution.py:55
  51.7 0.1 pad_add_fusion.place
  51.8 0.0 copy-done
  51.8 1.0 %shard_map.73.weight = bf16[8,192,512]{2,1,0:T(8,128)(2,1)S(1)} custom-call(s32[2]{0:T(128)S(1)} %pad_add_fusion.place, bf16[192,4096]{1,0:T(8,128)(2,1)S(1)} %bitcast.18), custom_call_target="tpu_custom_call" | custom-call | bytes 3145728 | tf_op jit(solution)/shard_map/pallas_call | solution.py:223
  52.9 0.0 copy-start.3
  52.9 0.0 collective-permute-done.one_a
  52.9 0.0 collective-permute-done.1.one_b
  52.9 1.9 %shard_map.74.before = f32[192,512]{1,0:T(8,128)S(1)} custom-call(s32[2]{0:T(128)S(1)} %pad_add_fusion.place, bf16[8,192,512]{2,1,0:T(8,128)(2,1)S(1)} %shard_map.73.weight, bf16[512,512]{1,0:T(8,128)(2,1)S(1)} %bitcast.17, bf16[512,512]{1,0:T(8,128)(2,1)} %collective-permute-done.one_a, bf16[512,512]{1,0:T(8,128)(2,1)} %collective-permute-done.1.one_b, ...), custom_call_target="tpu_custom_call" | custom-call | flops 503316480 | bytes 4194304 | tf_op jit(solution)/shard_map/pallas_call | solution.py:231
  54.8 0.0 copy-start.4
  54.8 0.0 copy-start.5
  54.8 0.0 copy-start.1
  54.8 0.0 copy-start.2
  54.8 0.7 collective-permute-done.4.four
  55.5 4.6 %collective-permute-done.5.three_a = bf16[512,512]{1,0:T(8,128)(2,1)} collective-permute-done((bf16[512,512]{1,0:T(8,128)(2,1)S(1)}, bf16[512,512]{1,0:T(8,128)(2,1)}, u32[]{:S(2)}, u32[]{:S(2)}) %collective-permute-start.5) | collective-permute-done | bytes 524320 | tf_op jit(solution)/shard_map/ppermute | solution.py:55
  60.1 0.9 collective-permute-done.6.three_b
  61.0 0.0 copy-done.3
  61.0 2.6 %shard_map.75 = bf16[256,512]{1,0:T(8,128)(2,1)} custom-call(s32[2]{0:T(128)S(1)} %pad_add_fusion.place, bf16[8,192,512]{2,1,0:T(8,128)(2,1)S(1)} %shard_map.73.weight, f32[192,512]{1,0:T(8,128)S(1)} %shard_map.74.before, bf16[512,512]{1,0:T(8,128)(2,1)} %collective-permute-done.4.four, bf16[512,512]{1,0:T(8,128)(2,1)} %collective-permute-done.5.three_a, ...), custom_call_target="tpu_custom_call" | custom-call | flops 301989888 | bytes 4194304 | tf_op jit(solution)/shard_map/pallas_call | solution.py:241
  63.6 11.7 %all-to-all-start.1 = ((bf16[8,32,512]{2,1,0:T(8,128)(2,1)}), bf16[8,32,512]{2,1,0:T(8,128)(2,1)S(1)}, u32[]{:S(2)}, u32[]{:S(2)}) async-start(bf16[8,32,512]{2,1,0:T(8,128)(2,1)} %bitcast.5), calls=%async_computation.1 | async-start | bytes 524288 | tf_op jit(solution)/shard_map/all_to_all | solution.py:252
  75.3 0.0 copy-done.4
  75.3 0.0 copy-done.5
  75.3 0.1 dynamic-slice_maximum_fusion
  75.4 0.1 copy.13
  75.5 6.3 %all-to-all-done.1 = bf16[8,32,512]{2,1,0:T(8,128)(2,1)S(1)} async-done(((bf16[8,32,512]{2,1,0:T(8,128)(2,1)}), bf16[8,32,512]{2,1,0:T(8,128)(2,1)S(1)}, u32[]{:S(2)}, u32[]{:S(2)}) %all-to-all-start.1) | async-done | bytes 262176 | tf_op jit(solution)/shard_map/all_to_all | solution.py:252
  81.8 0.0 copy-done.1
  81.8 0.0 copy-done.2
  81.8 0.7 shard_map.76
  82.5 8.3 %all_to_all.16 = bf16[8,8,512]{2,1,0:T(8,128)(2,1)S(1)} all-to-all(bf16[8,8,512]{2,1,0:T(8,128)(2,1)S(1)} %bitcast.20), channel_id=1, replica_groups=mesh['seq'=8,'chan'=64] {'seq'}, dimensions={0} | all-to-all | bytes 131072 | tf_op jit(solution)/shard_map/all_to_all | solution.py:266
  90.8 0.6 copy.15
  (1 shorter events, 0.0 us)
Async XLA Ops:
  0.0 51.8 %copy-start = (bf16[3,64,4096]{2,1,0:T(8,128)(2,1)S(1)}, bf16[3,64,4096]{2,1,0:T(8,128)(2,1)}, u32[]{:S(2)}) copy-start(bf16[3,64,4096]{2,1,0:T(8,128)(2,1)} %param.8) | copy-start | bytes 4718596
  23.8 14.4 %collective-permute-start.2 = (bf16[512,512]{1,0:T(8,128)(2,1)S(1)}, bf16[512,512]{1,0:T(8,128)(2,1)S(1)}, u32[]{:S(2)}, u32[]{:S(2)}) collective-permute-start(bf16[512,512]{1,0:T(8,128)(2,1)S(1)} %bitcast.13), channel_id=1, source_target_pairs={{0,16},{1,17},{2,18},{3,19},{4,20},{5,21},{6,22},{7,23},{8,56},{9,... | collective-permute-start | bytes 1572872 | tf_op jit(solution)/shard_map/ppermute | solution.py:55
  28.0 21.7 %collective-permute-start.3 = (bf16[512,512]{1,0:T(8,128)(2,1)S(1)}, bf16[512,512]{1,0:T(8,128)(2,1)S(1)}, u32[]{:S(2)}, u32[]{:S(2)}) collective-permute-start(bf16[512,512]{1,0:T(8,128)(2,1)S(1)} %bitcast.14), channel_id=1, source_target_pairs={{0,48},{1,49},{2,50},{3,51},{4,52},{5,53},{6,54},{7,55},{8,24},{9,... | collective-permute-start | bytes 1572872 | tf_op jit(solution)/shard_map/ppermute | solution.py:55
  31.6 21.3 %collective-permute-start = (bf16[512,512]{1,0:T(8,128)(2,1)S(1)}, bf16[512,512]{1,0:T(8,128)(2,1)}, u32[]{:S(2)}, u32[]{:S(2)}) collective-permute-start(bf16[512,512]{1,0:T(8,128)(2,1)S(1)} %bitcast.15), channel_id=1, source_target_pairs={{0,8},{1,9},{2,10},{3,11},{4,12},{5,13},{6,14},{7,15},{8,0},{9,1},... | collective-permute-start | bytes 1572872 | tf_op jit(solution)/shard_map/ppermute | solution.py:55
  33.9 18.9 %collective-permute-start.1 = (bf16[512,512]{1,0:T(8,128)(2,1)S(1)}, bf16[512,512]{1,0:T(8,128)(2,1)}, u32[]{:S(2)}, u32[]{:S(2)}) collective-permute-start(bf16[512,512]{1,0:T(8,128)(2,1)S(1)} %bitcast.16), channel_id=1, source_target_pairs={{0,56},{1,57},{2,58},{3,59},{4,60},{5,61},{6,62},{7,63},{8,16},{9,... | collective-permute-start | bytes 1572872 | tf_op jit(solution)/shard_map/ppermute | solution.py:55
  38.3 17.3 %collective-permute-start.4 = (bf16[512,512]{1,0:T(8,128)(2,1)S(1)}, bf16[512,512]{1,0:T(8,128)(2,1)}, u32[]{:S(2)}, u32[]{:S(2)}) collective-permute-start(bf16[512,512]{1,0:T(8,128)(2,1)S(1)} %collective-permute-done.2.two_a), channel_id=1, source_target_pairs={{0,16},{1,17},{2,18},{3,19},{4,20},{5,21},{6,22},{7,23},{8,56},{9,... | collective-permute-start | bytes 1572872 | tf_op jit(solution)/shard_map/ppermute | solution.py:55
  45.2 14.9 %collective-permute-start.5 = (bf16[512,512]{1,0:T(8,128)(2,1)S(1)}, bf16[512,512]{1,0:T(8,128)(2,1)}, u32[]{:S(2)}, u32[]{:S(2)}) collective-permute-start(bf16[512,512]{1,0:T(8,128)(2,1)S(1)} %collective-permute-done.2.two_a), channel_id=1, source_target_pairs={{0,8},{1,9},{2,10},{3,11},{4,12},{5,13},{6,14},{7,15},{8,0},{9,1},... | collective-permute-start | bytes 1572872 | tf_op jit(solution)/shard_map/ppermute | solution.py:55
  49.8 11.2 %collective-permute-start.6 = (bf16[512,512]{1,0:T(8,128)(2,1)S(1)}, bf16[512,512]{1,0:T(8,128)(2,1)}, u32[]{:S(2)}, u32[]{:S(2)}) collective-permute-start(bf16[512,512]{1,0:T(8,128)(2,1)S(1)} %collective-permute-done.3.two_b), channel_id=1, source_target_pairs={{0,56},{1,57},{2,58},{3,59},{4,60},{5,61},{6,62},{7,63},{8,16},{9,... | collective-permute-start | bytes 1572872 | tf_op jit(solution)/shard_map/ppermute | solution.py:55
  52.9 8.2 %copy-start.3 = (bf16[64,512]{1,0:T(8,128)(2,1)S(1)}, bf16[64,512]{1,0:T(8,128)(2,1)}, u32[]{:S(2)}) copy-start(bf16[64,512]{1,0:T(8,128)(2,1)} %lags.1) | copy-start | bytes 196612
  54.8 20.5 %copy-start.4 = (f32[3,3,64]{2,1,0:T(4,128)S(1)}, f32[3,3,64]{2,1,0:T(4,128)}, u32[]{:S(2)}) copy-start(f32[3,3,64]{2,1,0:T(4,128)} %param.9) | copy-start | bytes 6916
  54.8 20.5 %copy-start.5 = (f32[64]{0:T(128)S(1)}, f32[64]{0:T(128)}, u32[]{:S(2)}) copy-start(f32[64]{0:T(128)} %param.11) | copy-start | bytes 772
  54.8 27.0 %copy-start.1 = (bf16[512,1024]{1,0:T(8,128)(2,1)S(1)}, bf16[512,1024]{1,0:T(8,128)(2,1)}, u32[]{:S(2)}) copy-start(bf16[512,1024]{1,0:T(8,128)(2,1)} %constant.51.clone.forward) | copy-start | bytes 3145732
  54.8 27.0 %copy-start.2 = (bf16[1024,512]{1,0:T(8,128)(2,1)S(1)}, bf16[1024,512]{1,0:T(8,128)(2,1)}, u32[]{:S(2)}) copy-start(bf16[1024,512]{1,0:T(8,128)(2,1)} %constant.52.clone.inverse) | copy-start | bytes 3145732
  63.6 18.2 %all-to-all-start.1 = ((bf16[8,32,512]{2,1,0:T(8,128)(2,1)}), bf16[8,32,512]{2,1,0:T(8,128)(2,1)S(1)}, u32[]{:S(2)}, u32[]{:S(2)}) async-start(bf16[8,32,512]{2,1,0:T(8,128)(2,1)} %bitcast.5), calls=%async_computation.1 | async-start | bytes 524288 | tf_op jit(solution)/shard_map/all_to_all | solution.py:252

commit v3 on v2

--- a/solution.py
+++ b/solution.py
@@ -118,8 +118,12 @@
     out[...] = project(place, weight, blocks, None)
 
 
-def second_kernel(place, weight, before, four, three_a, three_b, lags, out):
-    total = project(place, weight, ((4, four), (3, three_a), (-3, three_b)), before[...])
+def second_kernel(place, weight, before, four, three_a, out):
+    out[...] = project(place, weight, ((4, four), (3, three_a)), before[...])
+
+
+def third_kernel(place, weight, before, three_b, lags, out):
+    total = project(place, weight, ((-3, three_b),), before[...])
     lag_rows = lags[...].astype(F32)
     pieces = []
     for d in range(RING):
@@ -238,16 +242,26 @@
             flops=2 * 5 * 192 * BLOCK * BLOCK, bytes_accessed=4 << 20, transcendentals=0
         ),
     )(place, weight, own, one_a, one_b, two_a, two_b)
+    before = pl.pallas_call(
+        second_kernel,
+        out_shape=jax.ShapeDtypeStruct((192, BLOCK), F32),
+        in_specs=[smem()] + [vmem()] * 4,
+        out_specs=vmem(),
+        compiler_params=params(12),
+        cost_estimate=pl.CostEstimate(
+            flops=2 * 2 * 192 * BLOCK * BLOCK, bytes_accessed=3 << 20, transcendentals=0
+        ),
+    )(place, weight, before, four, three_a)
     messages = pl.pallas_call(
-        second_kernel,
+        third_kernel,
         out_shape=jax.ShapeDtypeStruct((RING * 32, BLOCK), BF16),
-        in_specs=[smem()] + [vmem()] * 6,
-        out_specs=vmem(),
-        compiler_params=params(12),
-        cost_estimate=pl.CostEstimate(
-            flops=2 * 3 * 192 * BLOCK * BLOCK, bytes_accessed=4 << 20, transcendentals=0
-        ),
-    )(place, weight, before, four, three_a, three_b, long_filter)
+        in_specs=[smem()] + [vmem()] * 4,
+        out_specs=vmem(),
+        compiler_params=params(12),
+        cost_estimate=pl.CostEstimate(
+            flops=2 * 192 * BLOCK * BLOCK, bytes_accessed=2 << 20, transcendentals=0
+        ),
+    )(place, weight, before, three_b, long_filter)
 
     rows = lax.all_to_all(messages.reshape(RING, 32, BLOCK), "seq", 0, 0, tiled=True)
     taps = jnp.concatenate([short_taps.reshape(9, 64), skip_gain[None]], axis=0)

time: 91.9 us -> 91.8 us (level)
  Pallas kernels: 6.21 us -> 7.41 us
    pallas_call x1 -> x2, Pallas kernels: 2.56 us -> 3.76 us  [the longest x1 2.18 us: on_device(): pl.pallas_call(third_kernel, out_shape=jax.ShapeDtypeStruct((RING * 32, B...]
  transfers between devices with their start and end apart: 8 -> 8, of which waited for: 4 -> 3; matrix products, arithmetic and copies ran while one was open for 0% -> 0% of each run, Pallas kernels for 3% -> 5%
where the time goes in v3:
time: 91.8 us; the launch traced here: 91.2 us
  starting transfers between devices  39 us (42%)
  blocking collectives  31.1 us (34%)
  waiting for transfers between devices  11.7 us (13%)
  Pallas kernels  7.41 us (8%)
  local copies, waits for them, and re-layouts  1.75 us (2%)
    ppermute x7, starting transfers between devices, shift(): return lax.ppermute(block, BOTH, route)  27.8 us
    all_to_all x1, blocking collectives, on_device(): lax.all_to_all(jnp.broadcast_to(shard[None], (RING,) + shard.shape), BOTH...  22.8 us
    all_to_all x1, starting transfers between devices, on_device(): lax.all_to_all(messages.reshape(RING, 32, BLOCK), 'seq', 0, 0, tiled=True)  11.1 us
    all_to_all x1, blocking collectives, on_device(): lax.all_to_all(mixed.reshape(RING, 8, BLOCK), 'seq', 0, 0, tiled=True)  8.26 us
    all_to_all x1, waiting for transfers between devices, on_device(): lax.all_to_all(messages.reshape(RING, 32, BLOCK), 'seq', 0, 0, tiled=True)  6.32 us
    ppermute x7, waiting for transfers between devices, shift(): return lax.ppermute(block, BOTH, route)  5.35 us
    pallas_call x1, Pallas kernels, on_device(): pl.pallas_call(third_kernel, out_shape=jax.ShapeDtypeStruct((RING * 32, B...  2.18 us
    pallas_call x1, Pallas kernels, on_device(): pl.pallas_call(first_kernel, out_shape=jax.ShapeDtypeStruct((192, BLOCK),...  1.89 us
  transfers between devices with their start and end apart: 8, of which 3 were waited for; matrix products, arithmetic and copies ran while one was open for 0% of the time, Pallas kernels for 5%

profile of v3, /device:TPU:1, one launch (start us, length us, event | category | flops | bytes accessed | tf_op | source)
XLA Modules:
  0.0 91.2 jit_solution(5226684839179447530)
XLA Ops:
  0.0 0.0 copy-start
  0.0 1.0 %broadcast_in_dim.4 = bf16[8,64,512]{2,1,0:T(8,128)(2,1)S(1)} broadcast(bf16[64,512]{1,0:T(8,128)(2,1)} %bitcast.23), dimensions={1,2} | broadcast | bytes 589824 | tf_op jit(solution)/shard_map/broadcast_in_dim | solution.py:215
  1.0 22.8 %all_to_all.15 = bf16[8,64,512]{2,1,0:T(8,128)(2,1)S(1)} all-to-all(bf16[8,64,512]{2,1,0:T(8,128)(2,1)S(1)} %broadcast_in_dim.4), channel_id=1, replica_groups={{0,1,2,3,4,5,6,7},{8,9,10,11,12,13,14,15},{16,17,18,19,20,21,22,23},{24..., dimensions={0} | all-to-all | bytes 1048576 | tf_op jit(solution)/shard_map/all_to_all | solution.py:214
  23.8 4.2 %collective-permute-start.2 = (bf16[512,512]{1,0:T(8,128)(2,1)S(1)}, bf16[512,512]{1,0:T(8,128)(2,1)S(1)}, u32[]{:S(2)}, u32[]{:S(2)}) collective-permute-start(bf16[512,512]{1,0:T(8,128)(2,1)S(1)} %bitcast.13), channel_id=1, source_target_pairs={{0,16},{1,17},{2,18},{3,19},{4,20},{5,21},{6,22},{7,23},{8,56},{9,... | collective-permute-start | bytes 1572872 | tf_op jit(solution)/shard_map/ppermute | solution.py:55
  28.0 3.6 %collective-permute-start.3 = (bf16[512,512]{1,0:T(8,128)(2,1)S(1)}, bf16[512,512]{1,0:T(8,128)(2,1)S(1)}, u32[]{:S(2)}, u32[]{:S(2)}) collective-permute-start(bf16[512,512]{1,0:T(8,128)(2,1)S(1)} %bitcast.14), channel_id=1, source_target_pairs={{0,48},{1,49},{2,50},{3,51},{4,52},{5,53},{6,54},{7,55},{8,24},{9,... | collective-permute-start | bytes 1572872 | tf_op jit(solution)/shard_map/ppermute | solution.py:55
  31.6 2.3 %collective-permute-start = (bf16[512,512]{1,0:T(8,128)(2,1)S(1)}, bf16[512,512]{1,0:T(8,128)(2,1)}, u32[]{:S(2)}, u32[]{:S(2)}) collective-permute-start(bf16[512,512]{1,0:T(8,128)(2,1)S(1)} %bitcast.15), channel_id=1, source_target_pairs={{0,8},{1,9},{2,10},{3,11},{4,12},{5,13},{6,14},{7,15},{8,0},{9,1},... | collective-permute-start | bytes 1572872 | tf_op jit(solution)/shard_map/ppermute | solution.py:55
  33.9 4.3 %collective-permute-start.1 = (bf16[512,512]{1,0:T(8,128)(2,1)S(1)}, bf16[512,512]{1,0:T(8,128)(2,1)}, u32[]{:S(2)}, u32[]{:S(2)}) collective-permute-start(bf16[512,512]{1,0:T(8,128)(2,1)S(1)} %bitcast.16), channel_id=1, source_target_pairs={{0,56},{1,57},{2,58},{3,59},{4,60},{5,61},{6,62},{7,63},{8,16},{9,... | collective-permute-start | bytes 1572872 | tf_op jit(solution)/shard_map/ppermute | solution.py:55
  38.2 0.0 collective-permute-done.2.two_a
  38.3 7.0 %collective-permute-start.4 = (bf16[512,512]{1,0:T(8,128)(2,1)S(1)}, bf16[512,512]{1,0:T(8,128)(2,1)}, u32[]{:S(2)}, u32[]{:S(2)}) collective-permute-start(bf16[512,512]{1,0:T(8,128)(2,1)S(1)} %collective-permute-done.2.two_a), channel_id=1, source_target_pairs={{0,16},{1,17},{2,18},{3,19},{4,20},{5,21},{6,22},{7,23},{8,56},{9,... | collective-permute-start | bytes 1572872 | tf_op jit(solution)/shard_map/ppermute | solution.py:55
  45.2 4.5 %collective-permute-start.5 = (bf16[512,512]{1,0:T(8,128)(2,1)S(1)}, bf16[512,512]{1,0:T(8,128)(2,1)}, u32[]{:S(2)}, u32[]{:S(2)}) collective-permute-start(bf16[512,512]{1,0:T(8,128)(2,1)S(1)} %collective-permute-done.2.two_a), channel_id=1, source_target_pairs={{0,8},{1,9},{2,10},{3,11},{4,12},{5,13},{6,14},{7,15},{8,0},{9,1},... | collective-permute-start | bytes 1572872 | tf_op jit(solution)/shard_map/ppermute | solution.py:55
  49.8 0.0 collective-permute-done.3.two_b
  49.8 1.9 %collective-permute-start.6 = (bf16[512,512]{1,0:T(8,128)(2,1)S(1)}, bf16[512,512]{1,0:T(8,128)(2,1)}, u32[]{:S(2)}, u32[]{:S(2)}) collective-permute-start(bf16[512,512]{1,0:T(8,128)(2,1)S(1)} %collective-permute-done.3.two_b), channel_id=1, source_target_pairs={{0,56},{1,57},{2,58},{3,59},{4,60},{5,61},{6,62},{7,63},{8,16},{9,... | collective-permute-start | bytes 1572872 | tf_op jit(solution)/shard_map/ppermute | solution.py:55
  51.7 0.1 pad_add_fusion.place
  51.8 0.0 copy-done
  51.8 1.0 %shard_map.73.weight = bf16[8,192,512]{2,1,0:T(8,128)(2,1)S(1)} custom-call(s32[2]{0:T(128)S(1)} %pad_add_fusion.place, bf16[192,4096]{1,0:T(8,128)(2,1)S(1)} %bitcast.18), custom_call_target="tpu_custom_call" | custom-call | bytes 3145728 | tf_op jit(solution)/shard_map/pallas_call | solution.py:227
  52.9 0.0 collective-permute-done.one_a
  52.9 0.0 collective-permute-done.1.one_b
  52.9 1.9 %shard_map.74.before = f32[192,512]{1,0:T(8,128)S(1)} custom-call(s32[2]{0:T(128)S(1)} %pad_add_fusion.place, bf16[8,192,512]{2,1,0:T(8,128)(2,1)S(1)} %shard_map.73.weight, bf16[512,512]{1,0:T(8,128)(2,1)S(1)} %bitcast.17, bf16[512,512]{1,0:T(8,128)(2,1)} %collective-permute-done.one_a, bf16[512,512]{1,0:T(8,128)(2,1)} %collective-permute-done.1.one_b, ...), custom_call_target="tpu_custom_call" | custom-call | flops 503316480 | bytes 4194304 | tf_op jit(solution)/shard_map/pallas_call | solution.py:235
  54.8 0.0 copy-start.3
  54.8 0.8 collective-permute-done.4.four
  55.5 4.6 %collective-permute-done.5.three_a = bf16[512,512]{1,0:T(8,128)(2,1)} collective-permute-done((bf16[512,512]{1,0:T(8,128)(2,1)S(1)}, bf16[512,512]{1,0:T(8,128)(2,1)}, u32[]{:S(2)}, u32[]{:S(2)}) %collective-permute-start.5) | collective-permute-done | bytes 524320 | tf_op jit(solution)/shard_map/ppermute | solution.py:55
  60.1 1.6 %shard_map.75.before = f32[192,512]{1,0:T(8,128)S(1)} custom-call(s32[2]{0:T(128)S(1)} %pad_add_fusion.place, bf16[8,192,512]{2,1,0:T(8,128)(2,1)S(1)} %shard_map.73.weight, f32[192,512]{1,0:T(8,128)S(1)} %shard_map.74.before, bf16[512,512]{1,0:T(8,128)(2,1)} %collective-permute-done.4.four, bf16[512,512]{1,0:T(8,128)(2,1)} %collective-permute-done.5.three_a), custom_call_target="tpu_custom_call" | custom-call | flops 201326592 | bytes 3145728 | tf_op jit(solution)/shard_map/pallas_call | solution.py:245
  61.7 0.0 copy-start.4
  61.7 0.0 copy-start.5
  61.7 0.0 copy-start.1
  61.7 0.0 copy-start.2
  61.8 0.0 collective-permute-done.6.three_b
  61.8 0.0 copy-done.3
  61.8 2.2 %shard_map.76 = bf16[256,512]{1,0:T(8,128)(2,1)} custom-call(s32[2]{0:T(128)S(1)} %pad_add_fusion.place, bf16[8,192,512]{2,1,0:T(8,128)(2,1)S(1)} %shard_map.73.weight, f32[192,512]{1,0:T(8,128)S(1)} %shard_map.75.before, bf16[512,512]{1,0:T(8,128)(2,1)} %collective-permute-done.6.three_b, bf16[64,512]{1,0:T(8,128)(2,1)S(1)} %copy-done.3), custom_call_target="tpu_custom_call" | custom-call | flops 100663296 | bytes 2097152 | tf_op jit(solution)/shard_map/pallas_call | solution.py:255
  64.0 11.1 %all-to-all-start.1 = ((bf16[8,32,512]{2,1,0:T(8,128)(2,1)}), bf16[8,32,512]{2,1,0:T(8,128)(2,1)S(1)}, u32[]{:S(2)}, u32[]{:S(2)}) async-start(bf16[8,32,512]{2,1,0:T(8,128)(2,1)} %bitcast.5), calls=%async_computation.1 | async-start | bytes 524288 | tf_op jit(solution)/shard_map/all_to_all | solution.py:266
  75.1 0.0 copy-done.4
  75.1 0.0 copy-done.5
  75.1 0.1 dynamic-slice_maximum_fusion
  75.2 0.1 copy.13
  75.3 6.3 %all-to-all-done.1 = bf16[8,32,512]{2,1,0:T(8,128)(2,1)S(1)} async-done(((bf16[8,32,512]{2,1,0:T(8,128)(2,1)}), bf16[8,32,512]{2,1,0:T(8,128)(2,1)S(1)}, u32[]{:S(2)}, u32[]{:S(2)}) %all-to-all-start.1) | async-done | bytes 262176 | tf_op jit(solution)/shard_map/all_to_all | solution.py:266
  81.6 0.0 copy-done.1
  81.6 0.0 copy-done.2
  81.6 0.7 shard_map.77
  82.3 8.3 %all_to_all.16 = bf16[8,8,512]{2,1,0:T(8,128)(2,1)S(1)} all-to-all(bf16[8,8,512]{2,1,0:T(8,128)(2,1)S(1)} %bitcast.20), channel_id=1, replica_groups=mesh['seq'=8,'chan'=64] {'seq'}, dimensions={0} | all-to-all | bytes 131072 | tf_op jit(solution)/shard_map/all_to_all | solution.py:280
  90.6 0.6 copy.15
  (1 shorter events, 0.0 us)
Async XLA Ops:
  0.0 51.8 %copy-start = (bf16[3,64,4096]{2,1,0:T(8,128)(2,1)S(1)}, bf16[3,64,4096]{2,1,0:T(8,128)(2,1)}, u32[]{:S(2)}) copy-start(bf16[3,64,4096]{2,1,0:T(8,128)(2,1)} %param.8) | copy-start | bytes 4718596
  23.8 14.4 %collective-permute-start.2 = (bf16[512,512]{1,0:T(8,128)(2,1)S(1)}, bf16[512,512]{1,0:T(8,128)(2,1)S(1)}, u32[]{:S(2)}, u32[]{:S(2)}) collective-permute-start(bf16[512,512]{1,0:T(8,128)(2,1)S(1)} %bitcast.13), channel_id=1, source_target_pairs={{0,16},{1,17},{2,18},{3,19},{4,20},{5,21},{6,22},{7,23},{8,56},{9,... | collective-permute-start | bytes 1572872 | tf_op jit(solution)/shard_map/ppermute | solution.py:55
  28.0 21.7 %collective-permute-start.3 = (bf16[512,512]{1,0:T(8,128)(2,1)S(1)}, bf16[512,512]{1,0:T(8,128)(2,1)S(1)}, u32[]{:S(2)}, u32[]{:S(2)}) collective-permute-start(bf16[512,512]{1,0:T(8,128)(2,1)S(1)} %bitcast.14), channel_id=1, source_target_pairs={{0,48},{1,49},{2,50},{3,51},{4,52},{5,53},{6,54},{7,55},{8,24},{9,... | collective-permute-start | bytes 1572872 | tf_op jit(solution)/shard_map/ppermute | solution.py:55
  31.6 21.2 %collective-permute-start = (bf16[512,512]{1,0:T(8,128)(2,1)S(1)}, bf16[512,512]{1,0:T(8,128)(2,1)}, u32[]{:S(2)}, u32[]{:S(2)}) collective-permute-start(bf16[512,512]{1,0:T(8,128)(2,1)S(1)} %bitcast.15), channel_id=1, source_target_pairs={{0,8},{1,9},{2,10},{3,11},{4,12},{5,13},{6,14},{7,15},{8,0},{9,1},... | collective-permute-start | bytes 1572872 | tf_op jit(solution)/shard_map/ppermute | solution.py:55
  33.9 18.9 %collective-permute-start.1 = (bf16[512,512]{1,0:T(8,128)(2,1)S(1)}, bf16[512,512]{1,0:T(8,128)(2,1)}, u32[]{:S(2)}, u32[]{:S(2)}) collective-permute-start(bf16[512,512]{1,0:T(8,128)(2,1)S(1)} %bitcast.16), channel_id=1, source_target_pairs={{0,56},{1,57},{2,58},{3,59},{4,60},{5,61},{6,62},{7,63},{8,16},{9,... | collective-permute-start | bytes 1572872 | tf_op jit(solution)/shard_map/ppermute | solution.py:55
  38.3 17.3 %collective-permute-start.4 = (bf16[512,512]{1,0:T(8,128)(2,1)S(1)}, bf16[512,512]{1,0:T(8,128)(2,1)}, u32[]{:S(2)}, u32[]{:S(2)}) collective-permute-start(bf16[512,512]{1,0:T(8,128)(2,1)S(1)} %collective-permute-done.2.two_a), channel_id=1, source_target_pairs={{0,16},{1,17},{2,18},{3,19},{4,20},{5,21},{6,22},{7,23},{8,56},{9,... | collective-permute-start | bytes 1572872 | tf_op jit(solution)/shard_map/ppermute | solution.py:55
  45.2 14.9 %collective-permute-start.5 = (bf16[512,512]{1,0:T(8,128)(2,1)S(1)}, bf16[512,512]{1,0:T(8,128)(2,1)}, u32[]{:S(2)}, u32[]{:S(2)}) collective-permute-start(bf16[512,512]{1,0:T(8,128)(2,1)S(1)} %collective-permute-done.2.two_a), channel_id=1, source_target_pairs={{0,8},{1,9},{2,10},{3,11},{4,12},{5,13},{6,14},{7,15},{8,0},{9,1},... | collective-permute-start | bytes 1572872 | tf_op jit(solution)/shard_map/ppermute | solution.py:55
  49.8 12.0 %collective-permute-start.6 = (bf16[512,512]{1,0:T(8,128)(2,1)S(1)}, bf16[512,512]{1,0:T(8,128)(2,1)}, u32[]{:S(2)}, u32[]{:S(2)}) collective-permute-start(bf16[512,512]{1,0:T(8,128)(2,1)S(1)} %collective-permute-done.3.two_b), channel_id=1, source_target_pairs={{0,56},{1,57},{2,58},{3,59},{4,60},{5,61},{6,62},{7,63},{8,16},{9,... | collective-permute-start | bytes 1572872 | tf_op jit(solution)/shard_map/ppermute | solution.py:55
  54.8 7.0 %copy-start.3 = (bf16[64,512]{1,0:T(8,128)(2,1)S(1)}, bf16[64,512]{1,0:T(8,128)(2,1)}, u32[]{:S(2)}) copy-start(bf16[64,512]{1,0:T(8,128)(2,1)} %lags.1) | copy-start | bytes 196612
  61.7 13.4 %copy-start.4 = (f32[3,3,64]{2,1,0:T(4,128)S(1)}, f32[3,3,64]{2,1,0:T(4,128)}, u32[]{:S(2)}) copy-start(f32[3,3,64]{2,1,0:T(4,128)} %param.9) | copy-start | bytes 6916
  61.7 13.4 %copy-start.5 = (f32[64]{0:T(128)S(1)}, f32[64]{0:T(128)}, u32[]{:S(2)}) copy-start(f32[64]{0:T(128)} %param.11) | copy-start | bytes 772
  61.7 19.9 %copy-start.1 = (bf16[512,1024]{1,0:T(8,128)(2,1)S(1)}, bf16[512,1024]{1,0:T(8,128)(2,1)}, u32[]{:S(2)}) copy-start(bf16[512,1024]{1,0:T(8,128)(2,1)} %constant.51.clone.forward) | copy-start | bytes 3145732
  61.7 19.9 %copy-start.2 = (bf16[1024,512]{1,0:T(8,128)(2,1)S(1)}, bf16[1024,512]{1,0:T(8,128)(2,1)}, u32[]{:S(2)}) copy-start(bf16[1024,512]{1,0:T(8,128)(2,1)} %constant.52.clone.inverse) | copy-start | bytes 3145732
  64.0 17.6 %all-to-all-start.1 = ((bf16[8,32,512]{2,1,0:T(8,128)(2,1)}), bf16[8,32,512]{2,1,0:T(8,128)(2,1)S(1)}, u32[]{:S(2)}, u32[]{:S(2)}) async-start(bf16[8,32,512]{2,1,0:T(8,128)(2,1)} %bitcast.5), calls=%async_computation.1 | async-start | bytes 524288 | tf_op jit(solution)/shard_map/all_to_all | solution.py:266

commit v4 on v3

--- a/solution.py
+++ b/solution.py
@@ -224,6 +224,10 @@
     four = shift(two_a, 2, -2)
     three_a, three_b = shift(two_a, 1, -1), shift(two_b, -1, 1)
 
+    taps = jnp.concatenate([short_taps.reshape(9, 64), skip_gain[None]], axis=0)
+    taps = lax.dynamic_slice_in_dim(taps, position * 8, 8, axis=1).T
+    place, taps = lax.optimization_barrier((place, taps))
+
     weight = pl.pallas_call(
         weight_kernel,
         out_shape=jax.ShapeDtypeStruct((RING, 192, BLOCK), BF16),
@@ -264,8 +268,6 @@
     )(place, weight, before, three_b, long_filter)
 
     rows = lax.all_to_all(messages.reshape(RING, 32, BLOCK), "seq", 0, 0, tiled=True)
-    taps = jnp.concatenate([short_taps.reshape(9, 64), skip_gain[None]], axis=0)
-    taps = lax.dynamic_slice_in_dim(taps, position * 8, 8, axis=1).T
     forward, inverse = tables()
     mixed = pl.pallas_call(
         conv_kernel,

time: 91.8 us -> 90.8 us (0.989)
  blocking collectives: 31.1 us -> 48.5 us
  starting transfers between devices: 39 us -> 27.8 us
  waiting for transfers between devices: 11.7 us -> 5.16 us
    all_to_all x0 -> x1, blocking collectives: none -> 17.4 us  [on_device(): lax.all_to_all(messages.reshape(RING, 32, BLOCK), 'seq', 0, 0, tiled=True)]
    all_to_all x1 -> x0, starting transfers between devices: 11.1 us -> none  [on_device(): lax.all_to_all(messages.reshape(RING, 32, BLOCK), 'seq', 0, 0, tiled=True)]
    all_to_all x1 -> x0, waiting for transfers between devices: 6.32 us -> none  [on_device(): lax.all_to_all(messages.reshape(RING, 32, BLOCK), 'seq', 0, 0, tiled=True)]
  transfers between devices with their start and end apart: 8 -> 7, of which waited for: 3 -> 2; matrix products, arithmetic and copies ran while one was open for 0% -> 0% of each run, Pallas kernels for 5% -> 5%
where the time goes in v4:
time: 90.8 us; the launch traced here: 90.3 us
  blocking collectives  48.5 us (53%)
  starting transfers between devices  27.8 us (31%)
  Pallas kernels  6.72 us (7%)
  waiting for transfers between devices  5.16 us (6%)
  local copies, waits for them, and re-layouts  1.75 us (2%)
    ppermute x7, starting transfers between devices, shift(): return lax.ppermute(block, BOTH, route)  27.8 us
    all_to_all x1, blocking collectives, on_device(): lax.all_to_all(jnp.broadcast_to(shard[None], (RING,) + shard.shape), BOTH...  22.8 us
    all_to_all x1, blocking collectives, on_device(): lax.all_to_all(messages.reshape(RING, 32, BLOCK), 'seq', 0, 0, tiled=True)  17.4 us
    all_to_all x1, blocking collectives, on_device(): lax.all_to_all(mixed.reshape(RING, 8, BLOCK), 'seq', 0, 0, tiled=True)  8.26 us
    ppermute x7, waiting for transfers between devices, shift(): return lax.ppermute(block, BOTH, route)  5.16 us
    pallas_call x1, Pallas kernels, on_device(): pl.pallas_call(first_kernel, out_shape=jax.ShapeDtypeStruct((192, BLOCK),...  1.88 us
  transfers between devices with their start and end apart: 7, of which 2 were waited for; matrix products, arithmetic and copies ran while one was open for 0% of the time, Pallas kernels for 5%

profile of v4, /device:TPU:1, one launch (start us, length us, event | category | flops | bytes accessed | tf_op | source)
XLA Modules:
  0.0 90.3 jit_solution(12757291058900502373)
XLA Ops:
  0.0 0.0 copy-start.4
  0.0 0.0 copy-start.5
  0.0 0.0 copy-start
  0.0 1.0 %broadcast_in_dim.10 = bf16[8,64,512]{2,1,0:T(8,128)(2,1)S(1)} broadcast(bf16[64,512]{1,0:T(8,128)(2,1)} %bitcast.24), dimensions={1,2} | broadcast | bytes 589824 | tf_op jit(solution)/shard_map/broadcast_in_dim | solution.py:215
  1.0 22.8 %all_to_all.15 = bf16[8,64,512]{2,1,0:T(8,128)(2,1)S(1)} all-to-all(bf16[8,64,512]{2,1,0:T(8,128)(2,1)S(1)} %broadcast_in_dim.10), channel_id=1, replica_groups={{0,1,2,3,4,5,6,7},{8,9,10,11,12,13,14,15},{16,17,18,19,20,21,22,23},{24..., dimensions={0} | all-to-all | bytes 1048576 | tf_op jit(solution)/shard_map/all_to_all | solution.py:214
  23.8 4.2 %collective-permute-start.2 = (bf16[512,512]{1,0:T(8,128)(2,1)S(1)}, bf16[512,512]{1,0:T(8,128)(2,1)S(1)}, u32[]{:S(2)}, u32[]{:S(2)}) collective-permute-start(bf16[512,512]{1,0:T(8,128)(2,1)S(1)} %bitcast.13), channel_id=1, source_target_pairs={{0,16},{1,17},{2,18},{3,19},{4,20},{5,21},{6,22},{7,23},{8,56},{9,... | collective-permute-start | bytes 1572872 | tf_op jit(solution)/shard_map/ppermute | solution.py:55
  28.0 3.6 %collective-permute-start.3 = (bf16[512,512]{1,0:T(8,128)(2,1)S(1)}, bf16[512,512]{1,0:T(8,128)(2,1)S(1)}, u32[]{:S(2)}, u32[]{:S(2)}) collective-permute-start(bf16[512,512]{1,0:T(8,128)(2,1)S(1)} %bitcast.14), channel_id=1, source_target_pairs={{0,48},{1,49},{2,50},{3,51},{4,52},{5,53},{6,54},{7,55},{8,24},{9,... | collective-permute-start | bytes 1572872 | tf_op jit(solution)/shard_map/ppermute | solution.py:55
  31.6 2.3 %collective-permute-start = (bf16[512,512]{1,0:T(8,128)(2,1)S(1)}, bf16[512,512]{1,0:T(8,128)(2,1)}, u32[]{:S(2)}, u32[]{:S(2)}) collective-permute-start(bf16[512,512]{1,0:T(8,128)(2,1)S(1)} %bitcast.15), channel_id=1, source_target_pairs={{0,8},{1,9},{2,10},{3,11},{4,12},{5,13},{6,14},{7,15},{8,0},{9,1},... | collective-permute-start | bytes 1572872 | tf_op jit(solution)/shard_map/ppermute | solution.py:55
  33.9 4.3 %collective-permute-start.1 = (bf16[512,512]{1,0:T(8,128)(2,1)S(1)}, bf16[512,512]{1,0:T(8,128)(2,1)}, u32[]{:S(2)}, u32[]{:S(2)}) collective-permute-start(bf16[512,512]{1,0:T(8,128)(2,1)S(1)} %bitcast.16), channel_id=1, source_target_pairs={{0,56},{1,57},{2,58},{3,59},{4,60},{5,61},{6,62},{7,63},{8,16},{9,... | collective-permute-start | bytes 1572872 | tf_op jit(solution)/shard_map/ppermute | solution.py:55
  38.3 0.0 collective-permute-done.2.two_a
  38.3 7.0 %collective-permute-start.4 = (bf16[512,512]{1,0:T(8,128)(2,1)S(1)}, bf16[512,512]{1,0:T(8,128)(2,1)}, u32[]{:S(2)}, u32[]{:S(2)}) collective-permute-start(bf16[512,512]{1,0:T(8,128)(2,1)S(1)} %collective-permute-done.2.two_a), channel_id=1, source_target_pairs={{0,16},{1,17},{2,18},{3,19},{4,20},{5,21},{6,22},{7,23},{8,56},{9,... | collective-permute-start | bytes 1572872 | tf_op jit(solution)/shard_map/ppermute | solution.py:55
  45.2 4.5 %collective-permute-start.5 = (bf16[512,512]{1,0:T(8,128)(2,1)S(1)}, bf16[512,512]{1,0:T(8,128)(2,1)}, u32[]{:S(2)}, u32[]{:S(2)}) collective-permute-start(bf16[512,512]{1,0:T(8,128)(2,1)S(1)} %collective-permute-done.2.two_a), channel_id=1, source_target_pairs={{0,8},{1,9},{2,10},{3,11},{4,12},{5,13},{6,14},{7,15},{8,0},{9,1},... | collective-permute-start | bytes 1572872 | tf_op jit(solution)/shard_map/ppermute | solution.py:55
  49.8 0.0 collective-permute-done.3.two_b
  49.8 1.9 %collective-permute-start.6 = (bf16[512,512]{1,0:T(8,128)(2,1)S(1)}, bf16[512,512]{1,0:T(8,128)(2,1)}, u32[]{:S(2)}, u32[]{:S(2)}) collective-permute-start(bf16[512,512]{1,0:T(8,128)(2,1)S(1)} %collective-permute-done.3.two_b), channel_id=1, source_target_pairs={{0,56},{1,57},{2,58},{3,59},{4,60},{5,61},{6,62},{7,63},{8,16},{9,... | collective-permute-start | bytes 1572872 | tf_op jit(solution)/shard_map/ppermute | solution.py:55
  51.7 0.0 copy-done.4
  51.8 0.0 copy-done.5
  51.8 0.1 dynamic-slice_maximum_fusion
  51.9 0.1 copy.13
  51.9 0.1 pad_add_fusion.place
  52.0 0.0 copy-done
  52.0 1.0 %shard_map.73.weight = bf16[8,192,512]{2,1,0:T(8,128)(2,1)S(1)} custom-call(s32[2]{0:T(128)S(1)} %pad_add_fusion.place, bf16[192,4096]{1,0:T(8,128)(2,1)S(1)} %bitcast.18), custom_call_target="tpu_custom_call" | custom-call | bytes 3145728 | tf_op jit(solution)/shard_map/pallas_call | solution.py:231
  53.1 0.0 collective-permute-done.one_a
  53.1 0.0 collective-permute-done.1.one_b
  53.1 1.9 %shard_map.74.before = f32[192,512]{1,0:T(8,128)S(1)} custom-call(s32[2]{0:T(128)S(1)} %pad_add_fusion.place, bf16[8,192,512]{2,1,0:T(8,128)(2,1)S(1)} %shard_map.73.weight, bf16[512,512]{1,0:T(8,128)(2,1)S(1)} %bitcast.17, bf16[512,512]{1,0:T(8,128)(2,1)} %collective-permute-done.one_a, bf16[512,512]{1,0:T(8,128)(2,1)} %collective-permute-done.1.one_b, ...), custom_call_target="tpu_custom_call" | custom-call | flops 503316480 | bytes 4194304 | tf_op jit(solution)/shard_map/pallas_call | solution.py:239
  55.0 0.0 copy-start.3
  55.0 0.6 collective-permute-done.4.four
  55.5 4.6 %collective-permute-done.5.three_a = bf16[512,512]{1,0:T(8,128)(2,1)} collective-permute-done((bf16[512,512]{1,0:T(8,128)(2,1)S(1)}, bf16[512,512]{1,0:T(8,128)(2,1)}, u32[]{:S(2)}, u32[]{:S(2)}) %collective-permute-start.5) | collective-permute-done | bytes 524320 | tf_op jit(solution)/shard_map/ppermute | solution.py:55
  60.1 1.6 %shard_map.75.before = f32[192,512]{1,0:T(8,128)S(1)} custom-call(s32[2]{0:T(128)S(1)} %pad_add_fusion.place, bf16[8,192,512]{2,1,0:T(8,128)(2,1)S(1)} %shard_map.73.weight, f32[192,512]{1,0:T(8,128)S(1)} %shard_map.74.before, bf16[512,512]{1,0:T(8,128)(2,1)} %collective-permute-done.4.four, bf16[512,512]{1,0:T(8,128)(2,1)} %collective-permute-done.5.three_a), custom_call_target="tpu_custom_call" | custom-call | flops 201326592 | bytes 3145728 | tf_op jit(solution)/shard_map/pallas_call | solution.py:249
  61.7 0.0 copy-start.1
  61.7 0.0 copy-start.2
  61.7 0.0 collective-permute-done.6.three_b
  61.7 0.0 copy-done.3
  61.8 1.5 %shard_map.76 = bf16[256,512]{1,0:T(8,128)(2,1)S(1)} custom-call(s32[2]{0:T(128)S(1)} %pad_add_fusion.place, bf16[8,192,512]{2,1,0:T(8,128)(2,1)S(1)} %shard_map.73.weight, f32[192,512]{1,0:T(8,128)S(1)} %shard_map.75.before, bf16[512,512]{1,0:T(8,128)(2,1)} %collective-permute-done.6.three_b, bf16[64,512]{1,0:T(8,128)(2,1)S(1)} %copy-done.3), custom_call_target="tpu_custom_call" | custom-call | flops 100663296 | bytes 2097152 | tf_op jit(solution)/shard_map/pallas_call | solution.py:259
  63.2 17.4 %all_to_all.16 = bf16[8,32,512]{2,1,0:T(8,128)(2,1)S(1)} all-to-all(bf16[8,32,512]{2,1,0:T(8,128)(2,1)S(1)} %bitcast.19), channel_id=1, replica_groups=mesh['seq'=8,'chan'=64] {'seq'}, dimensions={0} | all-to-all | bytes 524288 | tf_op jit(solution)/shard_map/all_to_all | solution.py:270
  80.7 0.0 copy-done.1
  80.7 0.0 copy-done.2
  80.7 0.8 shard_map.77
  81.4 8.3 %all_to_all.17 = bf16[8,8,512]{2,1,0:T(8,128)(2,1)S(1)} all-to-all(bf16[8,8,512]{2,1,0:T(8,128)(2,1)S(1)} %bitcast.21), channel_id=1, replica_groups=mesh['seq'=8,'chan'=64] {'seq'}, dimensions={0} | all-to-all | bytes 131072 | tf_op jit(solution)/shard_map/all_to_all | solution.py:282
  89.7 0.6 copy.15
  (1 shorter events, 0.0 us)
Async XLA Ops:
  0.0 51.7 %copy-start.4 = (f32[3,3,64]{2,1,0:T(4,128)S(1)}, f32[3,3,64]{2,1,0:T(4,128)}, u32[]{:S(2)}) copy-start(f32[3,3,64]{2,1,0:T(4,128)} %param.9) | copy-start | bytes 6916
  0.0 51.8 %copy-start.5 = (f32[64]{0:T(128)S(1)}, f32[64]{0:T(128)}, u32[]{:S(2)}) copy-start(f32[64]{0:T(128)} %param.11) | copy-start | bytes 772
  0.0 52.0 %copy-start = (bf16[3,64,4096]{2,1,0:T(8,128)(2,1)S(1)}, bf16[3,64,4096]{2,1,0:T(8,128)(2,1)}, u32[]{:S(2)}) copy-start(bf16[3,64,4096]{2,1,0:T(8,128)(2,1)} %param.8) | copy-start | bytes 4718596
  23.8 14.4 %collective-permute-start.2 = (bf16[512,512]{1,0:T(8,128)(2,1)S(1)}, bf16[512,512]{1,0:T(8,128)(2,1)S(1)}, u32[]{:S(2)}, u32[]{:S(2)}) collective-permute-start(bf16[512,512]{1,0:T(8,128)(2,1)S(1)} %bitcast.13), channel_id=1, source_target_pairs={{0,16},{1,17},{2,18},{3,19},{4,20},{5,21},{6,22},{7,23},{8,56},{9,... | collective-permute-start | bytes 1572872 | tf_op jit(solution)/shard_map/ppermute | solution.py:55
  28.0 21.7 %collective-permute-start.3 = (bf16[512,512]{1,0:T(8,128)(2,1)S(1)}, bf16[512,512]{1,0:T(8,128)(2,1)S(1)}, u32[]{:S(2)}, u32[]{:S(2)}) collective-permute-start(bf16[512,512]{1,0:T(8,128)(2,1)S(1)} %bitcast.14), channel_id=1, source_target_pairs={{0,48},{1,49},{2,50},{3,51},{4,52},{5,53},{6,54},{7,55},{8,24},{9,... | collective-permute-start | bytes 1572872 | tf_op jit(solution)/shard_map/ppermute | solution.py:55
  31.6 21.4 %collective-permute-start = (bf16[512,512]{1,0:T(8,128)(2,1)S(1)}, bf16[512,512]{1,0:T(8,128)(2,1)}, u32[]{:S(2)}, u32[]{:S(2)}) collective-permute-start(bf16[512,512]{1,0:T(8,128)(2,1)S(1)} %bitcast.15), channel_id=1, source_target_pairs={{0,8},{1,9},{2,10},{3,11},{4,12},{5,13},{6,14},{7,15},{8,0},{9,1},... | collective-permute-start | bytes 1572872 | tf_op jit(solution)/shard_map/ppermute | solution.py:55
  33.9 19.1 %collective-permute-start.1 = (bf16[512,512]{1,0:T(8,128)(2,1)S(1)}, bf16[512,512]{1,0:T(8,128)(2,1)}, u32[]{:S(2)}, u32[]{:S(2)}) collective-permute-start(bf16[512,512]{1,0:T(8,128)(2,1)S(1)} %bitcast.16), channel_id=1, source_target_pairs={{0,56},{1,57},{2,58},{3,59},{4,60},{5,61},{6,62},{7,63},{8,16},{9,... | collective-permute-start | bytes 1572872 | tf_op jit(solution)/shard_map/ppermute | solution.py:55
  38.3 17.3 %collective-permute-start.4 = (bf16[512,512]{1,0:T(8,128)(2,1)S(1)}, bf16[512,512]{1,0:T(8,128)(2,1)}, u32[]{:S(2)}, u32[]{:S(2)}) collective-permute-start(bf16[512,512]{1,0:T(8,128)(2,1)S(1)} %collective-permute-done.2.two_a), channel_id=1, source_target_pairs={{0,16},{1,17},{2,18},{3,19},{4,20},{5,21},{6,22},{7,23},{8,56},{9,... | collective-permute-start | bytes 1572872 | tf_op jit(solution)/shard_map/ppermute | solution.py:55
  45.2 14.9 %collective-permute-start.5 = (bf16[512,512]{1,0:T(8,128)(2,1)S(1)}, bf16[512,512]{1,0:T(8,128)(2,1)}, u32[]{:S(2)}, u32[]{:S(2)}) collective-permute-start(bf16[512,512]{1,0:T(8,128)(2,1)S(1)} %collective-permute-done.2.two_a), channel_id=1, source_target_pairs={{0,8},{1,9},{2,10},{3,11},{4,12},{5,13},{6,14},{7,15},{8,0},{9,1},... | collective-permute-start | bytes 1572872 | tf_op jit(solution)/shard_map/ppermute | solution.py:55
  49.8 12.0 %collective-permute-start.6 = (bf16[512,512]{1,0:T(8,128)(2,1)S(1)}, bf16[512,512]{1,0:T(8,128)(2,1)}, u32[]{:S(2)}, u32[]{:S(2)}) collective-permute-start(bf16[512,512]{1,0:T(8,128)(2,1)S(1)} %collective-permute-done.3.two_b), channel_id=1, source_target_pairs={{0,56},{1,57},{2,58},{3,59},{4,60},{5,61},{6,62},{7,63},{8,16},{9,... | collective-permute-start | bytes 1572872 | tf_op jit(solution)/shard_map/ppermute | solution.py:55
  55.0 6.8 %copy-start.3 = (bf16[64,512]{1,0:T(8,128)(2,1)S(1)}, bf16[64,512]{1,0:T(8,128)(2,1)}, u32[]{:S(2)}) copy-start(bf16[64,512]{1,0:T(8,128)(2,1)} %lags.1) | copy-start | bytes 196612
  61.7 19.0 %copy-start.1 = (bf16[512,1024]{1,0:T(8,128)(2,1)S(1)}, bf16[512,1024]{1,0:T(8,128)(2,1)}, u32[]{:S(2)}) copy-start(bf16[512,1024]{1,0:T(8,128)(2,1)} %constant.51.clone.forward) | copy-start | bytes 3145732
  61.7 18.9 %copy-start.2 = (bf16[1024,512]{1,0:T(8,128)(2,1)S(1)}, bf16[1024,512]{1,0:T(8,128)(2,1)}, u32[]{:S(2)}) copy-start(bf16[1024,512]{1,0:T(8,128)(2,1)} %constant.52.clone.inverse) | copy-start | bytes 3145732

commit v5 on v2

--- a/solution.py
+++ b/solution.py
@@ -32,7 +32,7 @@
 def rings():
     return [
         [
-            device_number(x, core, line, i) if core == 0 else device_number(x, core, i, line)
+            device_number(x, core, line, i) if core == 1 else device_number(x, core, i, line)
             for i in range(RING)
         ]
         for x in range(4)
@@ -44,12 +44,12 @@
 def shift(block, even, odd):
     route = []
     for x, core, z, y in devices():
-        here = y if core else z
+        here = z if core else y
         there = here + (odd if here % 2 else even)
         route.append(
             (
                 device_number(x, core, z, y),
-                device_number(x, core, z, there) if core else device_number(x, core, there, y),
+                device_number(x, core, there, y) if core else device_number(x, core, z, there),
             )
         )
     return lax.ppermute(block, BOTH, route)
@@ -81,6 +81,14 @@
     return pl.BlockSpec(memory_space=pltpu.SMEM)
 
 
+def anywhere():
+    return pl.BlockSpec(memory_space=pl.ANY)
+
+
+def landing(count):
+    return [pltpu.VMEM((count, BLOCK, BLOCK), BF16), pltpu.SemaphoreType.DMA((count,))]
+
+
 def params(mib):
     return pltpu.CompilerParams(vmem_limit_bytes=mib * 1024 * 1024)
 
@@ -100,26 +108,32 @@
             )
 
 
-def project(place, weight, blocks, total):
+def project(place, weight, offsets, blocks, near, done, total):
     r = place[1]
     sign = 1 - 2 * lax.rem(r, 2)
-    for offset, block in blocks:
+    copies = [
+        pltpu.make_async_copy(block, near.at[i], done.at[i]) for i, block in enumerate(blocks)
+    ]
+    for copy in copies:
+        copy.start()
+    for i, offset in enumerate(offsets):
+        copies[i].wait()
         part = jnp.dot(
             weight[lax.rem(r + sign * offset + RING, RING)],
-            block[...],
+            near[i],
             preferred_element_type=F32,
         )
         total = part if total is None else total + part
     return total
 
 
-def first_kernel(place, weight, own, one_a, one_b, two_a, two_b, out):
-    blocks = ((0, own), (1, one_a), (-1, one_b), (-2, two_a), (2, two_b))
-    out[...] = project(place, weight, blocks, None)
-
-
-def second_kernel(place, weight, before, four, three_a, three_b, lags, out):
-    total = project(place, weight, ((4, four), (3, three_a), (-3, three_b)), before[...])
+def first_kernel(place, weight, own, one_a, one_b, two_a, two_b, four, out, near, done):
+    blocks = (own, one_a, one_b, two_a, two_b, four)
+    out[...] = project(place, weight, (0, 1, -1, -2, 2, 4), blocks, near, done, None)
+
+
+def second_kernel(place, weight, before, three_a, three_b, lags, out, near, done):
+    total = project(place, weight, (3, -3), (three_a, three_b), near, done, before[...])
     lag_rows = lags[...].astype(F32)
     pieces = []
     for d in range(RING):
@@ -201,10 +215,10 @@
 
 def on_device(activations, in_weight, short_taps, long_filter, skip_gain):
     position = lax.axis_index("seq")
-    core = position % 2
+    mixed_blocks = 1 - position % 2
     chan = lax.axis_index("chan")
-    ring_place = jnp.where(core == 0, chan // RING, chan % RING)
-    place = jnp.stack([core, ring_place]).astype(jnp.int32)
+    ring_place = jnp.where(mixed_blocks == 0, chan // RING, chan % RING)
+    place = jnp.stack([mixed_blocks, ring_place]).astype(jnp.int32)
 
     shard = activations.T
     own = lax.all_to_all(
@@ -220,6 +234,10 @@
     four = shift(two_a, 2, -2)
     three_a, three_b = shift(two_a, 1, -1), shift(two_b, -1, 1)
 
+    taps = jnp.concatenate([short_taps.reshape(9, 64), skip_gain[None]], axis=0)
+    taps = lax.dynamic_slice_in_dim(taps, position * 8, 8, axis=1).T
+    place, taps = lax.optimization_barrier((place, taps))
+
     weight = pl.pallas_call(
         weight_kernel,
         out_shape=jax.ShapeDtypeStruct((RING, 192, BLOCK), BF16),
@@ -231,27 +249,27 @@
     before = pl.pallas_call(
         first_kernel,
         out_shape=jax.ShapeDtypeStruct((192, BLOCK), F32),
-        in_specs=[smem()] + [vmem()] * 6,
-        out_specs=vmem(),
+        in_specs=[smem(), vmem()] + [anywhere()] * 6,
+        out_specs=vmem(),
+        scratch_shapes=landing(6),
         compiler_params=params(12),
         cost_estimate=pl.CostEstimate(
-            flops=2 * 5 * 192 * BLOCK * BLOCK, bytes_accessed=4 << 20, transcendentals=0
+            flops=2 * 6 * 192 * BLOCK * BLOCK, bytes_accessed=5 << 20, transcendentals=0
         ),
-    )(place, weight, own, one_a, one_b, two_a, two_b)
+    )(place, weight, own, one_a, one_b, two_a, two_b, four)
     messages = pl.pallas_call(
         second_kernel,
         out_shape=jax.ShapeDtypeStruct((RING * 32, BLOCK), BF16),
-        in_specs=[smem()] + [vmem()] * 6,
-        out_specs=vmem(),
+        in_specs=[smem(), vmem(), vmem()] + [anywhere()] * 2 + [vmem()],
+        out_specs=vmem(),
+        scratch_shapes=landing(2),
         compiler_params=params(12),
         cost_estimate=pl.CostEstimate(
-            flops=2 * 3 * 192 * BLOCK * BLOCK, bytes_accessed=4 << 20, transcendentals=0
+            flops=2 * 2 * 192 * BLOCK * BLOCK, bytes_accessed=3 << 20, transcendentals=0
         ),
-    )(place, weight, before, four, three_a, three_b, long_filter)
+    )(place, weight, before, three_a, three_b, long_filter)
 
     rows = lax.all_to_all(messages.reshape(RING, 32, BLOCK), "seq", 0, 0, tiled=True)
-    taps = jnp.concatenate([short_taps.reshape(9, 64), skip_gain[None]], axis=0)
-    taps = lax.dynamic_slice_in_dim(taps, position * 8, 8, axis=1).T
     forward, inverse = tables()
     mixed = pl.pallas_call(
         conv_kernel,

time: 91.9 us -> 88 us (0.958)
  blocking collectives: 31.1 us -> 40.8 us
  waiting for transfers between devices: 12.5 us -> 6.01 us
  starting transfers between devices: 39.5 us -> 33.5 us
  Pallas kernels: 6.21 us -> 5.19 us
    all_to_all x0 -> x1, blocking collectives: none -> 12.9 us  [on_device(): lax.all_to_all(messages.reshape(RING, 32, BLOCK), 'seq', 0, 0, tiled=True)]
    all_to_all x1 -> x0, starting transfers between devices: 11.7 us -> none  [on_device(): lax.all_to_all(messages.reshape(RING, 32, BLOCK), 'seq', 0, 0, tiled=True)]
    all_to_all x1 -> x0, waiting for transfers between devices: 6.32 us -> none  [on_device(): lax.all_to_all(messages.reshape(RING, 32, BLOCK), 'seq', 0, 0, tiled=True)]
    ppermute x7, starting transfers between devices: 27.8 us -> 33.5 us  [shift(): return lax.ppermute(block, BOTH, route)]
    all_to_all x1, blocking collectives: 22.8 us -> 19.6 us  [on_device(): lax.all_to_all(jnp.broadcast_to(shard[None], (RING,) + shard.shape), BOTH...]
    pallas_call x1, Pallas kernels: 2.56 us -> 1.07 us  [on_device(): pl.pallas_call(second_kernel, out_shape=jax.ShapeDtypeStruct((RING * 32,...]
  transfers between devices with their start and end apart: 8 -> 7, of which waited for: 4 -> 3; matrix products, arithmetic and copies ran while one was open for 0% -> 0% of each run, Pallas kernels for 3% -> 4%
where the time goes in v5:
time: 88 us; the launch traced here: 87.6 us
  blocking collectives  40.8 us (46%)
  starting transfers between devices  33.5 us (38%)
  waiting for transfers between devices  6.01 us (7%)
  Pallas kernels  5.19 us (6%)
  local copies, waits for them, and re-layouts  1.75 us (2%)
    ppermute x7, starting transfers between devices, shift(): return lax.ppermute(block, BOTH, route)  33.5 us
    all_to_all x1, blocking collectives, on_device(): lax.all_to_all(jnp.broadcast_to(shard[None], (RING,) + shard.shape), BOTH...  19.6 us
    all_to_all x1, blocking collectives, on_device(): lax.all_to_all(messages.reshape(RING, 32, BLOCK), 'seq', 0, 0, tiled=True)  12.9 us
    all_to_all x1, blocking collectives, on_device(): lax.all_to_all(mixed.reshape(RING, 8, BLOCK), 'seq', 0, 0, tiled=True)  8.26 us
    ppermute x7, waiting for transfers between devices, shift(): return lax.ppermute(block, BOTH, route)  6.01 us
    pallas_call x1, Pallas kernels, on_device(): pl.pallas_call(first_kernel, out_shape=jax.ShapeDtypeStruct((192, BLOCK),...  2.67 us
  transfers between devices with their start and end apart: 7, of which 3 were waited for; matrix products, arithmetic and copies ran while one was open for 0% of the time, Pallas kernels for 4%

profile of v5, /device:TPU:1, one launch (start us, length us, event | category | flops | bytes accessed | tf_op | source)
XLA Modules:
  0.0 87.6 jit_solution(6493055488133374742)
XLA Ops:
  0.0 0.0 copy-start.4
  0.0 0.0 copy-start.5
  0.0 0.0 copy-start
  0.0 1.0 %broadcast_in_dim.10 = bf16[8,64,512]{2,1,0:T(8,128)(2,1)S(1)} broadcast(bf16[64,512]{1,0:T(8,128)(2,1)} %bitcast.24), dimensions={1,2} | broadcast | bytes 589824 | tf_op jit(solution)/shard_map/broadcast_in_dim | solution.py:225
  1.0 19.6 %all_to_all.15 = bf16[8,64,512]{2,1,0:T(8,128)(2,1)S(1)} all-to-all(bf16[8,64,512]{2,1,0:T(8,128)(2,1)S(1)} %broadcast_in_dim.10), channel_id=1, replica_groups={{0,8,16,24,32,40,48,56},{1,9,17,25,33,41,49,57},{2,10,18,26,34,42,50,58..., dimensions={0} | all-to-all | bytes 1048576 | tf_op jit(solution)/shard_map/all_to_all | solution.py:224
  20.6 5.8 %collective-permute-start.2 = (bf16[512,512]{1,0:T(8,128)(2,1)S(1)}, bf16[512,512]{1,0:T(8,128)(2,1)}, u32[]{:S(2)}, u32[]{:S(2)}) collective-permute-start(bf16[512,512]{1,0:T(8,128)(2,1)S(1)} %bitcast.13), channel_id=1, source_target_pairs={{0,2},{1,7},{2,4},{3,1},{4,6},{5,3},{6,0},{7,5},{8,10},{9,15},{10,... | collective-permute-start | bytes 1572872 | tf_op jit(solution)/shard_map/ppermute | solution.py:55
  26.4 6.8 %collective-permute-start.3 = (bf16[512,512]{1,0:T(8,128)(2,1)S(1)}, bf16[512,512]{1,0:T(8,128)(2,1)}, u32[]{:S(2)}, u32[]{:S(2)}) collective-permute-start(bf16[512,512]{1,0:T(8,128)(2,1)S(1)} %bitcast.14), channel_id=1, source_target_pairs={{0,6},{1,3},{2,0},{3,5},{4,2},{5,7},{6,4},{7,1},{8,14},{9,11},{10,... | collective-permute-start | bytes 1572872 | tf_op jit(solution)/shard_map/ppermute | solution.py:55
  33.2 3.1 %collective-permute-start = (bf16[512,512]{1,0:T(8,128)(2,1)S(1)}, bf16[512,512]{1,0:T(8,128)(2,1)}, u32[]{:S(2)}, u32[]{:S(2)}) collective-permute-start(bf16[512,512]{1,0:T(8,128)(2,1)S(1)} %bitcast.15), channel_id=1, source_target_pairs={{0,1},{1,0},{2,3},{3,2},{4,5},{5,4},{6,7},{7,6},{8,9},{9,8},{10,11... | collective-permute-start | bytes 1572872 | tf_op jit(solution)/shard_map/ppermute | solution.py:55
  36.3 4.3 %collective-permute-start.1 = (bf16[512,512]{1,0:T(8,128)(2,1)S(1)}, bf16[512,512]{1,0:T(8,128)(2,1)}, u32[]{:S(2)}, u32[]{:S(2)}) collective-permute-start(bf16[512,512]{1,0:T(8,128)(2,1)S(1)} %bitcast.16), channel_id=1, source_target_pairs={{0,7},{1,2},{2,1},{3,4},{4,3},{5,6},{6,5},{7,0},{8,15},{9,10},{10,... | collective-permute-start | bytes 1572872 | tf_op jit(solution)/shard_map/ppermute | solution.py:55
  40.6 0.0 collective-permute-done.2.two_a
  40.6 4.6 %collective-permute-start.4 = (bf16[512,512]{1,0:T(8,128)(2,1)}, bf16[512,512]{1,0:T(8,128)(2,1)}, u32[]{:S(2)}, u32[]{:S(2)}) collective-permute-start(bf16[512,512]{1,0:T(8,128)(2,1)} %collective-permute-done.2.two_a), channel_id=1, source_target_pairs={{0,2},{1,7},{2,4},{3,1},{4,6},{5,3},{6,0},{7,5},{8,10},{9,15},{10,... | collective-permute-start | bytes 1572872 | tf_op jit(solution)/shard_map/ppermute | solution.py:55
  45.2 7.0 %collective-permute-start.5 = (bf16[512,512]{1,0:T(8,128)(2,1)}, bf16[512,512]{1,0:T(8,128)(2,1)S(1)}, u32[]{:S(2)}, u32[]{:S(2)}) collective-permute-start(bf16[512,512]{1,0:T(8,128)(2,1)} %collective-permute-done.2.two_a), channel_id=1, source_target_pairs={{0,1},{1,0},{2,3},{3,2},{4,5},{5,4},{6,7},{7,6},{8,9},{9,8},{10,11... | collective-permute-start | bytes 1572872 | tf_op jit(solution)/shard_map/ppermute | solution.py:55
  52.2 0.0 collective-permute-done.3.two_b
  52.2 1.9 %collective-permute-start.6 = (bf16[512,512]{1,0:T(8,128)(2,1)}, bf16[512,512]{1,0:T(8,128)(2,1)S(1)}, u32[]{:S(2)}, u32[]{:S(2)}) collective-permute-start(bf16[512,512]{1,0:T(8,128)(2,1)} %collective-permute-done.3.two_b), channel_id=1, source_target_pairs={{0,7},{1,2},{2,1},{3,4},{4,3},{5,6},{6,5},{7,0},{8,15},{9,10},{10,... | collective-permute-start | bytes 1572872 | tf_op jit(solution)/shard_map/ppermute | solution.py:55
  54.2 0.0 copy-done.4
  54.2 0.0 copy-done.5
  54.2 0.1 dynamic-slice_maximum_fusion
  54.3 0.1 copy.13
  54.4 0.1 pad_add_fusion.place
  54.5 0.0 copy-done
  54.5 0.7 shard_map.73.weight
  55.1 0.0 copy-start.3
  55.1 0.0 collective-permute-done.one_a
  55.2 0.0 collective-permute-done.1.one_b
  55.2 1.5 %collective-permute-done.4.four = bf16[512,512]{1,0:T(8,128)(2,1)} collective-permute-done((bf16[512,512]{1,0:T(8,128)(2,1)}, bf16[512,512]{1,0:T(8,128)(2,1)}, u32[]{:S(2)}, u32[]{:S(2)}) %collective-permute-start.4) | collective-permute-done | bytes 524320 | tf_op jit(solution)/shard_map/ppermute | solution.py:55
  56.6 2.7 %shard_map.74.before = f32[192,512]{1,0:T(8,128)S(1)} custom-call(s32[2]{0:T(128)S(1)} %pad_add_fusion.place, bf16[8,192,512]{2,1,0:T(8,128)(2,1)S(1)} %shard_map.73.weight, bf16[512,512]{1,0:T(8,128)(2,1)S(1)} %bitcast.17, bf16[512,512]{1,0:T(8,128)(2,1)} %collective-permute-done.one_a, bf16[512,512]{1,0:T(8,128)(2,1)} %collective-permute-done.1.one_b, ...), custom_call_target="tpu_custom_call" | custom-call | flops 603979776 | bytes 5242880 | tf_op jit(solution)/shard_map/pallas_call | solution.py:249
  59.3 0.0 copy-start.1
  59.3 0.0 copy-start.2
  59.3 3.6 %collective-permute-done.5.three_a = bf16[512,512]{1,0:T(8,128)(2,1)S(1)} collective-permute-done((bf16[512,512]{1,0:T(8,128)(2,1)}, bf16[512,512]{1,0:T(8,128)(2,1)S(1)}, u32[]{:S(2)}, u32[]{:S(2)}) %collective-permute-start.5) | collective-permute-done | bytes 524320 | tf_op jit(solution)/shard_map/ppermute | solution.py:55
  63.0 0.9 %collective-permute-done.6.three_b = bf16[512,512]{1,0:T(8,128)(2,1)S(1)} collective-permute-done((bf16[512,512]{1,0:T(8,128)(2,1)}, bf16[512,512]{1,0:T(8,128)(2,1)S(1)}, u32[]{:S(2)}, u32[]{:S(2)}) %collective-permute-start.6) | collective-permute-done | bytes 524320 | tf_op jit(solution)/shard_map/ppermute | solution.py:55
  63.9 0.0 copy-done.3
  63.9 1.1 %shard_map.75 = bf16[256,512]{1,0:T(8,128)(2,1)S(1)} custom-call(s32[2]{0:T(128)S(1)} %pad_add_fusion.place, bf16[8,192,512]{2,1,0:T(8,128)(2,1)S(1)} %shard_map.73.weight, f32[192,512]{1,0:T(8,128)S(1)} %shard_map.74.before, bf16[512,512]{1,0:T(8,128)(2,1)S(1)} %collective-permute-done.5.three_a, bf16[512,512]{1,0:T(8,128)(2,1)S(1)} %collective-permute-done.6.three_b, ...), custom_call_target="tpu_custom_call" | custom-call | flops 201326592 | bytes 3145728 | tf_op jit(solution)/shard_map/pallas_call | solution.py:260
  65.0 12.9 %all_to_all.16 = bf16[8,32,512]{2,1,0:T(8,128)(2,1)S(1)} all-to-all(bf16[8,32,512]{2,1,0:T(8,128)(2,1)S(1)} %bitcast.20), channel_id=1, replica_groups=mesh['seq'=8,'chan'=64] {'seq'}, dimensions={0} | all-to-all | bytes 524288 | tf_op jit(solution)/shard_map/all_to_all | solution.py:272
  77.9 0.0 copy-done.1
  77.9 0.0 copy-done.2
  77.9 0.8 shard_map.76
  78.7 8.3 %all_to_all.17 = bf16[8,8,512]{2,1,0:T(8,128)(2,1)S(1)} all-to-all(bf16[8,8,512]{2,1,0:T(8,128)(2,1)S(1)} %bitcast.21), channel_id=1, replica_groups=mesh['seq'=8,'chan'=64] {'seq'}, dimensions={0} | all-to-all | bytes 131072 | tf_op jit(solution)/shard_map/all_to_all | solution.py:284
  86.9 0.6 copy.15
  (1 shorter events, 0.0 us)
Async XLA Ops:
  0.0 54.2 %copy-start.4 = (f32[3,3,64]{2,1,0:T(4,128)S(1)}, f32[3,3,64]{2,1,0:T(4,128)}, u32[]{:S(2)}) copy-start(f32[3,3,64]{2,1,0:T(4,128)} %param.9) | copy-start | bytes 6916
  0.0 54.2 %copy-start.5 = (f32[64]{0:T(128)S(1)}, f32[64]{0:T(128)}, u32[]{:S(2)}) copy-start(f32[64]{0:T(128)} %param.11) | copy-start | bytes 772
  0.0 54.5 %copy-start = (bf16[3,64,4096]{2,1,0:T(8,128)(2,1)S(1)}, bf16[3,64,4096]{2,1,0:T(8,128)(2,1)}, u32[]{:S(2)}) copy-start(bf16[3,64,4096]{2,1,0:T(8,128)(2,1)} %param.8) | copy-start | bytes 4718596
  20.6 20.0 %collective-permute-start.2 = (bf16[512,512]{1,0:T(8,128)(2,1)S(1)}, bf16[512,512]{1,0:T(8,128)(2,1)}, u32[]{:S(2)}, u32[]{:S(2)}) collective-permute-start(bf16[512,512]{1,0:T(8,128)(2,1)S(1)} %bitcast.13), channel_id=1, source_target_pairs={{0,2},{1,7},{2,4},{3,1},{4,6},{5,3},{6,0},{7,5},{8,10},{9,15},{10,... | collective-permute-start | bytes 1572872 | tf_op jit(solution)/shard_map/ppermute | solution.py:55
  26.4 25.8 %collective-permute-start.3 = (bf16[512,512]{1,0:T(8,128)(2,1)S(1)}, bf16[512,512]{1,0:T(8,128)(2,1)}, u32[]{:S(2)}, u32[]{:S(2)}) collective-permute-start(bf16[512,512]{1,0:T(8,128)(2,1)S(1)} %bitcast.14), channel_id=1, source_target_pairs={{0,6},{1,3},{2,0},{3,5},{4,2},{5,7},{6,4},{7,1},{8,14},{9,11},{10,... | collective-permute-start | bytes 1572872 | tf_op jit(solution)/shard_map/ppermute | solution.py:55
  33.2 22.0 %collective-permute-start = (bf16[512,512]{1,0:T(8,128)(2,1)S(1)}, bf16[512,512]{1,0:T(8,128)(2,1)}, u32[]{:S(2)}, u32[]{:S(2)}) collective-permute-start(bf16[512,512]{1,0:T(8,128)(2,1)S(1)} %bitcast.15), channel_id=1, source_target_pairs={{0,1},{1,0},{2,3},{3,2},{4,5},{5,4},{6,7},{7,6},{8,9},{9,8},{10,11... | collective-permute-start | bytes 1572872 | tf_op jit(solution)/shard_map/ppermute | solution.py:55
  36.3 18.9 %collective-permute-start.1 = (bf16[512,512]{1,0:T(8,128)(2,1)S(1)}, bf16[512,512]{1,0:T(8,128)(2,1)}, u32[]{:S(2)}, u32[]{:S(2)}) collective-permute-start(bf16[512,512]{1,0:T(8,128)(2,1)S(1)} %bitcast.16), channel_id=1, source_target_pairs={{0,7},{1,2},{2,1},{3,4},{4,3},{5,6},{6,5},{7,0},{8,15},{9,10},{10,... | collective-permute-start | bytes 1572872 | tf_op jit(solution)/shard_map/ppermute | solution.py:55
  40.6 16.0 %collective-permute-start.4 = (bf16[512,512]{1,0:T(8,128)(2,1)}, bf16[512,512]{1,0:T(8,128)(2,1)}, u32[]{:S(2)}, u32[]{:S(2)}) collective-permute-start(bf16[512,512]{1,0:T(8,128)(2,1)} %collective-permute-done.2.two_a), channel_id=1, source_target_pairs={{0,2},{1,7},{2,4},{3,1},{4,6},{5,3},{6,0},{7,5},{8,10},{9,15},{10,... | collective-permute-start | bytes 1572872 | tf_op jit(solution)/shard_map/ppermute | solution.py:55
  45.2 17.7 %collective-permute-start.5 = (bf16[512,512]{1,0:T(8,128)(2,1)}, bf16[512,512]{1,0:T(8,128)(2,1)S(1)}, u32[]{:S(2)}, u32[]{:S(2)}) collective-permute-start(bf16[512,512]{1,0:T(8,128)(2,1)} %collective-permute-done.2.two_a), channel_id=1, source_target_pairs={{0,1},{1,0},{2,3},{3,2},{4,5},{5,4},{6,7},{7,6},{8,9},{9,8},{10,11... | collective-permute-start | bytes 1572872 | tf_op jit(solution)/shard_map/ppermute | solution.py:55
  52.2 11.6 %collective-permute-start.6 = (bf16[512,512]{1,0:T(8,128)(2,1)}, bf16[512,512]{1,0:T(8,128)(2,1)S(1)}, u32[]{:S(2)}, u32[]{:S(2)}) collective-permute-start(bf16[512,512]{1,0:T(8,128)(2,1)} %collective-permute-done.3.two_b), channel_id=1, source_target_pairs={{0,7},{1,2},{2,1},{3,4},{4,3},{5,6},{6,5},{7,0},{8,15},{9,10},{10,... | collective-permute-start | bytes 1572872 | tf_op jit(solution)/shard_map/ppermute | solution.py:55
  55.1 8.7 %copy-start.3 = (bf16[64,512]{1,0:T(8,128)(2,1)S(1)}, bf16[64,512]{1,0:T(8,128)(2,1)}, u32[]{:S(2)}) copy-start(bf16[64,512]{1,0:T(8,128)(2,1)} %lags.1) | copy-start | bytes 196612
  59.3 18.6 %copy-start.1 = (bf16[512,1024]{1,0:T(8,128)(2,1)S(1)}, bf16[512,1024]{1,0:T(8,128)(2,1)}, u32[]{:S(2)}) copy-start(bf16[512,1024]{1,0:T(8,128)(2,1)} %constant.52.clone.forward) | copy-start | bytes 3145732
  59.3 18.6 %copy-start.2 = (bf16[1024,512]{1,0:T(8,128)(2,1)S(1)}, bf16[1024,512]{1,0:T(8,128)(2,1)}, u32[]{:S(2)}) copy-start(bf16[1024,512]{1,0:T(8,128)(2,1)} %constant.53.clone.inverse) | copy-start | bytes 3145732

commit v6 on v5

--- a/solution.py
+++ b/solution.py
@@ -45,7 +45,7 @@
     route = []
     for x, core, z, y in devices():
         here = z if core else y
-        there = here + (odd if here % 2 else even)
+        there = here + (odd if (here + 1 - core) % 2 else even)
         route.append(
             (
                 device_number(x, core, z, y),
@@ -110,7 +110,7 @@
 
 def project(place, weight, offsets, blocks, near, done, total):
     r = place[1]
-    sign = 1 - 2 * lax.rem(r, 2)
+    sign = 1 - 2 * lax.rem(r + place[0], 2)
     copies = [
         pltpu.make_async_copy(block, near.at[i], done.at[i]) for i, block in enumerate(blocks)
     ]

time: 88 us -> 86.1 us (0.978)
  blocking collectives: 40.8 us -> 39.2 us
    all_to_all x1, blocking collectives: 12.9 us -> 11.3 us  [on_device(): lax.all_to_all(messages.reshape(RING, 32, BLOCK), 'seq', 0, 0, tiled=True)]
where the time goes in v6:
time: 86.1 us; the launch traced here: 85.7 us
  blocking collectives  39.2 us (46%)
  starting transfers between devices  33.5 us (39%)
  waiting for transfers between devices  5.72 us (7%)
  Pallas kernels  5.19 us (6%)
  local copies, waits for them, and re-layouts  1.75 us (2%)
    ppermute x7, starting transfers between devices, shift(): return lax.ppermute(block, BOTH, route)  33.5 us
    all_to_all x1, blocking collectives, on_device(): lax.all_to_all(jnp.broadcast_to(shard[None], (RING,) + shard.shape), BOTH...  19.6 us
    all_to_all x1, blocking collectives, on_device(): lax.all_to_all(messages.reshape(RING, 32, BLOCK), 'seq', 0, 0, tiled=True)  11.3 us
    all_to_all x1, blocking collectives, on_device(): lax.all_to_all(mixed.reshape(RING, 8, BLOCK), 'seq', 0, 0, tiled=True)  8.26 us
    ppermute x7, waiting for transfers between devices, shift(): return lax.ppermute(block, BOTH, route)  5.72 us
    pallas_call x1, Pallas kernels, on_device(): pl.pallas_call(first_kernel, out_shape=jax.ShapeDtypeStruct((192, BLOCK),...  2.67 us
  transfers between devices with their start and end apart: 7, of which 3 were waited for; matrix products, arithmetic and copies ran while one was open for 0% of the time, Pallas kernels for 4%

profile of v6, /device:TPU:1, one launch (start us, length us, event | category | flops | bytes accessed | tf_op | source)
XLA Modules:
  0.0 85.7 jit_solution(18243298646953793709)
XLA Ops:
  0.0 0.0 copy-start.4
  0.0 0.0 copy-start.5
  0.0 0.0 copy-start
  0.0 1.0 %broadcast_in_dim.10 = bf16[8,64,512]{2,1,0:T(8,128)(2,1)S(1)} broadcast(bf16[64,512]{1,0:T(8,128)(2,1)} %bitcast.24), dimensions={1,2} | broadcast | bytes 589824 | tf_op jit(solution)/shard_map/broadcast_in_dim | solution.py:225
  1.0 19.6 %all_to_all.15 = bf16[8,64,512]{2,1,0:T(8,128)(2,1)S(1)} all-to-all(bf16[8,64,512]{2,1,0:T(8,128)(2,1)S(1)} %broadcast_in_dim.10), channel_id=1, replica_groups={{0,8,16,24,32,40,48,56},{1,9,17,25,33,41,49,57},{2,10,18,26,34,42,50,58..., dimensions={0} | all-to-all | bytes 1048576 | tf_op jit(solution)/shard_map/all_to_all | solution.py:224
  20.6 5.8 %collective-permute-start.2 = (bf16[512,512]{1,0:T(8,128)(2,1)S(1)}, bf16[512,512]{1,0:T(8,128)(2,1)}, u32[]{:S(2)}, u32[]{:S(2)}) collective-permute-start(bf16[512,512]{1,0:T(8,128)(2,1)S(1)} %bitcast.13), channel_id=1, source_target_pairs={{0,6},{1,3},{2,0},{3,5},{4,2},{5,7},{6,4},{7,1},{8,14},{9,11},{10,... | collective-permute-start | bytes 1572872 | tf_op jit(solution)/shard_map/ppermute | solution.py:55
  26.4 6.8 %collective-permute-start.3 = (bf16[512,512]{1,0:T(8,128)(2,1)S(1)}, bf16[512,512]{1,0:T(8,128)(2,1)}, u32[]{:S(2)}, u32[]{:S(2)}) collective-permute-start(bf16[512,512]{1,0:T(8,128)(2,1)S(1)} %bitcast.14), channel_id=1, source_target_pairs={{0,2},{1,7},{2,4},{3,1},{4,6},{5,3},{6,0},{7,5},{8,10},{9,15},{10,... | collective-permute-start | bytes 1572872 | tf_op jit(solution)/shard_map/ppermute | solution.py:55
  33.2 3.1 %collective-permute-start = (bf16[512,512]{1,0:T(8,128)(2,1)S(1)}, bf16[512,512]{1,0:T(8,128)(2,1)}, u32[]{:S(2)}, u32[]{:S(2)}) collective-permute-start(bf16[512,512]{1,0:T(8,128)(2,1)S(1)} %bitcast.15), channel_id=1, source_target_pairs={{0,7},{1,2},{2,1},{3,4},{4,3},{5,6},{6,5},{7,0},{8,15},{9,10},{10,... | collective-permute-start | bytes 1572872 | tf_op jit(solution)/shard_map/ppermute | solution.py:55
  36.3 4.3 %collective-permute-start.1 = (bf16[512,512]{1,0:T(8,128)(2,1)S(1)}, bf16[512,512]{1,0:T(8,128)(2,1)}, u32[]{:S(2)}, u32[]{:S(2)}) collective-permute-start(bf16[512,512]{1,0:T(8,128)(2,1)S(1)} %bitcast.16), channel_id=1, source_target_pairs={{0,1},{1,0},{2,3},{3,2},{4,5},{5,4},{6,7},{7,6},{8,9},{9,8},{10,11... | collective-permute-start | bytes 1572872 | tf_op jit(solution)/shard_map/ppermute | solution.py:55
  40.6 0.0 collective-permute-done.2.two_a
  40.6 4.6 %collective-permute-start.4 = (bf16[512,512]{1,0:T(8,128)(2,1)}, bf16[512,512]{1,0:T(8,128)(2,1)}, u32[]{:S(2)}, u32[]{:S(2)}) collective-permute-start(bf16[512,512]{1,0:T(8,128)(2,1)} %collective-permute-done.2.two_a), channel_id=1, source_target_pairs={{0,6},{1,3},{2,0},{3,5},{4,2},{5,7},{6,4},{7,1},{8,14},{9,11},{10,... | collective-permute-start | bytes 1572872 | tf_op jit(solution)/shard_map/ppermute | solution.py:55
  45.2 7.0 %collective-permute-start.5 = (bf16[512,512]{1,0:T(8,128)(2,1)}, bf16[512,512]{1,0:T(8,128)(2,1)S(1)}, u32[]{:S(2)}, u32[]{:S(2)}) collective-permute-start(bf16[512,512]{1,0:T(8,128)(2,1)} %collective-permute-done.2.two_a), channel_id=1, source_target_pairs={{0,7},{1,2},{2,1},{3,4},{4,3},{5,6},{6,5},{7,0},{8,15},{9,10},{10,... | collective-permute-start | bytes 1572872 | tf_op jit(solution)/shard_map/ppermute | solution.py:55
  52.2 0.0 collective-permute-done.3.two_b
  52.2 1.9 %collective-permute-start.6 = (bf16[512,512]{1,0:T(8,128)(2,1)}, bf16[512,512]{1,0:T(8,128)(2,1)S(1)}, u32[]{:S(2)}, u32[]{:S(2)}) collective-permute-start(bf16[512,512]{1,0:T(8,128)(2,1)} %collective-permute-done.3.two_b), channel_id=1, source_target_pairs={{0,1},{1,0},{2,3},{3,2},{4,5},{5,4},{6,7},{7,6},{8,9},{9,8},{10,11... | collective-permute-start | bytes 1572872 | tf_op jit(solution)/shard_map/ppermute | solution.py:55
  54.2 0.0 copy-done.4
  54.2 0.0 copy-done.5
  54.2 0.1 dynamic-slice_maximum_fusion
  54.3 0.1 copy.13
  54.4 0.1 pad_add_fusion.place
  54.5 0.0 copy-done
  54.5 0.7 shard_map.73.weight
  55.1 0.0 copy-start.3
  55.1 0.0 collective-permute-done.one_a
  55.2 0.0 collective-permute-done.1.one_b
  55.2 1.2 %collective-permute-done.4.four = bf16[512,512]{1,0:T(8,128)(2,1)} collective-permute-done((bf16[512,512]{1,0:T(8,128)(2,1)}, bf16[512,512]{1,0:T(8,128)(2,1)}, u32[]{:S(2)}, u32[]{:S(2)}) %collective-permute-start.4) | collective-permute-done | bytes 524320 | tf_op jit(solution)/shard_map/ppermute | solution.py:55
  56.3 2.7 %shard_map.74.before = f32[192,512]{1,0:T(8,128)S(1)} custom-call(s32[2]{0:T(128)S(1)} %pad_add_fusion.place, bf16[8,192,512]{2,1,0:T(8,128)(2,1)S(1)} %shard_map.73.weight, bf16[512,512]{1,0:T(8,128)(2,1)S(1)} %bitcast.17, bf16[512,512]{1,0:T(8,128)(2,1)} %collective-permute-done.one_a, bf16[512,512]{1,0:T(8,128)(2,1)} %collective-permute-done.1.one_b, ...), custom_call_target="tpu_custom_call" | custom-call | flops 603979776 | bytes 5242880 | tf_op jit(solution)/shard_map/pallas_call | solution.py:249
  59.0 0.0 copy-start.1
  59.0 0.0 copy-start.2
  59.0 3.9 %collective-permute-done.5.three_a = bf16[512,512]{1,0:T(8,128)(2,1)S(1)} collective-permute-done((bf16[512,512]{1,0:T(8,128)(2,1)}, bf16[512,512]{1,0:T(8,128)(2,1)S(1)}, u32[]{:S(2)}, u32[]{:S(2)}) %collective-permute-start.5) | collective-permute-done | bytes 524320 | tf_op jit(solution)/shard_map/ppermute | solution.py:55
  63.0 0.6 collective-permute-done.6.three_b
  63.6 0.0 copy-done.3
  63.6 1.1 %shard_map.75 = bf16[256,512]{1,0:T(8,128)(2,1)S(1)} custom-call(s32[2]{0:T(128)S(1)} %pad_add_fusion.place, bf16[8,192,512]{2,1,0:T(8,128)(2,1)S(1)} %shard_map.73.weight, f32[192,512]{1,0:T(8,128)S(1)} %shard_map.74.before, bf16[512,512]{1,0:T(8,128)(2,1)S(1)} %collective-permute-done.5.three_a, bf16[512,512]{1,0:T(8,128)(2,1)S(1)} %collective-permute-done.6.three_b, ...), custom_call_target="tpu_custom_call" | custom-call | flops 201326592 | bytes 3145728 | tf_op jit(solution)/shard_map/pallas_call | solution.py:260
  64.7 11.3 %all_to_all.16 = bf16[8,32,512]{2,1,0:T(8,128)(2,1)S(1)} all-to-all(bf16[8,32,512]{2,1,0:T(8,128)(2,1)S(1)} %bitcast.20), channel_id=1, replica_groups=mesh['seq'=8,'chan'=64] {'seq'}, dimensions={0} | all-to-all | bytes 524288 | tf_op jit(solution)/shard_map/all_to_all | solution.py:272
  76.0 0.0 copy-done.1
  76.0 0.0 copy-done.2
  76.0 0.8 shard_map.76
  76.8 8.3 %all_to_all.17 = bf16[8,8,512]{2,1,0:T(8,128)(2,1)S(1)} all-to-all(bf16[8,8,512]{2,1,0:T(8,128)(2,1)S(1)} %bitcast.21), channel_id=1, replica_groups=mesh['seq'=8,'chan'=64] {'seq'}, dimensions={0} | all-to-all | bytes 131072 | tf_op jit(solution)/shard_map/all_to_all | solution.py:284
  85.0 0.6 copy.15
  (1 shorter events, 0.0 us)
Async XLA Ops:
  0.0 54.2 %copy-start.4 = (f32[3,3,64]{2,1,0:T(4,128)S(1)}, f32[3,3,64]{2,1,0:T(4,128)}, u32[]{:S(2)}) copy-start(f32[3,3,64]{2,1,0:T(4,128)} %param.9) | copy-start | bytes 6916
  0.0 54.2 %copy-start.5 = (f32[64]{0:T(128)S(1)}, f32[64]{0:T(128)}, u32[]{:S(2)}) copy-start(f32[64]{0:T(128)} %param.11) | copy-start | bytes 772
  0.0 54.5 %copy-start = (bf16[3,64,4096]{2,1,0:T(8,128)(2,1)S(1)}, bf16[3,64,4096]{2,1,0:T(8,128)(2,1)}, u32[]{:S(2)}) copy-start(bf16[3,64,4096]{2,1,0:T(8,128)(2,1)} %param.8) | copy-start | bytes 4718596
  20.6 20.0 %collective-permute-start.2 = (bf16[512,512]{1,0:T(8,128)(2,1)S(1)}, bf16[512,512]{1,0:T(8,128)(2,1)}, u32[]{:S(2)}, u32[]{:S(2)}) collective-permute-start(bf16[512,512]{1,0:T(8,128)(2,1)S(1)} %bitcast.13), channel_id=1, source_target_pairs={{0,6},{1,3},{2,0},{3,5},{4,2},{5,7},{6,4},{7,1},{8,14},{9,11},{10,... | collective-permute-start | bytes 1572872 | tf_op jit(solution)/shard_map/ppermute | solution.py:55
  26.4 25.8 %collective-permute-start.3 = (bf16[512,512]{1,0:T(8,128)(2,1)S(1)}, bf16[512,512]{1,0:T(8,128)(2,1)}, u32[]{:S(2)}, u32[]{:S(2)}) collective-permute-start(bf16[512,512]{1,0:T(8,128)(2,1)S(1)} %bitcast.14), channel_id=1, source_target_pairs={{0,2},{1,7},{2,4},{3,1},{4,6},{5,3},{6,0},{7,5},{8,10},{9,15},{10,... | collective-permute-start | bytes 1572872 | tf_op jit(solution)/shard_map/ppermute | solution.py:55
  33.2 22.0 %collective-permute-start = (bf16[512,512]{1,0:T(8,128)(2,1)S(1)}, bf16[512,512]{1,0:T(8,128)(2,1)}, u32[]{:S(2)}, u32[]{:S(2)}) collective-permute-start(bf16[512,512]{1,0:T(8,128)(2,1)S(1)} %bitcast.15), channel_id=1, source_target_pairs={{0,7},{1,2},{2,1},{3,4},{4,3},{5,6},{6,5},{7,0},{8,15},{9,10},{10,... | collective-permute-start | bytes 1572872 | tf_op jit(solution)/shard_map/ppermute | solution.py:55
  36.3 18.9 %collective-permute-start.1 = (bf16[512,512]{1,0:T(8,128)(2,1)S(1)}, bf16[512,512]{1,0:T(8,128)(2,1)}, u32[]{:S(2)}, u32[]{:S(2)}) collective-permute-start(bf16[512,512]{1,0:T(8,128)(2,1)S(1)} %bitcast.16), channel_id=1, source_target_pairs={{0,1},{1,0},{2,3},{3,2},{4,5},{5,4},{6,7},{7,6},{8,9},{9,8},{10,11... | collective-permute-start | bytes 1572872 | tf_op jit(solution)/shard_map/ppermute | solution.py:55
  40.6 15.7 %collective-permute-start.4 = (bf16[512,512]{1,0:T(8,128)(2,1)}, bf16[512,512]{1,0:T(8,128)(2,1)}, u32[]{:S(2)}, u32[]{:S(2)}) collective-permute-start(bf16[512,512]{1,0:T(8,128)(2,1)} %collective-permute-done.2.two_a), channel_id=1, source_target_pairs={{0,6},{1,3},{2,0},{3,5},{4,2},{5,7},{6,4},{7,1},{8,14},{9,11},{10,... | collective-permute-start | bytes 1572872 | tf_op jit(solution)/shard_map/ppermute | solution.py:55
  45.2 17.7 %collective-permute-start.5 = (bf16[512,512]{1,0:T(8,128)(2,1)}, bf16[512,512]{1,0:T(8,128)(2,1)S(1)}, u32[]{:S(2)}, u32[]{:S(2)}) collective-permute-start(bf16[512,512]{1,0:T(8,128)(2,1)} %collective-permute-done.2.two_a), channel_id=1, source_target_pairs={{0,7},{1,2},{2,1},{3,4},{4,3},{5,6},{6,5},{7,0},{8,15},{9,10},{10,... | collective-permute-start | bytes 1572872 | tf_op jit(solution)/shard_map/ppermute | solution.py:55
  52.2 11.3 %collective-permute-start.6 = (bf16[512,512]{1,0:T(8,128)(2,1)}, bf16[512,512]{1,0:T(8,128)(2,1)S(1)}, u32[]{:S(2)}, u32[]{:S(2)}) collective-permute-start(bf16[512,512]{1,0:T(8,128)(2,1)} %collective-permute-done.3.two_b), channel_id=1, source_target_pairs={{0,1},{1,0},{2,3},{3,2},{4,5},{5,4},{6,7},{7,6},{8,9},{9,8},{10,11... | collective-permute-start | bytes 1572872 | tf_op jit(solution)/shard_map/ppermute | solution.py:55
  55.1 8.4 %copy-start.3 = (bf16[64,512]{1,0:T(8,128)(2,1)S(1)}, bf16[64,512]{1,0:T(8,128)(2,1)}, u32[]{:S(2)}) copy-start(bf16[64,512]{1,0:T(8,128)(2,1)} %lags.1) | copy-start | bytes 196612
  59.0 17.0 %copy-start.1 = (bf16[512,1024]{1,0:T(8,128)(2,1)S(1)}, bf16[512,1024]{1,0:T(8,128)(2,1)}, u32[]{:S(2)}) copy-start(bf16[512,1024]{1,0:T(8,128)(2,1)} %constant.52.clone.forward) | copy-start | bytes 3145732
  59.0 17.0 %copy-start.2 = (bf16[1024,512]{1,0:T(8,128)(2,1)S(1)}, bf16[1024,512]{1,0:T(8,128)(2,1)}, u32[]{:S(2)}) copy-start(bf16[1024,512]{1,0:T(8,128)(2,1)} %constant.53.clone.inverse) | copy-start | bytes 3145732

commit v7 on v6

--- a/solution.py
+++ b/solution.py
@@ -229,11 +229,6 @@
         tiled=True,
         axis_index_groups=rings(),
     ).reshape(BLOCK, BLOCK)
-    two_a, two_b = shift(own, 2, -2), shift(own, -2, 2)
-    one_a, one_b = shift(own, 1, -1), shift(own, -1, 1)
-    four = shift(two_a, 2, -2)
-    three_a, three_b = shift(two_a, 1, -1), shift(two_b, -1, 1)
-
     taps = jnp.concatenate([short_taps.reshape(9, 64), skip_gain[None]], axis=0)
     taps = lax.dynamic_slice_in_dim(taps, position * 8, 8, axis=1).T
     place, taps = lax.optimization_barrier((place, taps))
@@ -246,6 +241,12 @@
         compiler_params=params(12),
         cost_estimate=pl.CostEstimate(flops=0, bytes_accessed=3 << 20, transcendentals=0),
     )(place, in_weight.reshape(192, RING * BLOCK))
+    two_a, two_b = shift(own, 2, -2), shift(own, -2, 2)
+    later, weight = lax.optimization_barrier((own, weight))
+    one_a, one_b = shift(later, 1, -1), shift(later, -1, 1)
+    four = shift(two_a, 2, -2)
+    three_a, three_b = shift(two_a, 1, -1), shift(two_b, -1, 1)
+
     before = pl.pallas_call(
         first_kernel,
         out_shape=jax.ShapeDtypeStruct((192, BLOCK), F32),

time: 86.1 us -> 85.7 us (level)
  waiting for transfers between devices: 5.72 us -> 7.3 us
  starting transfers between devices: 33.5 us -> 32.4 us
    ppermute x7, waiting for transfers between devices: 5.72 us -> 7.3 us  [shift(): return lax.ppermute(block, BOTH, route)]
    ppermute x7, starting transfers between devices: 33.5 us -> 32.4 us  [shift(): return lax.ppermute(block, BOTH, route)]
  transfers between devices with their start and end apart: 7 -> 7, of which waited for: 3 -> 3; matrix products, arithmetic and copies ran while one was open for 0% -> 0% of each run, Pallas kernels for 4% -> 3%
where the time goes in v7:
time: 85.7 us; the launch traced here: 85.3 us
  blocking collectives  39.1 us (46%)
  starting transfers between devices  32.4 us (38%)
  waiting for transfers between devices  7.3 us (9%)
  Pallas kernels  4.37 us (5%)
  local copies, waits for them, and re-layouts  1.75 us (2%)
    ppermute x7, starting transfers between devices, shift(): return lax.ppermute(block, BOTH, route)  32.4 us
    all_to_all x1, blocking collectives, on_device(): lax.all_to_all(jnp.broadcast_to(shard[None], (RING,) + shard.shape), BOTH...  19.6 us
    all_to_all x1, blocking collectives, on_device(): lax.all_to_all(messages.reshape(RING, 32, BLOCK), 'seq', 0, 0, tiled=True)  11.3 us
    all_to_all x1, blocking collectives, on_device(): lax.all_to_all(mixed.reshape(RING, 8, BLOCK), 'seq', 0, 0, tiled=True)  8.25 us
    ppermute x7, waiting for transfers between devices, shift(): return lax.ppermute(block, BOTH, route)  7.3 us
    pallas_call x1, Pallas kernels, on_device(): pl.pallas_call(first_kernel, out_shape=jax.ShapeDtypeStruct((192, BLOCK),...  1.86 us
  transfers between devices with their start and end apart: 7, of which 3 were waited for; matrix products, arithmetic and copies ran while one was open for 0% of the time, Pallas kernels for 3%

profile of v7, /device:TPU:1, one launch (start us, length us, event | category | flops | bytes accessed | tf_op | source)
XLA Modules:
  0.0 85.3 jit_solution(1799885192758405809)
XLA Ops:
  0.0 0.0 copy-start.4
  0.0 0.0 copy-start.5
  0.0 0.0 copy-start
  0.0 1.0 %broadcast_in_dim.10 = bf16[8,64,512]{2,1,0:T(8,128)(2,1)S(1)} broadcast(bf16[64,512]{1,0:T(8,128)(2,1)} %bitcast.24), dimensions={1,2} | broadcast | bytes 589824 | tf_op jit(solution)/shard_map/broadcast_in_dim | solution.py:225
  1.0 19.6 %all_to_all.15 = bf16[8,64,512]{2,1,0:T(8,128)(2,1)S(1)} all-to-all(bf16[8,64,512]{2,1,0:T(8,128)(2,1)S(1)} %broadcast_in_dim.10), channel_id=1, replica_groups={{0,8,16,24,32,40,48,56},{1,9,17,25,33,41,49,57},{2,10,18,26,34,42,50,58..., dimensions={0} | all-to-all | bytes 1048576 | tf_op jit(solution)/shard_map/all_to_all | solution.py:224
  20.6 5.8 %collective-permute-start.2 = (bf16[512,512]{1,0:T(8,128)(2,1)S(1)}, bf16[512,512]{1,0:T(8,128)(2,1)S(1)}, u32[]{:S(2)}, u32[]{:S(2)}) collective-permute-start(bf16[512,512]{1,0:T(8,128)(2,1)S(1)} %bitcast.13), channel_id=1, source_target_pairs={{0,6},{1,3},{2,0},{3,5},{4,2},{5,7},{6,4},{7,1},{8,14},{9,11},{10,... | collective-permute-start | bytes 1572872 | tf_op jit(solution)/shard_map/ppermute | solution.py:55
  26.4 6.8 %collective-permute-start.3 = (bf16[512,512]{1,0:T(8,128)(2,1)S(1)}, bf16[512,512]{1,0:T(8,128)(2,1)S(1)}, u32[]{:S(2)}, u32[]{:S(2)}) collective-permute-start(bf16[512,512]{1,0:T(8,128)(2,1)S(1)} %bitcast.14), channel_id=1, source_target_pairs={{0,2},{1,7},{2,4},{3,1},{4,6},{5,3},{6,0},{7,5},{8,10},{9,15},{10,... | collective-permute-start | bytes 1572872 | tf_op jit(solution)/shard_map/ppermute | solution.py:55
  33.2 0.0 copy-done.4
  33.2 0.0 copy-done.5
  33.2 0.1 dynamic-slice_maximum_fusion
  33.3 0.1 copy.13
  33.4 0.1 pad_add_fusion.place
  33.5 0.0 copy-done
  33.5 0.7 shard_map.73.weight
  34.2 0.0 copy-start.3
  34.2 3.2 %collective-permute-start = (bf16[512,512]{1,0:T(8,128)(2,1)S(1)}, bf16[512,512]{1,0:T(8,128)(2,1)S(1)}, u32[]{:S(2)}, u32[]{:S(2)}) collective-permute-start(bf16[512,512]{1,0:T(8,128)(2,1)S(1)} %bitcast.15), channel_id=1, source_target_pairs={{0,7},{1,2},{2,1},{3,4},{4,3},{5,6},{6,5},{7,0},{8,15},{9,10},{10,... | collective-permute-start | bytes 1572872 | tf_op jit(solution)/shard_map/ppermute | solution.py:55
  37.4 4.3 %collective-permute-start.1 = (bf16[512,512]{1,0:T(8,128)(2,1)S(1)}, bf16[512,512]{1,0:T(8,128)(2,1)S(1)}, u32[]{:S(2)}, u32[]{:S(2)}) collective-permute-start(bf16[512,512]{1,0:T(8,128)(2,1)S(1)} %bitcast.16), channel_id=1, source_target_pairs={{0,1},{1,0},{2,3},{3,2},{4,5},{5,4},{6,7},{7,6},{8,9},{9,8},{10,11... | collective-permute-start | bytes 1572872 | tf_op jit(solution)/shard_map/ppermute | solution.py:55
  41.7 0.0 collective-permute-done.2.two_a
  41.7 3.5 %collective-permute-start.4 = (bf16[512,512]{1,0:T(8,128)(2,1)S(1)}, bf16[512,512]{1,0:T(8,128)(2,1)S(1)}, u32[]{:S(2)}, u32[]{:S(2)}) collective-permute-start(bf16[512,512]{1,0:T(8,128)(2,1)S(1)} %collective-permute-done.2.two_a), channel_id=1, source_target_pairs={{0,6},{1,3},{2,0},{3,5},{4,2},{5,7},{6,4},{7,1},{8,14},{9,11},{10,... | collective-permute-start | bytes 1572872 | tf_op jit(solution)/shard_map/ppermute | solution.py:55
  45.2 6.9 %collective-permute-start.5 = (bf16[512,512]{1,0:T(8,128)(2,1)S(1)}, bf16[512,512]{1,0:T(8,128)(2,1)S(1)}, u32[]{:S(2)}, u32[]{:S(2)}) collective-permute-start(bf16[512,512]{1,0:T(8,128)(2,1)S(1)} %collective-permute-done.2.two_a), channel_id=1, source_target_pairs={{0,7},{1,2},{2,1},{3,4},{4,3},{5,6},{6,5},{7,0},{8,15},{9,10},{10,... | collective-permute-start | bytes 1572872 | tf_op jit(solution)/shard_map/ppermute | solution.py:55
  52.1 0.0 collective-permute-done.3.two_b
  52.1 1.9 %collective-permute-start.6 = (bf16[512,512]{1,0:T(8,128)(2,1)S(1)}, bf16[512,512]{1,0:T(8,128)(2,1)S(1)}, u32[]{:S(2)}, u32[]{:S(2)}) collective-permute-start(bf16[512,512]{1,0:T(8,128)(2,1)S(1)} %collective-permute-done.3.two_b), channel_id=1, source_target_pairs={{0,1},{1,0},{2,3},{3,2},{4,5},{5,4},{6,7},{7,6},{8,9},{9,8},{10,11... | collective-permute-start | bytes 1572872 | tf_op jit(solution)/shard_map/ppermute | solution.py:55
  54.1 0.0 collective-permute-done.one_a
  54.1 0.0 collective-permute-done.1.one_b
  54.1 2.2 %collective-permute-done.4.four = bf16[512,512]{1,0:T(8,128)(2,1)S(1)} collective-permute-done((bf16[512,512]{1,0:T(8,128)(2,1)S(1)}, bf16[512,512]{1,0:T(8,128)(2,1)S(1)}, u32[]{:S(2)}, u32[]{:S(2)}) %collective-permute-start.4) | collective-permute-done | bytes 524320 | tf_op jit(solution)/shard_map/ppermute | solution.py:55
  56.2 1.9 %shard_map.74.before = f32[192,512]{1,0:T(8,128)S(1)} custom-call(s32[2]{0:T(128)S(1)} %pad_add_fusion.place, bf16[8,192,512]{2,1,0:T(8,128)(2,1)S(1)} %shard_map.73.weight, bf16[512,512]{1,0:T(8,128)(2,1)S(1)} %bitcast.17, bf16[512,512]{1,0:T(8,128)(2,1)S(1)} %collective-permute-done.one_a, bf16[512,512]{1,0:T(8,128)(2,1)S(1)} %collective-permute-done.1.one_b, ...), custom_call_target="tpu_custom_call" | custom-call | flops 603979776 | bytes 5242880 | tf_op jit(solution)/shard_map/pallas_call | solution.py:250
  58.1 0.0 copy-start.1
  58.1 0.0 copy-start.2
  58.1 4.5 %collective-permute-done.5.three_a = bf16[512,512]{1,0:T(8,128)(2,1)S(1)} collective-permute-done((bf16[512,512]{1,0:T(8,128)(2,1)S(1)}, bf16[512,512]{1,0:T(8,128)(2,1)S(1)}, u32[]{:S(2)}, u32[]{:S(2)}) %collective-permute-start.5) | collective-permute-done | bytes 524320 | tf_op jit(solution)/shard_map/ppermute | solution.py:55
  62.7 0.6 collective-permute-done.6.three_b
  63.3 0.0 copy-done.3
  63.3 1.1 %shard_map.75 = bf16[256,512]{1,0:T(8,128)(2,1)S(1)} custom-call(s32[2]{0:T(128)S(1)} %pad_add_fusion.place, bf16[8,192,512]{2,1,0:T(8,128)(2,1)S(1)} %shard_map.73.weight, f32[192,512]{1,0:T(8,128)S(1)} %shard_map.74.before, bf16[512,512]{1,0:T(8,128)(2,1)S(1)} %collective-permute-done.5.three_a, bf16[512,512]{1,0:T(8,128)(2,1)S(1)} %collective-permute-done.6.three_b, ...), custom_call_target="tpu_custom_call" | custom-call | flops 201326592 | bytes 3145728 | tf_op jit(solution)/shard_map/pallas_call | solution.py:261
  64.3 11.3 %all_to_all.16 = bf16[8,32,512]{2,1,0:T(8,128)(2,1)S(1)} all-to-all(bf16[8,32,512]{2,1,0:T(8,128)(2,1)S(1)} %bitcast.20), channel_id=1, replica_groups=mesh['seq'=8,'chan'=64] {'seq'}, dimensions={0} | all-to-all | bytes 524288 | tf_op jit(solution)/shard_map/all_to_all | solution.py:273
  75.6 0.0 copy-done.1
  75.6 0.0 copy-done.2
  75.6 0.8 shard_map.76
  76.4 8.3 %all_to_all.17 = bf16[8,8,512]{2,1,0:T(8,128)(2,1)S(1)} all-to-all(bf16[8,8,512]{2,1,0:T(8,128)(2,1)S(1)} %bitcast.21), channel_id=1, replica_groups=mesh['seq'=8,'chan'=64] {'seq'}, dimensions={0} | all-to-all | bytes 131072 | tf_op jit(solution)/shard_map/all_to_all | solution.py:285
  84.7 0.6 copy.15
  (1 shorter events, 0.0 us)
Async XLA Ops:
  0.0 33.2 %copy-start.4 = (f32[3,3,64]{2,1,0:T(4,128)S(1)}, f32[3,3,64]{2,1,0:T(4,128)}, u32[]{:S(2)}) copy-start(f32[3,3,64]{2,1,0:T(4,128)} %param.9) | copy-start | bytes 6916
  0.0 33.2 %copy-start.5 = (f32[64]{0:T(128)S(1)}, f32[64]{0:T(128)}, u32[]{:S(2)}) copy-start(f32[64]{0:T(128)} %param.11) | copy-start | bytes 772
  0.0 33.5 %copy-start = (bf16[3,64,4096]{2,1,0:T(8,128)(2,1)S(1)}, bf16[3,64,4096]{2,1,0:T(8,128)(2,1)}, u32[]{:S(2)}) copy-start(bf16[3,64,4096]{2,1,0:T(8,128)(2,1)} %param.8) | copy-start | bytes 4718596
  20.6 21.1 %collective-permute-start.2 = (bf16[512,512]{1,0:T(8,128)(2,1)S(1)}, bf16[512,512]{1,0:T(8,128)(2,1)S(1)}, u32[]{:S(2)}, u32[]{:S(2)}) collective-permute-start(bf16[512,512]{1,0:T(8,128)(2,1)S(1)} %bitcast.13), channel_id=1, source_target_pairs={{0,6},{1,3},{2,0},{3,5},{4,2},{5,7},{6,4},{7,1},{8,14},{9,11},{10,... | collective-permute-start | bytes 1572872 | tf_op jit(solution)/shard_map/ppermute | solution.py:55
  26.4 25.7 %collective-permute-start.3 = (bf16[512,512]{1,0:T(8,128)(2,1)S(1)}, bf16[512,512]{1,0:T(8,128)(2,1)S(1)}, u32[]{:S(2)}, u32[]{:S(2)}) collective-permute-start(bf16[512,512]{1,0:T(8,128)(2,1)S(1)} %bitcast.14), channel_id=1, source_target_pairs={{0,2},{1,7},{2,4},{3,1},{4,6},{5,3},{6,0},{7,5},{8,10},{9,15},{10,... | collective-permute-start | bytes 1572872 | tf_op jit(solution)/shard_map/ppermute | solution.py:55
  34.2 29.1 %copy-start.3 = (bf16[64,512]{1,0:T(8,128)(2,1)S(1)}, bf16[64,512]{1,0:T(8,128)(2,1)}, u32[]{:S(2)}) copy-start(bf16[64,512]{1,0:T(8,128)(2,1)} %lags.1) | copy-start | bytes 196612
  34.2 19.9 %collective-permute-start = (bf16[512,512]{1,0:T(8,128)(2,1)S(1)}, bf16[512,512]{1,0:T(8,128)(2,1)S(1)}, u32[]{:S(2)}, u32[]{:S(2)}) collective-permute-start(bf16[512,512]{1,0:T(8,128)(2,1)S(1)} %bitcast.15), channel_id=1, source_target_pairs={{0,7},{1,2},{2,1},{3,4},{4,3},{5,6},{6,5},{7,0},{8,15},{9,10},{10,... | collective-permute-start | bytes 1572872 | tf_op jit(solution)/shard_map/ppermute | solution.py:55
  37.4 16.7 %collective-permute-start.1 = (bf16[512,512]{1,0:T(8,128)(2,1)S(1)}, bf16[512,512]{1,0:T(8,128)(2,1)S(1)}, u32[]{:S(2)}, u32[]{:S(2)}) collective-permute-start(bf16[512,512]{1,0:T(8,128)(2,1)S(1)} %bitcast.16), channel_id=1, source_target_pairs={{0,1},{1,0},{2,3},{3,2},{4,5},{5,4},{6,7},{7,6},{8,9},{9,8},{10,11... | collective-permute-start | bytes 1572872 | tf_op jit(solution)/shard_map/ppermute | solution.py:55
  41.7 14.5 %collective-permute-start.4 = (bf16[512,512]{1,0:T(8,128)(2,1)S(1)}, bf16[512,512]{1,0:T(8,128)(2,1)S(1)}, u32[]{:S(2)}, u32[]{:S(2)}) collective-permute-start(bf16[512,512]{1,0:T(8,128)(2,1)S(1)} %collective-permute-done.2.two_a), channel_id=1, source_target_pairs={{0,6},{1,3},{2,0},{3,5},{4,2},{5,7},{6,4},{7,1},{8,14},{9,11},{10,... | collective-permute-start | bytes 1572872 | tf_op jit(solution)/shard_map/ppermute | solution.py:55
  45.2 17.5 %collective-permute-start.5 = (bf16[512,512]{1,0:T(8,128)(2,1)S(1)}, bf16[512,512]{1,0:T(8,128)(2,1)S(1)}, u32[]{:S(2)}, u32[]{:S(2)}) collective-permute-start(bf16[512,512]{1,0:T(8,128)(2,1)S(1)} %collective-permute-done.2.two_a), channel_id=1, source_target_pairs={{0,7},{1,2},{2,1},{3,4},{4,3},{5,6},{6,5},{7,0},{8,15},{9,10},{10,... | collective-permute-start | bytes 1572872 | tf_op jit(solution)/shard_map/ppermute | solution.py:55
  52.1 11.1 %collective-permute-start.6 = (bf16[512,512]{1,0:T(8,128)(2,1)S(1)}, bf16[512,512]{1,0:T(8,128)(2,1)S(1)}, u32[]{:S(2)}, u32[]{:S(2)}) collective-permute-start(bf16[512,512]{1,0:T(8,128)(2,1)S(1)} %collective-permute-done.3.two_b), channel_id=1, source_target_pairs={{0,1},{1,0},{2,3},{3,2},{4,5},{5,4},{6,7},{7,6},{8,9},{9,8},{10,11... | collective-permute-start | bytes 1572872 | tf_op jit(solution)/shard_map/ppermute | solution.py:55
  58.1 17.5 %copy-start.1 = (bf16[512,1024]{1,0:T(8,128)(2,1)S(1)}, bf16[512,1024]{1,0:T(8,128)(2,1)}, u32[]{:S(2)}) copy-start(bf16[512,1024]{1,0:T(8,128)(2,1)} %constant.52.clone.forward) | copy-start | bytes 3145732
  58.1 17.5 %copy-start.2 = (bf16[1024,512]{1,0:T(8,128)(2,1)S(1)}, bf16[1024,512]{1,0:T(8,128)(2,1)}, u32[]{:S(2)}) copy-start(bf16[1024,512]{1,0:T(8,128)(2,1)} %constant.53.clone.inverse) | copy-start | bytes 3145732

commit v8 on v7

--- a/solution.py
+++ b/solution.py
@@ -127,9 +127,13 @@
     return total
 
 
-def first_kernel(place, weight, own, one_a, one_b, two_a, two_b, four, out, near, done):
-    blocks = (own, one_a, one_b, two_a, two_b, four)
-    out[...] = project(place, weight, (0, 1, -1, -2, 2, 4), blocks, near, done, None)
+def own_kernel(place, weight, own, out, near, done):
+    out[...] = project(place, weight, (0,), (own,), near, done, None)
+
+
+def first_kernel(place, weight, before, one_a, one_b, two_a, two_b, four, out, near, done):
+    blocks = (one_a, one_b, two_a, two_b, four)
+    out[...] = project(place, weight, (1, -1, -2, 2, 4), blocks, near, done, before[...])
 
 
 def second_kernel(place, weight, before, three_a, three_b, lags, out, near, done):
@@ -242,7 +246,18 @@
         cost_estimate=pl.CostEstimate(flops=0, bytes_accessed=3 << 20, transcendentals=0),
     )(place, in_weight.reshape(192, RING * BLOCK))
     two_a, two_b = shift(own, 2, -2), shift(own, -2, 2)
-    later, weight = lax.optimization_barrier((own, weight))
+    before = pl.pallas_call(
+        own_kernel,
+        out_shape=jax.ShapeDtypeStruct((192, BLOCK), F32),
+        in_specs=[smem(), vmem(), anywhere()],
+        out_specs=vmem(),
+        scratch_shapes=landing(1),
+        compiler_params=params(12),
+        cost_estimate=pl.CostEstimate(
+            flops=2 * 192 * BLOCK * BLOCK, bytes_accessed=1 << 20, transcendentals=0
+        ),
+    )(place, weight, own)
+    later, before = lax.optimization_barrier((own, before))
     one_a, one_b = shift(later, 1, -1), shift(later, -1, 1)
     four = shift(two_a, 2, -2)
     three_a, three_b = shift(two_a, 1, -1), shift(two_b, -1, 1)
@@ -250,14 +265,14 @@
     before = pl.pallas_call(
         first_kernel,
         out_shape=jax.ShapeDtypeStruct((192, BLOCK), F32),
-        in_specs=[smem(), vmem()] + [anywhere()] * 6,
-        out_specs=vmem(),
-        scratch_shapes=landing(6),
+        in_specs=[smem(), vmem(), vmem()] + [anywhere()] * 5,
+        out_specs=vmem(),
+        scratch_shapes=landing(5),
         compiler_params=params(12),
         cost_estimate=pl.CostEstimate(
-            flops=2 * 6 * 192 * BLOCK * BLOCK, bytes_accessed=5 << 20, transcendentals=0
+            flops=2 * 5 * 192 * BLOCK * BLOCK, bytes_accessed=5 << 20, transcendentals=0
         ),
-    )(place, weight, own, one_a, one_b, two_a, two_b, four)
+    )(place, weight, before, one_a, one_b, two_a, two_b, four)
     messages = pl.pallas_call(
         second_kernel,
         out_shape=jax.ShapeDtypeStruct((RING * 32, BLOCK), BF16),

time: 85.7 us -> 85.7 us (level)
  starting transfers between devices: 32.4 us -> 31.5 us
    ppermute x7, starting transfers between devices: 32.4 us -> 31.5 us  [shift(): return lax.ppermute(block, BOTH, route)]
    pallas_call x0 -> x1, Pallas kernels: none -> 0.86 us  [on_device(): pl.pallas_call(own_kernel, out_shape=jax.ShapeDtypeStruct((192, BLOCK), F...]
  transfers between devices with their start and end apart: 7 -> 7, of which waited for: 3 -> 3; matrix products, arithmetic and copies ran while one was open for 0% -> 0% of each run, Pallas kernels for 3% -> 4%
where the time goes in v8:
time: 85.7 us; the launch traced here: 85.2 us
  blocking collectives  39.1 us (46%)
  starting transfers between devices  31.5 us (37%)
  waiting for transfers between devices  7.5 us (9%)
  Pallas kernels  5.04 us (6%)
  local copies, waits for them, and re-layouts  1.75 us (2%)
    ppermute x7, starting transfers between devices, shift(): return lax.ppermute(block, BOTH, route)  31.5 us
    all_to_all x1, blocking collectives, on_device(): lax.all_to_all(jnp.broadcast_to(shard[None], (RING,) + shard.shape), BOTH...  19.6 us
    all_to_all x1, blocking collectives, on_device(): lax.all_to_all(messages.reshape(RING, 32, BLOCK), 'seq', 0, 0, tiled=True)  11.2 us
    all_to_all x1, blocking collectives, on_device(): lax.all_to_all(mixed.reshape(RING, 8, BLOCK), 'seq', 0, 0, tiled=True)  8.26 us
    ppermute x7, waiting for transfers between devices, shift(): return lax.ppermute(block, BOTH, route)  7.5 us
  transfers between devices with their start and end apart: 7, of which 3 were waited for; matrix products, arithmetic and copies ran while one was open for 0% of the time, Pallas kernels for 4%

profile of v8, /device:TPU:1, one launch (start us, length us, event | category | flops | bytes accessed | tf_op | source)
XLA Modules:
  0.0 85.2 jit_solution(17037126769503278696)
XLA Ops:
  0.0 0.0 copy-start.4
  0.0 0.0 copy-start.5
  0.0 0.0 copy-start
  0.0 1.0 %broadcast_in_dim.10 = bf16[8,64,512]{2,1,0:T(8,128)(2,1)S(1)} broadcast(bf16[64,512]{1,0:T(8,128)(2,1)} %bitcast.24), dimensions={1,2} | broadcast | bytes 589824 | tf_op jit(solution)/shard_map/broadcast_in_dim | solution.py:229
  1.0 19.6 %all_to_all.15 = bf16[8,64,512]{2,1,0:T(8,128)(2,1)S(1)} all-to-all(bf16[8,64,512]{2,1,0:T(8,128)(2,1)S(1)} %broadcast_in_dim.10), channel_id=1, replica_groups={{0,8,16,24,32,40,48,56},{1,9,17,25,33,41,49,57},{2,10,18,26,34,42,50,58..., dimensions={0} | all-to-all | bytes 1048576 | tf_op jit(solution)/shard_map/all_to_all | solution.py:228
  20.6 5.8 %collective-permute-start.2 = (bf16[512,512]{1,0:T(8,128)(2,1)S(1)}, bf16[512,512]{1,0:T(8,128)(2,1)S(1)}, u32[]{:S(2)}, u32[]{:S(2)}) collective-permute-start(bf16[512,512]{1,0:T(8,128)(2,1)S(1)} %bitcast.13), channel_id=1, source_target_pairs={{0,6},{1,3},{2,0},{3,5},{4,2},{5,7},{6,4},{7,1},{8,14},{9,11},{10,... | collective-permute-start | bytes 1572872 | tf_op jit(solution)/shard_map/ppermute | solution.py:55
  26.4 6.8 %collective-permute-start.3 = (bf16[512,512]{1,0:T(8,128)(2,1)S(1)}, bf16[512,512]{1,0:T(8,128)(2,1)S(1)}, u32[]{:S(2)}, u32[]{:S(2)}) collective-permute-start(bf16[512,512]{1,0:T(8,128)(2,1)S(1)} %bitcast.14), channel_id=1, source_target_pairs={{0,2},{1,7},{2,4},{3,1},{4,6},{5,3},{6,0},{7,5},{8,10},{9,15},{10,... | collective-permute-start | bytes 1572872 | tf_op jit(solution)/shard_map/ppermute | solution.py:55
  33.2 0.0 copy-done.4
  33.2 0.0 copy-done.5
  33.2 0.1 dynamic-slice_maximum_fusion
  33.3 0.1 copy.13
  33.4 0.1 pad_add_fusion.place
  33.5 0.0 copy-done
  33.5 0.7 shard_map.73.weight
  34.2 0.9 %shard_map.74.before = f32[192,512]{1,0:T(8,128)S(1)} custom-call(s32[2]{0:T(128)S(1)} %pad_add_fusion.place, bf16[8,192,512]{2,1,0:T(8,128)(2,1)S(1)} %shard_map.73.weight, bf16[512,512]{1,0:T(8,128)(2,1)S(1)} %bitcast.15), custom_call_target="tpu_custom_call" | custom-call | flops 100663296 | bytes 1048576 | tf_op jit(solution)/shard_map/pallas_call | solution.py:249
  35.0 0.0 copy-start.3
  35.0 3.2 %collective-permute-start = (bf16[512,512]{1,0:T(8,128)(2,1)S(1)}, bf16[512,512]{1,0:T(8,128)(2,1)S(1)}, u32[]{:S(2)}, u32[]{:S(2)}) collective-permute-start(bf16[512,512]{1,0:T(8,128)(2,1)S(1)} %bitcast.16), channel_id=1, source_target_pairs={{0,7},{1,2},{2,1},{3,4},{4,3},{5,6},{6,5},{7,0},{8,15},{9,10},{10,... | collective-permute-start | bytes 1572872 | tf_op jit(solution)/shard_map/ppermute | solution.py:55
  38.3 4.3 %collective-permute-start.1 = (bf16[512,512]{1,0:T(8,128)(2,1)S(1)}, bf16[512,512]{1,0:T(8,128)(2,1)S(1)}, u32[]{:S(2)}, u32[]{:S(2)}) collective-permute-start(bf16[512,512]{1,0:T(8,128)(2,1)S(1)} %bitcast.17), channel_id=1, source_target_pairs={{0,1},{1,0},{2,3},{3,2},{4,5},{5,4},{6,7},{7,6},{8,9},{9,8},{10,11... | collective-permute-start | bytes 1572872 | tf_op jit(solution)/shard_map/ppermute | solution.py:55
  42.6 0.0 collective-permute-done.2.two_a
  42.6 2.6 %collective-permute-start.4 = (bf16[512,512]{1,0:T(8,128)(2,1)S(1)}, bf16[512,512]{1,0:T(8,128)(2,1)S(1)}, u32[]{:S(2)}, u32[]{:S(2)}) collective-permute-start(bf16[512,512]{1,0:T(8,128)(2,1)S(1)} %collective-permute-done.2.two_a), channel_id=1, source_target_pairs={{0,6},{1,3},{2,0},{3,5},{4,2},{5,7},{6,4},{7,1},{8,14},{9,11},{10,... | collective-permute-start | bytes 1572872 | tf_op jit(solution)/shard_map/ppermute | solution.py:55
  45.2 6.9 %collective-permute-start.5 = (bf16[512,512]{1,0:T(8,128)(2,1)S(1)}, bf16[512,512]{1,0:T(8,128)(2,1)S(1)}, u32[]{:S(2)}, u32[]{:S(2)}) collective-permute-start(bf16[512,512]{1,0:T(8,128)(2,1)S(1)} %collective-permute-done.2.two_a), channel_id=1, source_target_pairs={{0,7},{1,2},{2,1},{3,4},{4,3},{5,6},{6,5},{7,0},{8,15},{9,10},{10,... | collective-permute-start | bytes 1572872 | tf_op jit(solution)/shard_map/ppermute | solution.py:55
  52.1 0.0 collective-permute-done.3.two_b
  52.1 1.9 %collective-permute-start.6 = (bf16[512,512]{1,0:T(8,128)(2,1)S(1)}, bf16[512,512]{1,0:T(8,128)(2,1)S(1)}, u32[]{:S(2)}, u32[]{:S(2)}) collective-permute-start(bf16[512,512]{1,0:T(8,128)(2,1)S(1)} %collective-permute-done.3.two_b), channel_id=1, source_target_pairs={{0,1},{1,0},{2,3},{3,2},{4,5},{5,4},{6,7},{7,6},{8,9},{9,8},{10,11... | collective-permute-start | bytes 1572872 | tf_op jit(solution)/shard_map/ppermute | solution.py:55
  54.0 0.0 collective-permute-done.one_a
  54.0 0.0 collective-permute-done.1.one_b
  54.1 2.2 %collective-permute-done.4.four = bf16[512,512]{1,0:T(8,128)(2,1)S(1)} collective-permute-done((bf16[512,512]{1,0:T(8,128)(2,1)S(1)}, bf16[512,512]{1,0:T(8,128)(2,1)S(1)}, u32[]{:S(2)}, u32[]{:S(2)}) %collective-permute-start.4) | collective-permute-done | bytes 524320 | tf_op jit(solution)/shard_map/ppermute | solution.py:55
  56.2 1.7 %shard_map.75.before = f32[192,512]{1,0:T(8,128)S(1)} custom-call(s32[2]{0:T(128)S(1)} %pad_add_fusion.place, bf16[8,192,512]{2,1,0:T(8,128)(2,1)S(1)} %shard_map.73.weight, f32[192,512]{1,0:T(8,128)S(1)} %shard_map.74.before, bf16[512,512]{1,0:T(8,128)(2,1)S(1)} %collective-permute-done.one_a, bf16[512,512]{1,0:T(8,128)(2,1)S(1)} %collective-permute-done.1.one_b, ...), custom_call_target="tpu_custom_call" | custom-call | flops 503316480 | bytes 5242880 | tf_op jit(solution)/shard_map/pallas_call | solution.py:265
  57.9 0.0 copy-start.1
  57.9 0.0 copy-start.2
  57.9 4.7 %collective-permute-done.5.three_a = bf16[512,512]{1,0:T(8,128)(2,1)S(1)} collective-permute-done((bf16[512,512]{1,0:T(8,128)(2,1)S(1)}, bf16[512,512]{1,0:T(8,128)(2,1)S(1)}, u32[]{:S(2)}, u32[]{:S(2)}) %collective-permute-start.5) | collective-permute-done | bytes 524320 | tf_op jit(solution)/shard_map/ppermute | solution.py:55
  62.6 0.6 collective-permute-done.6.three_b
  63.2 0.0 copy-done.3
  63.2 1.1 %shard_map.76 = bf16[256,512]{1,0:T(8,128)(2,1)S(1)} custom-call(s32[2]{0:T(128)S(1)} %pad_add_fusion.place, bf16[8,192,512]{2,1,0:T(8,128)(2,1)S(1)} %shard_map.73.weight, f32[192,512]{1,0:T(8,128)S(1)} %shard_map.75.before, bf16[512,512]{1,0:T(8,128)(2,1)S(1)} %collective-permute-done.5.three_a, bf16[512,512]{1,0:T(8,128)(2,1)S(1)} %collective-permute-done.6.three_b, ...), custom_call_target="tpu_custom_call" | custom-call | flops 201326592 | bytes 3145728 | tf_op jit(solution)/shard_map/pallas_call | solution.py:276
  64.3 11.2 %all_to_all.16 = bf16[8,32,512]{2,1,0:T(8,128)(2,1)S(1)} all-to-all(bf16[8,32,512]{2,1,0:T(8,128)(2,1)S(1)} %bitcast.20), channel_id=1, replica_groups=mesh['seq'=8,'chan'=64] {'seq'}, dimensions={0} | all-to-all | bytes 524288 | tf_op jit(solution)/shard_map/all_to_all | solution.py:288
  75.6 0.0 copy-done.1
  75.6 0.0 copy-done.2
  75.6 0.8 shard_map.77
  76.4 8.3 %all_to_all.17 = bf16[8,8,512]{2,1,0:T(8,128)(2,1)S(1)} all-to-all(bf16[8,8,512]{2,1,0:T(8,128)(2,1)S(1)} %bitcast.21), channel_id=1, replica_groups=mesh['seq'=8,'chan'=64] {'seq'}, dimensions={0} | all-to-all | bytes 131072 | tf_op jit(solution)/shard_map/all_to_all | solution.py:300
  84.6 0.6 copy.15
  (1 shorter events, 0.0 us)
Async XLA Ops:
  0.0 33.2 %copy-start.4 = (f32[3,3,64]{2,1,0:T(4,128)S(1)}, f32[3,3,64]{2,1,0:T(4,128)}, u32[]{:S(2)}) copy-start(f32[3,3,64]{2,1,0:T(4,128)} %param.9) | copy-start | bytes 6916
  0.0 33.2 %copy-start.5 = (f32[64]{0:T(128)S(1)}, f32[64]{0:T(128)}, u32[]{:S(2)}) copy-start(f32[64]{0:T(128)} %param.11) | copy-start | bytes 772
  0.0 33.5 %copy-start = (bf16[3,64,4096]{2,1,0:T(8,128)(2,1)S(1)}, bf16[3,64,4096]{2,1,0:T(8,128)(2,1)}, u32[]{:S(2)}) copy-start(bf16[3,64,4096]{2,1,0:T(8,128)(2,1)} %param.8) | copy-start | bytes 4718596
  20.6 22.0 %collective-permute-start.2 = (bf16[512,512]{1,0:T(8,128)(2,1)S(1)}, bf16[512,512]{1,0:T(8,128)(2,1)S(1)}, u32[]{:S(2)}, u32[]{:S(2)}) collective-permute-start(bf16[512,512]{1,0:T(8,128)(2,1)S(1)} %bitcast.13), channel_id=1, source_target_pairs={{0,6},{1,3},{2,0},{3,5},{4,2},{5,7},{6,4},{7,1},{8,14},{9,11},{10,... | collective-permute-start | bytes 1572872 | tf_op jit(solution)/shard_map/ppermute | solution.py:55
  26.4 25.7 %collective-permute-start.3 = (bf16[512,512]{1,0:T(8,128)(2,1)S(1)}, bf16[512,512]{1,0:T(8,128)(2,1)S(1)}, u32[]{:S(2)}, u32[]{:S(2)}) collective-permute-start(bf16[512,512]{1,0:T(8,128)(2,1)S(1)} %bitcast.14), channel_id=1, source_target_pairs={{0,2},{1,7},{2,4},{3,1},{4,6},{5,3},{6,0},{7,5},{8,10},{9,15},{10,... | collective-permute-start | bytes 1572872 | tf_op jit(solution)/shard_map/ppermute | solution.py:55
  35.0 28.2 %copy-start.3 = (bf16[64,512]{1,0:T(8,128)(2,1)S(1)}, bf16[64,512]{1,0:T(8,128)(2,1)}, u32[]{:S(2)}) copy-start(bf16[64,512]{1,0:T(8,128)(2,1)} %lags.1) | copy-start | bytes 196612
  35.0 19.0 %collective-permute-start = (bf16[512,512]{1,0:T(8,128)(2,1)S(1)}, bf16[512,512]{1,0:T(8,128)(2,1)S(1)}, u32[]{:S(2)}, u32[]{:S(2)}) collective-permute-start(bf16[512,512]{1,0:T(8,128)(2,1)S(1)} %bitcast.16), channel_id=1, source_target_pairs={{0,7},{1,2},{2,1},{3,4},{4,3},{5,6},{6,5},{7,0},{8,15},{9,10},{10,... | collective-permute-start | bytes 1572872 | tf_op jit(solution)/shard_map/ppermute | solution.py:55
  38.3 15.8 %collective-permute-start.1 = (bf16[512,512]{1,0:T(8,128)(2,1)S(1)}, bf16[512,512]{1,0:T(8,128)(2,1)S(1)}, u32[]{:S(2)}, u32[]{:S(2)}) collective-permute-start(bf16[512,512]{1,0:T(8,128)(2,1)S(1)} %bitcast.17), channel_id=1, source_target_pairs={{0,1},{1,0},{2,3},{3,2},{4,5},{5,4},{6,7},{7,6},{8,9},{9,8},{10,11... | collective-permute-start | bytes 1572872 | tf_op jit(solution)/shard_map/ppermute | solution.py:55
  42.6 13.6 %collective-permute-start.4 = (bf16[512,512]{1,0:T(8,128)(2,1)S(1)}, bf16[512,512]{1,0:T(8,128)(2,1)S(1)}, u32[]{:S(2)}, u32[]{:S(2)}) collective-permute-start(bf16[512,512]{1,0:T(8,128)(2,1)S(1)} %collective-permute-done.2.two_a), channel_id=1, source_target_pairs={{0,6},{1,3},{2,0},{3,5},{4,2},{5,7},{6,4},{7,1},{8,14},{9,11},{10,... | collective-permute-start | bytes 1572872 | tf_op jit(solution)/shard_map/ppermute | solution.py:55
  45.2 17.5 %collective-permute-start.5 = (bf16[512,512]{1,0:T(8,128)(2,1)S(1)}, bf16[512,512]{1,0:T(8,128)(2,1)S(1)}, u32[]{:S(2)}, u32[]{:S(2)}) collective-permute-start(bf16[512,512]{1,0:T(8,128)(2,1)S(1)} %collective-permute-done.2.two_a), channel_id=1, source_target_pairs={{0,7},{1,2},{2,1},{3,4},{4,3},{5,6},{6,5},{7,0},{8,15},{9,10},{10,... | collective-permute-start | bytes 1572872 | tf_op jit(solution)/shard_map/ppermute | solution.py:55
  52.1 11.1 %collective-permute-start.6 = (bf16[512,512]{1,0:T(8,128)(2,1)S(1)}, bf16[512,512]{1,0:T(8,128)(2,1)S(1)}, u32[]{:S(2)}, u32[]{:S(2)}) collective-permute-start(bf16[512,512]{1,0:T(8,128)(2,1)S(1)} %collective-permute-done.3.two_b), channel_id=1, source_target_pairs={{0,1},{1,0},{2,3},{3,2},{4,5},{5,4},{6,7},{7,6},{8,9},{9,8},{10,11... | collective-permute-start | bytes 1572872 | tf_op jit(solution)/shard_map/ppermute | solution.py:55
  57.9 17.7 %copy-start.1 = (bf16[512,1024]{1,0:T(8,128)(2,1)S(1)}, bf16[512,1024]{1,0:T(8,128)(2,1)}, u32[]{:S(2)}) copy-start(bf16[512,1024]{1,0:T(8,128)(2,1)} %constant.52.clone.forward) | copy-start | bytes 3145732
  57.9 17.6 %copy-start.2 = (bf16[1024,512]{1,0:T(8,128)(2,1)S(1)}, bf16[1024,512]{1,0:T(8,128)(2,1)}, u32[]{:S(2)}) copy-start(bf16[1024,512]{1,0:T(8,128)(2,1)} %constant.53.clone.inverse) | copy-start | bytes 3145732

commit v9 on v8

--- a/solution.py
+++ b/solution.py
@@ -45,7 +45,7 @@
     route = []
     for x, core, z, y in devices():
         here = z if core else y
-        there = here + (odd if (here + 1 - core) % 2 else even)
+        there = here + (odd if (here + 1) % 2 else even)
         route.append(
             (
                 device_number(x, core, z, y),
@@ -110,7 +110,7 @@
 
 def project(place, weight, offsets, blocks, near, done, total):
     r = place[1]
-    sign = 1 - 2 * lax.rem(r + place[0], 2)
+    sign = 1 - 2 * lax.rem(r + 1, 2)
     copies = [
         pltpu.make_async_copy(block, near.at[i], done.at[i]) for i, block in enumerate(blocks)
     ]

time: 85.7 us -> 85.7 us (level)
  starting transfers between devices: 31.5 us -> 28.8 us
  waiting for transfers between devices: 7.5 us -> 8.94 us
  blocking collectives: 39.1 us -> 40.4 us
    ppermute x7, starting transfers between devices: 31.5 us -> 28.8 us  [shift(): return lax.ppermute(block, BOTH, route)]
    ppermute x7, waiting for transfers between devices: 7.5 us -> 8.94 us  [shift(): return lax.ppermute(block, BOTH, route)]
    all_to_all x1, blocking collectives: 11.2 us -> 12.6 us  [on_device(): lax.all_to_all(messages.reshape(RING, 32, BLOCK), 'seq', 0, 0, tiled=True)]
where the time goes in v9:
time: 85.7 us; the launch traced here: 85.2 us
  blocking collectives  40.4 us (47%)
  starting transfers between devices  28.8 us (34%)
  waiting for transfers between devices  8.94 us (10%)
  Pallas kernels  5.04 us (6%)
  local copies, waits for them, and re-layouts  1.75 us (2%)
    ppermute x7, starting transfers between devices, shift(): return lax.ppermute(block, BOTH, route)  28.8 us
    all_to_all x1, blocking collectives, on_device(): lax.all_to_all(jnp.broadcast_to(shard[None], (RING,) + shard.shape), BOTH...  19.6 us
    all_to_all x1, blocking collectives, on_device(): lax.all_to_all(messages.reshape(RING, 32, BLOCK), 'seq', 0, 0, tiled=True)  12.6 us
    ppermute x7, waiting for transfers between devices, shift(): return lax.ppermute(block, BOTH, route)  8.94 us
    all_to_all x1, blocking collectives, on_device(): lax.all_to_all(mixed.reshape(RING, 8, BLOCK), 'seq', 0, 0, tiled=True)  8.26 us
  transfers between devices with their start and end apart: 7, of which 3 were waited for; matrix products, arithmetic and copies ran while one was open for 0% of the time, Pallas kernels for 4%

profile of v9, /device:TPU:1, one launch (start us, length us, event | category | flops | bytes accessed | tf_op | source)
XLA Modules:
  0.0 85.2 jit_solution(7498075720197051727)
XLA Ops:
  0.0 0.0 copy-start.4
  0.0 0.0 copy-start.5
  0.0 0.0 copy-start
  0.0 1.0 %broadcast_in_dim.10 = bf16[8,64,512]{2,1,0:T(8,128)(2,1)S(1)} broadcast(bf16[64,512]{1,0:T(8,128)(2,1)} %bitcast.24), dimensions={1,2} | broadcast | bytes 589824 | tf_op jit(solution)/shard_map/broadcast_in_dim | solution.py:229
  1.0 19.6 %all_to_all.15 = bf16[8,64,512]{2,1,0:T(8,128)(2,1)S(1)} all-to-all(bf16[8,64,512]{2,1,0:T(8,128)(2,1)S(1)} %broadcast_in_dim.10), channel_id=1, replica_groups={{0,8,16,24,32,40,48,56},{1,9,17,25,33,41,49,57},{2,10,18,26,34,42,50,58..., dimensions={0} | all-to-all | bytes 1048576 | tf_op jit(solution)/shard_map/all_to_all | solution.py:228
  20.6 10.6 %collective-permute-start.2 = (bf16[512,512]{1,0:T(8,128)(2,1)S(1)}, bf16[512,512]{1,0:T(8,128)(2,1)S(1)}, u32[]{:S(2)}, u32[]{:S(2)}) collective-permute-start(bf16[512,512]{1,0:T(8,128)(2,1)S(1)} %bitcast.13), channel_id=1, source_target_pairs={{0,6},{1,3},{2,0},{3,5},{4,2},{5,7},{6,4},{7,1},{8,14},{9,11},{10,... | collective-permute-start | bytes 1572872 | tf_op jit(solution)/shard_map/ppermute | solution.py:55
  31.3 1.9 %collective-permute-start.3 = (bf16[512,512]{1,0:T(8,128)(2,1)S(1)}, bf16[512,512]{1,0:T(8,128)(2,1)S(1)}, u32[]{:S(2)}, u32[]{:S(2)}) collective-permute-start(bf16[512,512]{1,0:T(8,128)(2,1)S(1)} %bitcast.14), channel_id=1, source_target_pairs={{0,2},{1,7},{2,4},{3,1},{4,6},{5,3},{6,0},{7,5},{8,10},{9,15},{10,... | collective-permute-start | bytes 1572872 | tf_op jit(solution)/shard_map/ppermute | solution.py:55
  33.2 0.0 copy-done.4
  33.2 0.0 copy-done.5
  33.2 0.1 dynamic-slice_maximum_fusion
  33.3 0.1 copy.13
  33.4 0.1 pad_add_fusion.place
  33.5 0.0 copy-done
  33.5 0.7 shard_map.73.weight
  34.2 0.9 %shard_map.74.before = f32[192,512]{1,0:T(8,128)S(1)} custom-call(s32[2]{0:T(128)S(1)} %pad_add_fusion.place, bf16[8,192,512]{2,1,0:T(8,128)(2,1)S(1)} %shard_map.73.weight, bf16[512,512]{1,0:T(8,128)(2,1)S(1)} %bitcast.15), custom_call_target="tpu_custom_call" | custom-call | flops 100663296 | bytes 1048576 | tf_op jit(solution)/shard_map/pallas_call | solution.py:249
  35.0 0.0 copy-start.3
  35.0 4.4 %collective-permute-start = (bf16[512,512]{1,0:T(8,128)(2,1)S(1)}, bf16[512,512]{1,0:T(8,128)(2,1)S(1)}, u32[]{:S(2)}, u32[]{:S(2)}) collective-permute-start(bf16[512,512]{1,0:T(8,128)(2,1)S(1)} %bitcast.16), channel_id=1, source_target_pairs={{0,7},{1,2},{2,1},{3,4},{4,3},{5,6},{6,5},{7,0},{8,15},{9,10},{10,... | collective-permute-start | bytes 1572872 | tf_op jit(solution)/shard_map/ppermute | solution.py:55
  39.4 1.9 %collective-permute-start.1 = (bf16[512,512]{1,0:T(8,128)(2,1)S(1)}, bf16[512,512]{1,0:T(8,128)(2,1)S(1)}, u32[]{:S(2)}, u32[]{:S(2)}) collective-permute-start(bf16[512,512]{1,0:T(8,128)(2,1)S(1)} %bitcast.17), channel_id=1, source_target_pairs={{0,1},{1,0},{2,3},{3,2},{4,5},{5,4},{6,7},{7,6},{8,9},{9,8},{10,11... | collective-permute-start | bytes 1572872 | tf_op jit(solution)/shard_map/ppermute | solution.py:55
  41.4 1.6 %collective-permute-done.2.two_a = bf16[512,512]{1,0:T(8,128)(2,1)S(1)} collective-permute-done((bf16[512,512]{1,0:T(8,128)(2,1)S(1)}, bf16[512,512]{1,0:T(8,128)(2,1)S(1)}, u32[]{:S(2)}, u32[]{:S(2)}) %collective-permute-start.2) | collective-permute-done | bytes 524320 | tf_op jit(solution)/shard_map/ppermute | solution.py:55
  43.0 6.0 %collective-permute-start.4 = (bf16[512,512]{1,0:T(8,128)(2,1)S(1)}, bf16[512,512]{1,0:T(8,128)(2,1)S(1)}, u32[]{:S(2)}, u32[]{:S(2)}) collective-permute-start(bf16[512,512]{1,0:T(8,128)(2,1)S(1)} %collective-permute-done.2.two_a), channel_id=1, source_target_pairs={{0,6},{1,3},{2,0},{3,5},{4,2},{5,7},{6,4},{7,1},{8,14},{9,11},{10,... | collective-permute-start | bytes 1572872 | tf_op jit(solution)/shard_map/ppermute | solution.py:55
  49.0 1.9 %collective-permute-start.5 = (bf16[512,512]{1,0:T(8,128)(2,1)S(1)}, bf16[512,512]{1,0:T(8,128)(2,1)S(1)}, u32[]{:S(2)}, u32[]{:S(2)}) collective-permute-start(bf16[512,512]{1,0:T(8,128)(2,1)S(1)} %collective-permute-done.2.two_a), channel_id=1, source_target_pairs={{0,7},{1,2},{2,1},{3,4},{4,3},{5,6},{6,5},{7,0},{8,15},{9,10},{10,... | collective-permute-start | bytes 1572872 | tf_op jit(solution)/shard_map/ppermute | solution.py:55
  50.9 0.0 collective-permute-done.3.two_b
  50.9 1.9 %collective-permute-start.6 = (bf16[512,512]{1,0:T(8,128)(2,1)S(1)}, bf16[512,512]{1,0:T(8,128)(2,1)S(1)}, u32[]{:S(2)}, u32[]{:S(2)}) collective-permute-start(bf16[512,512]{1,0:T(8,128)(2,1)S(1)} %collective-permute-done.3.two_b), channel_id=1, source_target_pairs={{0,1},{1,0},{2,3},{3,2},{4,5},{5,4},{6,7},{7,6},{8,9},{9,8},{10,11... | collective-permute-start | bytes 1572872 | tf_op jit(solution)/shard_map/ppermute | solution.py:55
  52.9 0.0 collective-permute-done.one_a
  52.9 2.4 %collective-permute-done.1.one_b = bf16[512,512]{1,0:T(8,128)(2,1)S(1)} collective-permute-done((bf16[512,512]{1,0:T(8,128)(2,1)S(1)}, bf16[512,512]{1,0:T(8,128)(2,1)S(1)}, u32[]{:S(2)}, u32[]{:S(2)}) %collective-permute-start.1) | collective-permute-done | bytes 524320 | tf_op jit(solution)/shard_map/ppermute | solution.py:55
  55.3 0.0 collective-permute-done.4.four
  55.3 1.7 %shard_map.75.before = f32[192,512]{1,0:T(8,128)S(1)} custom-call(s32[2]{0:T(128)S(1)} %pad_add_fusion.place, bf16[8,192,512]{2,1,0:T(8,128)(2,1)S(1)} %shard_map.73.weight, f32[192,512]{1,0:T(8,128)S(1)} %shard_map.74.before, bf16[512,512]{1,0:T(8,128)(2,1)S(1)} %collective-permute-done.one_a, bf16[512,512]{1,0:T(8,128)(2,1)S(1)} %collective-permute-done.1.one_b, ...), custom_call_target="tpu_custom_call" | custom-call | flops 503316480 | bytes 5242880 | tf_op jit(solution)/shard_map/pallas_call | solution.py:265
  57.0 0.0 copy-start.1
  57.0 0.0 copy-start.2
  57.0 4.9 %collective-permute-done.5.three_a = bf16[512,512]{1,0:T(8,128)(2,1)S(1)} collective-permute-done((bf16[512,512]{1,0:T(8,128)(2,1)S(1)}, bf16[512,512]{1,0:T(8,128)(2,1)S(1)}, u32[]{:S(2)}, u32[]{:S(2)}) %collective-permute-start.5) | collective-permute-done | bytes 524320 | tf_op jit(solution)/shard_map/ppermute | solution.py:55
  61.9 0.0 collective-permute-done.6.three_b
  61.9 0.0 copy-done.3
  61.9 1.1 %shard_map.76 = bf16[256,512]{1,0:T(8,128)(2,1)S(1)} custom-call(s32[2]{0:T(128)S(1)} %pad_add_fusion.place, bf16[8,192,512]{2,1,0:T(8,128)(2,1)S(1)} %shard_map.73.weight, f32[192,512]{1,0:T(8,128)S(1)} %shard_map.75.before, bf16[512,512]{1,0:T(8,128)(2,1)S(1)} %collective-permute-done.5.three_a, bf16[512,512]{1,0:T(8,128)(2,1)S(1)} %collective-permute-done.6.three_b, ...), custom_call_target="tpu_custom_call" | custom-call | flops 201326592 | bytes 3145728 | tf_op jit(solution)/shard_map/pallas_call | solution.py:276
  63.0 12.6 %all_to_all.16 = bf16[8,32,512]{2,1,0:T(8,128)(2,1)S(1)} all-to-all(bf16[8,32,512]{2,1,0:T(8,128)(2,1)S(1)} %bitcast.20), channel_id=1, replica_groups=mesh['seq'=8,'chan'=64] {'seq'}, dimensions={0} | all-to-all | bytes 524288 | tf_op jit(solution)/shard_map/all_to_all | solution.py:288
  75.6 0.0 copy-done.1
  75.6 0.0 copy-done.2
  75.6 0.8 shard_map.77
  76.4 8.3 %all_to_all.17 = bf16[8,8,512]{2,1,0:T(8,128)(2,1)S(1)} all-to-all(bf16[8,8,512]{2,1,0:T(8,128)(2,1)S(1)} %bitcast.21), channel_id=1, replica_groups=mesh['seq'=8,'chan'=64] {'seq'}, dimensions={0} | all-to-all | bytes 131072 | tf_op jit(solution)/shard_map/all_to_all | solution.py:300
  84.6 0.6 copy.15
  (1 shorter events, 0.0 us)
Async XLA Ops:
  0.0 33.2 %copy-start.4 = (f32[3,3,64]{2,1,0:T(4,128)S(1)}, f32[3,3,64]{2,1,0:T(4,128)}, u32[]{:S(2)}) copy-start(f32[3,3,64]{2,1,0:T(4,128)} %param.9) | copy-start | bytes 6916
  0.0 33.2 %copy-start.5 = (f32[64]{0:T(128)S(1)}, f32[64]{0:T(128)}, u32[]{:S(2)}) copy-start(f32[64]{0:T(128)} %param.11) | copy-start | bytes 772
  0.0 33.5 %copy-start = (bf16[3,64,4096]{2,1,0:T(8,128)(2,1)S(1)}, bf16[3,64,4096]{2,1,0:T(8,128)(2,1)}, u32[]{:S(2)}) copy-start(bf16[3,64,4096]{2,1,0:T(8,128)(2,1)} %param.8) | copy-start | bytes 4718596
  20.6 22.4 %collective-permute-start.2 = (bf16[512,512]{1,0:T(8,128)(2,1)S(1)}, bf16[512,512]{1,0:T(8,128)(2,1)S(1)}, u32[]{:S(2)}, u32[]{:S(2)}) collective-permute-start(bf16[512,512]{1,0:T(8,128)(2,1)S(1)} %bitcast.13), channel_id=1, source_target_pairs={{0,6},{1,3},{2,0},{3,5},{4,2},{5,7},{6,4},{7,1},{8,14},{9,11},{10,... | collective-permute-start | bytes 1572872 | tf_op jit(solution)/shard_map/ppermute | solution.py:55
  31.3 19.7 %collective-permute-start.3 = (bf16[512,512]{1,0:T(8,128)(2,1)S(1)}, bf16[512,512]{1,0:T(8,128)(2,1)S(1)}, u32[]{:S(2)}, u32[]{:S(2)}) collective-permute-start(bf16[512,512]{1,0:T(8,128)(2,1)S(1)} %bitcast.14), channel_id=1, source_target_pairs={{0,2},{1,7},{2,4},{3,1},{4,6},{5,3},{6,0},{7,5},{8,10},{9,15},{10,... | collective-permute-start | bytes 1572872 | tf_op jit(solution)/shard_map/ppermute | solution.py:55
  35.0 26.9 %copy-start.3 = (bf16[64,512]{1,0:T(8,128)(2,1)S(1)}, bf16[64,512]{1,0:T(8,128)(2,1)}, u32[]{:S(2)}) copy-start(bf16[64,512]{1,0:T(8,128)(2,1)} %lags.1) | copy-start | bytes 196612
  35.0 17.8 %collective-permute-start = (bf16[512,512]{1,0:T(8,128)(2,1)S(1)}, bf16[512,512]{1,0:T(8,128)(2,1)S(1)}, u32[]{:S(2)}, u32[]{:S(2)}) collective-permute-start(bf16[512,512]{1,0:T(8,128)(2,1)S(1)} %bitcast.16), channel_id=1, source_target_pairs={{0,7},{1,2},{2,1},{3,4},{4,3},{5,6},{6,5},{7,0},{8,15},{9,10},{10,... | collective-permute-start | bytes 1572872 | tf_op jit(solution)/shard_map/ppermute | solution.py:55
  39.4 15.8 %collective-permute-start.1 = (bf16[512,512]{1,0:T(8,128)(2,1)S(1)}, bf16[512,512]{1,0:T(8,128)(2,1)S(1)}, u32[]{:S(2)}, u32[]{:S(2)}) collective-permute-start(bf16[512,512]{1,0:T(8,128)(2,1)S(1)} %bitcast.17), channel_id=1, source_target_pairs={{0,1},{1,0},{2,3},{3,2},{4,5},{5,4},{6,7},{7,6},{8,9},{9,8},{10,11... | collective-permute-start | bytes 1572872 | tf_op jit(solution)/shard_map/ppermute | solution.py:55
  43.0 12.3 %collective-permute-start.4 = (bf16[512,512]{1,0:T(8,128)(2,1)S(1)}, bf16[512,512]{1,0:T(8,128)(2,1)S(1)}, u32[]{:S(2)}, u32[]{:S(2)}) collective-permute-start(bf16[512,512]{1,0:T(8,128)(2,1)S(1)} %collective-permute-done.2.two_a), channel_id=1, source_target_pairs={{0,6},{1,3},{2,0},{3,5},{4,2},{5,7},{6,4},{7,1},{8,14},{9,11},{10,... | collective-permute-start | bytes 1572872 | tf_op jit(solution)/shard_map/ppermute | solution.py:55
  49.0 12.9 %collective-permute-start.5 = (bf16[512,512]{1,0:T(8,128)(2,1)S(1)}, bf16[512,512]{1,0:T(8,128)(2,1)S(1)}, u32[]{:S(2)}, u32[]{:S(2)}) collective-permute-start(bf16[512,512]{1,0:T(8,128)(2,1)S(1)} %collective-permute-done.2.two_a), channel_id=1, source_target_pairs={{0,7},{1,2},{2,1},{3,4},{4,3},{5,6},{6,5},{7,0},{8,15},{9,10},{10,... | collective-permute-start | bytes 1572872 | tf_op jit(solution)/shard_map/ppermute | solution.py:55
  50.9 11.0 %collective-permute-start.6 = (bf16[512,512]{1,0:T(8,128)(2,1)S(1)}, bf16[512,512]{1,0:T(8,128)(2,1)S(1)}, u32[]{:S(2)}, u32[]{:S(2)}) collective-permute-start(bf16[512,512]{1,0:T(8,128)(2,1)S(1)} %collective-permute-done.3.two_b), channel_id=1, source_target_pairs={{0,1},{1,0},{2,3},{3,2},{4,5},{5,4},{6,7},{7,6},{8,9},{9,8},{10,11... | collective-permute-start | bytes 1572872 | tf_op jit(solution)/shard_map/ppermute | solution.py:55
  57.0 18.6 %copy-start.1 = (bf16[512,1024]{1,0:T(8,128)(2,1)S(1)}, bf16[512,1024]{1,0:T(8,128)(2,1)}, u32[]{:S(2)}) copy-start(bf16[512,1024]{1,0:T(8,128)(2,1)} %constant.52.clone.forward) | copy-start | bytes 3145732
  57.0 18.6 %copy-start.2 = (bf16[1024,512]{1,0:T(8,128)(2,1)S(1)}, bf16[1024,512]{1,0:T(8,128)(2,1)}, u32[]{:S(2)}) copy-start(bf16[1024,512]{1,0:T(8,128)(2,1)} %constant.53.clone.inverse) | copy-start | bytes 3145732
